TPU v7x, 256 devices: a whole 4x4x8 slice. The times are simulated.
256 devices in a mesh: dp: 16 (over z, core), mp: 16 (over y, x).
Axes of the slice: x: 4, y: 4, z: 8, core: 2. Of those that a mesh axis runs over, the one named last changes fastest.
Arguments:
- acts: bfloat16 [2048, 8192], P('dp'), may hold values from -6 to 6
- cotangent: bfloat16 [2048, 8192], P('dp', 'mp'), may hold values from -0.01171875 to 0.01171875
- factors: float32 [16, 96, 2, 256, 256], P('dp', 'mp')
- roots: bfloat16 [16, 96, 2, 256, 256], P('dp', 'mp')
- owner_of: int32 [16, 16, 4], replicated, may hold values from 0 to 15, as said below
- slot_of: int32 [16, 16, 4], replicated, may hold values from 0 to 5, as said below
- refresh_ids: int32 [16, 16], replicated, may hold values from 0 to 63, as said below
Outputs:
- direction: float32 [8192, 8192], P('dp', 'mp')
- factors_next: float32 [16, 96, 2, 256, 256], P('dp', 'mp')
- roots_next: bfloat16 [16, 96, 2, 256, 256], P('dp', 'mp')
Inputs may be any that keep to these rules, and one draw needn't show every extreme that they name: Within each d, owner_of[d, m, j] names the owner of block j of device (d, m) and slot_of[d, m, j] its slot there; the blocks of one owner have distinct slots; one owner holds at most 6 blocks of a d, and some owner holds exactly 6; at most 1 of one device's blocks go to one owner, reached. `slot_of`: slots as described with owner_of. `refresh_ids`: distinct local ids m * 4 + j; one owner holds at most 2 of a row's refreshed blocks, and some owner exactly that many.
All inputs are finite; a program needn't handle non-finite values.
Results may differ from a plain program's by a relative error of at most 0.0017.
Values may be sent and summed in bfloat16 or wider, within the bound.
No kernel may reach another device: no remote copies, remote signals or barrier semaphores. Data moves between devices by JAX's collectives and lax.ppermute only.
A program may use at most 128 MiB of HBM per device.

v0:
```python
import jax
import jax.numpy as jnp
from jax import lax
from jax.sharding import PartitionSpec as P

ITERS = 10
REFRESH_MOST = 2


EPSILON = 0.1


def product(left, right):
    return jnp.matmul(left, right, precision=lax.Precision.HIGHEST)


def inverse_root(matrices):
    edge = matrices.shape[-1]
    identity = jnp.eye(edge, dtype=matrices.dtype)
    shifted = matrices + EPSILON * identity
    frob_norm = jnp.sqrt(jnp.sum(shifted * shifted, axis=(1, 2), keepdims=True))
    scaled = shifted / frob_norm
    result = jnp.broadcast_to(identity, matrices.shape) / jnp.sqrt(jnp.sqrt(frob_norm))

    def newton_step(iteration, carry):
        current, moving = carry
        factor = (5.0 * identity - moving) * 0.25
        square = product(factor, factor)
        return (product(current, factor), product(product(square, square), moving))

    result, scaled = lax.fori_loop(0, ITERS, newton_step, (result, scaled))
    return result


def body(acts, cotangent, factors, roots, owner_of, slot_of, refresh_ids):
    dp_count = lax.axis_size("dp")
    mp_count = lax.axis_size("mp")
    dp_index = lax.axis_index("dp")
    mp_index = lax.axis_index("mp")
    block_edge = factors.shape[-1]
    slot_total = factors.shape[1]
    row_count = acts.shape[1] // dp_count
    slab_width = cotangent.shape[1]
    local_blocks = owner_of.shape[2]
    send_depth = (slot_total + mp_count - 1) // mp_count
    row_blocks = row_count // block_edge
    col_blocks = slab_width // block_edge
    gradient = lax.psum_scatter(
        lax.dot_general(
            acts, cotangent, (((0,), (0,)), ((), ())), preferred_element_type=jnp.float32
        ),
        "dp",
        scatter_dimension=0,
        tiled=True,
    )
    blocks = gradient.reshape(row_blocks, block_edge, col_blocks, block_edge).transpose(0, 2, 1, 3)
    blocks = blocks.reshape(local_blocks, block_edge, block_edge)
    owners_row = lax.dynamic_index_in_dim(owner_of, dp_index, 0, keepdims=False)
    slots_row = lax.dynamic_index_in_dim(slot_of, dp_index, 0, keepdims=False)
    refresh_row = lax.dynamic_index_in_dim(refresh_ids, dp_index, 0, keepdims=False)
    block_range = jnp.arange(local_blocks, dtype=jnp.int32)
    earlier = block_range[None, :] < block_range[:, None]
    same_owner = owners_row[:, :, None] == owners_row[:, None, :]
    rank_all = jnp.sum((same_owner & earlier[None]).astype(jnp.int32), axis=2)
    outbound_all = owners_row * send_depth + rank_all
    outbound = lax.dynamic_index_in_dim(outbound_all, mp_index, 0, keepdims=False)
    outgoing = (
        jnp.zeros((mp_count * send_depth, block_edge, block_edge), jnp.float32)
        .at[outbound]
        .set(blocks)
    )
    incoming = lax.all_to_all(outgoing, "mp", split_axis=0, concat_axis=0, tiled=True)
    arrival = jnp.arange(mp_count, dtype=jnp.int32)[:, None] * send_depth + rank_all
    held_here = owners_row == mp_index
    slot_range = jnp.arange(slot_total, dtype=jnp.int32)
    matched = held_here[None] & (slots_row[None] == slot_range[:, None, None])
    occupied = jnp.any(matched, axis=(1, 2))
    where_from = jnp.sum(matched.astype(jnp.int32) * arrival[None], axis=(1, 2))
    gathered = jnp.take(incoming, where_from, axis=0) * occupied[:, None, None].astype(jnp.float32)
    state = factors[0]
    left_new = state[:, 0] + jnp.einsum(
        "sik,sjk->sij", gathered, gathered, precision=lax.Precision.HIGHEST
    )
    right_new = state[:, 1] + jnp.einsum(
        "ski,skj->sij", gathered, gathered, precision=lax.Precision.HIGHEST
    )
    new_state = jnp.stack([left_new, right_new], axis=1)
    block_ids = jnp.arange(mp_count, dtype=jnp.int32)[:, None] * local_blocks + block_range[None, :]
    is_fresh = jnp.any(refresh_row[:, None, None] == block_ids[None], axis=0)
    fresh = jnp.any(matched & is_fresh[None], axis=(1, 2))
    ranking = jnp.cumsum(fresh.astype(jnp.int32)) - 1
    refresh_range = jnp.arange(REFRESH_MOST, dtype=jnp.int32)
    selected = (refresh_range[:, None] == ranking[None, :]) & fresh[None, :]
    picked = jnp.sum(selected.astype(jnp.int32) * slot_range[None, :], axis=1)
    batch_mats = jnp.take(new_state, picked, axis=0).reshape(
        REFRESH_MOST * 2, block_edge, block_edge
    )
    computed = (
        inverse_root(batch_mats)
        .astype(jnp.bfloat16)
        .reshape(REFRESH_MOST, 2, block_edge, block_edge)
    )
    spread = jnp.take(computed, jnp.clip(ranking, 0, REFRESH_MOST - 1), axis=0)
    roots_new = jnp.where(fresh[:, None, None, None], spread, roots[0])
    current = roots_new.astype(jnp.float32)
    precond = product(product(current[:, 0], gathered), current[:, 1])
    ratio = jnp.sqrt(
        jnp.sum(gathered * gathered, axis=(1, 2))
        / (jnp.sum(precond * precond, axis=(1, 2)) + 1e-06)
    )
    grafted = precond * ratio[:, None, None]
    where_home = jnp.where(occupied, where_from, mp_count * send_depth)
    homeward = (
        jnp.zeros((mp_count * send_depth, block_edge, block_edge), jnp.float32)
        .at[where_home]
        .set(grafted, mode="drop")
    )
    returned = lax.all_to_all(homeward, "mp", split_axis=0, concat_axis=0, tiled=True)
    mine_back = jnp.take(returned, outbound, axis=0)
    direction = mine_back.reshape(row_blocks, col_blocks, block_edge, block_edge).transpose(
        0, 2, 1, 3
    )
    direction = direction.reshape(row_count, slab_width)
    return (direction, new_state[None], roots_new[None])


def solution(mesh):
    in_specs = (
        P("dp", None),
        P("dp", "mp"),
        P("dp", "mp", None, None, None),
        P("dp", "mp", None, None, None),
        P(),
        P(),
        P(),
    )
    out_specs = (P("dp", "mp"), P("dp", "mp", None, None, None), P("dp", "mp", None, None, None))
    return jax.shard_map(body, mesh=mesh, in_specs=in_specs, out_specs=out_specs, check_vma=False)
```

profile of v0, /device:TPU:96, one launch (start us, length us, event | category | flops | bytes accessed | tf_op | source)
XLA Modules:
  0.0 388.6 jit_solution(13573157920675557644)
XLA Ops:
  7.2 1.5 copy-done
  8.8 9.0 %fusion.47 = f32[8192,512]{1,0:T(8,128)} fusion(bf16[128,8192]{1,0:T(8,128)(2,1)S(1)} %copy-done, bf16[128,512]{1,0:T(8,128)(2,1)} %param.10), kind=kOutput, calls=%fused_computation.109 | convolution fusion | flops 1073741824 | bytes 19005440 | tf_op jit(solution)/shard_map/dot_general | solution.py:49
  19.5 98.0 %reduce-scatter.2.cloned.1.call-done = f32[512,512]{1,0:T(8,128)} async-done(((f32[8192,512]{1,0:T(8,128)}), f32[512,512]{1,0:T(8,128)}) %reduce-scatter.2.cloned.1.call-update) | async-done | bytes 1048592 | tf_op jit(solution)/shard_map/reduce_scatter | solution.py:48
  117.5 1.9 reshape.257
  119.5 2.4 broadcast.289.clone
  121.9 2.8 scatter_fusion
  124.7 6.8 %all-to-all-start = ((f32[16,256,256]{2,1,0:T(8,128)}), f32[16,256,256]{2,1,0:T(8,128)}, u32[]{:S(2)}, u32[]{:S(2)}) async-start(f32[16,256,256]{2,1,0:T(8,128)} %scatter_fusion), calls=%async_computation.1 | async-start | bytes 8388608 | tf_op jit(solution)/shard_map/all_to_all | solution.py:72
  134.2 3.8 copy.62
  138.7 56.1 %all-to-all-done = f32[16,256,256]{2,1,0:T(8,128)} async-done(((f32[16,256,256]{2,1,0:T(8,128)}), f32[16,256,256]{2,1,0:T(8,128)}, u32[]{:S(2)}, u32[]{:S(2)}) %all-to-all-start) | async-done | bytes 4194336 | tf_op jit(solution)/shard_map/all_to_all | solution.py:72
  194.8 2.8 gather_fusion
  197.7 4.5 %fusion.11 = f32[6,1,256,256]{3,2,0,1:T(8,128)S(1)} fusion(f32[6,2,256,256]{3,2,0,1:T(8,128)} %bitcast.114, f32[6,256,256]{2,1,0:T(8,128)S(1)} %gather_fusion, f32[6]{0:T(128)S(1)} %convert_element_type.39, pred[6]{0:T(512)(128)(4,1)S(1)} %get-tuple-element.62), kind=kOutput, calls=%fused_computation.22 | convolution fusion | flops 1209139200 | bytes 4718622 | tf_op jit(solution)/shard_map/ski,skj->sij/dot_general | solution.py:84
  202.2 1.9 fusion.13
  204.5 3.5 fusion.42
  208.0 2.5 gather_fusion.1
  212.3 78.4 %while.13 = (s32[]{:T(128)}, f32[4,256,256]{1,2,0:T(8,128)S(1)}, f32[4,256,256]{2,1,0:T(8,128)}, s32[]{:T(128)}) while((s32[]{:T(128)}, f32[4,256,256]{1,2,0:T(8,128)S(1)}, f32[4,256,256]{2,1,0:T(8,128)}, s32[]{:T(128)}) %tuple.36), condition=%wide.region_11.12_spmd.clone, body=%wide.region_10.11_spmd.clone.sunk | while | flops 3222405120 | bytes 15466549 | solution.py:31
  212.5 1.2 copy.79
  213.8 1.9 convolution_bitcast_fusion.2
  215.7 1.3 fusion.71
  218.2 2.1 fusion.73
  220.3 1.2 copy.79
  221.6 1.9 convolution_bitcast_fusion.2
  223.5 1.3 fusion.71
  226.0 2.1 fusion.73
  228.1 1.2 copy.79
  229.5 1.9 convolution_bitcast_fusion.2
  231.4 1.3 fusion.71
  233.8 2.1 fusion.73
  236.0 1.2 copy.79
  237.3 1.9 convolution_bitcast_fusion.2
  239.2 1.3 fusion.71
  241.7 2.1 fusion.73
  243.8 1.2 copy.79
  245.1 1.9 convolution_bitcast_fusion.2
  247.0 1.3 fusion.71
  249.5 2.1 fusion.73
  252.9 1.9 convolution_bitcast_fusion.2
  254.8 1.3 fusion.71
  257.3 2.1 fusion.73
  259.4 1.2 copy.79
  260.7 1.9 convolution_bitcast_fusion.2
  262.7 1.3 fusion.71
  265.1 2.1 fusion.73
  267.2 1.2 copy.79
  268.6 1.9 convolution_bitcast_fusion.2
  270.5 1.3 fusion.71
  272.9 2.1 fusion.73
  275.1 1.2 copy.79
  276.4 1.9 convolution_bitcast_fusion.2
  278.3 1.3 fusion.71
  280.8 2.1 fusion.73
  282.9 1.2 copy.79
  284.2 1.9 convolution_bitcast_fusion.2
  286.1 1.3 fusion.71
  288.6 2.1 fusion.73
  291.6 1.2 copy.48
  292.8 1.8 gather_fusion.2
  294.6 2.1 bitcast_select_fusion.1
  299.3 2.4 broadcast.289
  301.7 3.3 scatter_fusion.1
  305.0 4.9 %all-to-all-start.1 = ((f32[16,256,256]{2,1,0:T(8,128)}), f32[16,256,256]{2,1,0:T(8,128)}, u32[]{:S(2)}, u32[]{:S(2)}) async-start(f32[16,256,256]{2,1,0:T(8,128)} %scatter_fusion.1), calls=%async_computation.2 | async-start | bytes 8388608 | tf_op jit(solution)/shard_map/all_to_all | solution.py:118
  310.1 3.9 %copy.52 = f32[1,6,2,256,256]{4,3,2,1,0:T(8,128)} copy(f32[1,6,2,256,256]{4,3,1,2,0:T(8,128)} %get-tuple-element.52) | data formatting | bytes 6291456
  314.0 1.4 fusion.14
  315.4 61.5 %all-to-all-done.1 = f32[16,256,256]{2,1,0:T(8,128)} async-done(((f32[16,256,256]{2,1,0:T(8,128)}), f32[16,256,256]{2,1,0:T(8,128)}, u32[]{:S(2)}, u32[]{:S(2)}) %all-to-all-start.1) | async-done | bytes 4194336 | tf_op jit(solution)/shard_map/all_to_all | solution.py:118
  376.9 2.8 gather_fusion.3
  (92 shorter events, 26.4 us)
Async XLA Ops:
  7.2 1.6 copy-start
  7.2 110.3 %reduce-scatter.2.cloned.1.call-start = ((), (), s32[]{:S(2)}) async-start(), calls=%async_computation.3 | async-start | bytes 17825792 | tf_op jit(solution)/shard_map/reduce_scatter | solution.py:48
  124.7 70.2 %all-to-all-start = ((f32[16,256,256]{2,1,0:T(8,128)}), f32[16,256,256]{2,1,0:T(8,128)}, u32[]{:S(2)}, u32[]{:S(2)}) async-start(f32[16,256,256]{2,1,0:T(8,128)} %scatter_fusion), calls=%async_computation.1 | async-start | bytes 8388608 | tf_op jit(solution)/shard_map/all_to_all | solution.py:72
  197.7 4.5 %copy-start.3 = (f32[1,6,2,256,256]{4,3,1,2,0:T(8,128)S(1)}, f32[1,6,2,256,256]{4,3,1,2,0:T(8,128)}, u32[]{:S(2)}) copy-start(f32[1,6,2,256,256]{4,3,1,2,0:T(8,128)} %copy.62) | copy-start | bytes 9437188
  305.0 71.9 %all-to-all-start.1 = ((f32[16,256,256]{2,1,0:T(8,128)}), f32[16,256,256]{2,1,0:T(8,128)}, u32[]{:S(2)}, u32[]{:S(2)}) async-start(f32[16,256,256]{2,1,0:T(8,128)} %scatter_fusion.1), calls=%async_computation.2 | async-start | bytes 8388608 | tf_op jit(solution)/shard_map/all_to_all | solution.py:118
  310.1 3.9 %copy-start.2 = (bf16[6,2,256,256]{3,2,1,0:T(8,128)(2,1)S(1)}, bf16[6,2,256,256]{3,2,1,0:T(8,128)(2,1)}, u32[]{:S(2)}) copy-start(bf16[6,2,256,256]{3,2,1,0:T(8,128)(2,1)} %gather_fusion.2) | copy-start | bytes 4718596
  310.1 3.9 %copy-start.4 = (bf16[1,6,2,256,256]{4,3,2,1,0:T(8,128)(2,1)S(1)}, bf16[1,6,2,256,256]{4,3,2,1,0:T(8,128)(2,1)}, u32[]{:S(2)}) copy-start(bf16[1,6,2,256,256]{4,3,2,1,0:T(8,128)(2,1)} %param.12) | copy-start | bytes 4718596
  379.9 1.9 copy-start.1
Sparse Core Ops, SparseCore 0:
  17.9 99.5 reduce-scatter.1
where the time goes:
time: 391 us; the launch traced here: 389 us
  waiting for transfers between devices  216 us (55%)
  matrix products  82.4 us (21%)
  local copies, waits for them, and re-layouts  50.9 us (13%)
  between operations  14.3 us (4%)
  other arithmetic  13 us (3%)
  starting transfers between devices  11.8 us (3%)
    reduce_scatter x1, waiting for transfers between devices, body(): lax.psum_scatter(lax.dot_general(acts, cotangent, (((0,), (0,)), ((), ())...  98 us
    dot_general x42, matrix products, product(): return jnp.matmul(left, right, precision=lax.Precision.HIGHEST)  67 us
    all_to_all x1, waiting for transfers between devices, body(): lax.all_to_all(homeward, 'mp', split_axis=0, concat_axis=0, tiled=True)  61.5 us
    all_to_all x1, waiting for transfers between devices, body(): lax.all_to_all(outgoing, 'mp', split_axis=0, concat_axis=0, tiled=True)  56.1 us
    while x20, local copies, waits for them, and re-layouts  13 us
    unnamed x13, local copies, waits for them, and re-layouts  10.3 us
    dot_general x1, matrix products, body(): lax.dot_general(acts, cotangent, (((0,), (0,)), ((), ())), preferred_elem...  8.99 us
  transfers between devices with their start and end apart: 3, of which 3 were waited for; matrix products, arithmetic and copies ran while one was open for 4% of the time, Pallas kernels for 0%

commit v1 on v0

v1 whole, which is shorter than its diff:
```python
import functools

import jax
import jax.numpy as jnp
from jax import lax
from jax.experimental import pallas as pl
from jax.experimental.pallas import tpu as pltpu
from jax.sharding import PartitionSpec as P

ITERS = 10
REFRESH_MOST = 2
EPSILON = 0.1
PAD = 16
TOP_BITS = 14
F32 = jnp.float32
BF16 = jnp.bfloat16
VMEM = pltpu.VMEM
SMEM = pltpu.SMEM


def matmul(left, right, dims=((1,), (0,))):
    return lax.dot_general(left, right, (dims, ((), ())), preferred_element_type=F32)


def split(x):
    high = x.astype(BF16)
    return high, (x - high.astype(F32)).astype(BF16)


def product(left, right):
    lh, ll = left
    rh, rl = right
    return matmul(
        jnp.concatenate([lh, lh, ll], axis=1), jnp.concatenate([rh, rl, rh], axis=0)
    )


def code(block, out_ref, place):
    edge = block.shape[0]
    most = jnp.maximum(jnp.max(jnp.abs(block), axis=(0, 1), keepdims=True), 1e-30)
    shift = TOP_BITS - jnp.floor(jnp.log2(most))
    scaled = jnp.clip(jnp.round(block * jnp.exp2(shift)), -32767.0, 32767.0)
    out_ref[place, :edge, :] = scaled.astype(jnp.int32).astype(jnp.int16)
    out_ref[place, edge:, :] = jnp.broadcast_to(
        shift.astype(jnp.int32), (PAD, block.shape[1])
    ).astype(jnp.int16)


def decode(in_ref, place, edge):
    whole = in_ref[place, :edge, :].astype(jnp.int32).astype(F32)
    shift = in_ref[place, edge:, :].astype(jnp.int32).astype(F32)[:1, :]
    return whole, jnp.exp2(-shift)


def pick_kernel(meta_ref, acts_ref, out_ref):
    parts, rows, tokens = out_ref.shape
    width = acts_ref.shape[1] // parts
    lanes = 128
    mp_index = meta_ref[0]
    group = mp_index * rows // lanes
    inside = lax.rem(mp_index * rows, lanes)
    row = lax.broadcasted_iota(jnp.int32, (rows, lanes), 0)
    col = lax.broadcasted_iota(jnp.int32, (rows, lanes), 1)
    chosen = (col == row + inside).astype(F32).astype(BF16)
    for part in range(parts):
        start = pl.multiple_of(part * width + group * lanes, lanes)
        piece = acts_ref[:, pl.ds(start, lanes)]
        out_ref[part] = matmul(chosen, piece, ((1,), (1,))).astype(BF16)


def gradient_kernel(edge, meta_ref, left_ref, right_ref, out_ref):
    sources, times, rows, tokens = left_ref.shape
    total = sources * rows
    col_blocks = right_ref.shape[1] // edge
    per_edge = edge // rows
    for row_block in range(total // edge):
        pieces = [
            left_ref[row_block * per_edge : (row_block + 1) * per_edge, t].reshape(edge, tokens)
            for t in range(times)
        ]
        strip = jnp.concatenate(pieces, axis=1)
        for col_block in range(col_blocks):
            block = matmul(strip, right_ref[:, col_block * edge : (col_block + 1) * edge])
            code(block, out_ref, meta_ref[2 + row_block * col_blocks + col_block])


def owner_kernel(
    local_blocks,
    meta_ref,
    in_ref,
    factors_hbm,
    roots_hbm,
    factors_out,
    roots_out,
    out_ref,
    state,
    roots,
    moving,
    current,
    table,
    picked,
    state_in,
    state_done,
    roots_sems,
):
    slots, _, edge, _ = state.shape
    sources = in_ref.shape[0]
    ids = sources * local_blocks
    owners, places, fresh = 2 + local_blocks, 2 + local_blocks + ids, 2 + local_blocks + 2 * ids
    refreshed = meta_ref.shape[0] - fresh
    mp_index = meta_ref[0]
    load_roots = pltpu.make_async_copy(roots_hbm, roots, roots_sems.at[0])
    load_roots.start()
    loads = [
        pltpu.make_async_copy(factors_hbm.at[s], state.at[s], state_in.at[s]) for s in range(slots)
    ]
    saves = [
        pltpu.make_async_copy(state.at[s], factors_out.at[s], state_done.at[s])
        for s in range(slots)
    ]
    for load in loads:
        load.start()

    for s in range(slots + 1):
        table[s] = -1
    for s in range(REFRESH_MOST + 1):
        picked[s] = -1

    def place_block(e, carry):
        held = meta_ref[owners + e] == mp_index
        table[jnp.where(held, meta_ref[places + e], slots)] = e // local_blocks
        return carry

    lax.fori_loop(0, ids, place_block, 0)

    def place_fresh(i, count):
        e = meta_ref[fresh + i]
        held = meta_ref[owners + e] == mp_index
        picked[jnp.where(held, count, REFRESH_MOST)] = meta_ref[places + e]
        return count + held.astype(jnp.int32)

    lax.fori_loop(0, refreshed, place_fresh, jnp.int32(0))

    for s in range(slots):
        loads[s].wait()

        @pl.when(table[s] >= 0)
        def _():
            whole, unit = decode(in_ref, table[s], edge)
            high, low = split(whole)
            unit = unit * unit
            left = jnp.concatenate([high, high, low], axis=1)
            right = jnp.concatenate([high, low, high], axis=1)
            state[s, 0] = state[s, 0] + matmul(left, right, ((1,), (1,))) * unit
            left = jnp.concatenate([high, high, low], axis=0)
            right = jnp.concatenate([high, low, high], axis=0)
            state[s, 1] = state[s, 1] + matmul(left, right, ((0,), (0,))) * unit

        saves[s].start()

    row = lax.broadcasted_iota(jnp.int32, (edge, edge), 0)
    col = lax.broadcasted_iota(jnp.int32, (edge, edge), 1)
    identity = (row == col).astype(F32)
    count = REFRESH_MOST * 2
    for b in range(count):
        slot = jnp.maximum(picked[b // 2], 0)
        shifted = state[slot, b % 2] + EPSILON * identity
        norm = jnp.sqrt(jnp.sum(shifted * shifted, axis=(0, 1), keepdims=True))
        scaled = shifted / norm
        factor = (5.0 * identity - scaled) * 0.25
        current[b] = factor / jnp.sqrt(jnp.sqrt(norm))
        half = split(factor)
        half = split(product(half, half))
        half = split(product(half, half))
        moving[b] = product(half, split(scaled))

    def step(iteration, carry):
        old = [moving[b] for b in range(count)]
        factors = [split((5.0 * identity - old[b]) * 0.25) for b in range(count)]
        squares = [split(product(factors[b], factors[b])) for b in range(count)]
        for b in range(count):
            current[b] = product(split(current[b]), factors[b])
        fourth = [split(product(squares[b], squares[b])) for b in range(count)]
        for b in range(count):
            moving[b] = product(fourth[b], split(old[b]))
        return carry

    lax.fori_loop(1, ITERS - 1, step, 0)
    load_roots.wait()
    for b in range(count):
        factor = split((5.0 * identity - moving[b]) * 0.25)
        final = product(split(current[b]), factor).astype(BF16)

        @pl.when(picked[b // 2] >= 0)
        def _():
            roots[picked[b // 2], b % 2] = final

    save_roots = pltpu.make_async_copy(roots, roots_out, roots_sems.at[1])
    save_roots.start()

    for s in range(slots):

        @pl.when(table[s] >= 0)
        def _():
            whole, unit = decode(in_ref, table[s], edge)
            high, low = split(whole)
            left = roots[s, 0]
            right = roots[s, 1]
            first = matmul(
                jnp.concatenate([left, left], axis=1), jnp.concatenate([high, low], axis=0)
            )
            fh, fl = split(first)
            precond = matmul(
                jnp.concatenate([fh, fl], axis=1), jnp.concatenate([right, right], axis=0)
            )
            precond = precond * unit
            block = whole * unit
            block_sum = jnp.sum(block * block, axis=(0, 1), keepdims=True)
            precond_sum = jnp.sum(precond * precond, axis=(0, 1), keepdims=True)
            ratio = jnp.sqrt(block_sum / (precond_sum + 1e-06))
            code(precond * ratio, out_ref, table[s])

    save_roots.wait()
    for save in saves:
        save.wait()


def home_kernel(edge, meta_ref, in_ref, out_ref):
    col_blocks = out_ref.shape[1] // edge
    for j in range((out_ref.shape[0] // edge) * col_blocks):
        top, left = (j // col_blocks) * edge, (j % col_blocks) * edge
        whole, unit = decode(in_ref, meta_ref[2 + j], edge)
        out_ref[top : top + edge, left : left + edge] = whole * unit


def body(acts, cotangent, factors, roots, owner_of, slot_of, refresh_ids):
    dp_count = lax.axis_size("dp")
    mp_count = lax.axis_size("mp")
    dp_index = lax.axis_index("dp")
    mp_index = lax.axis_index("mp")
    edge = factors.shape[-1]
    slots = factors.shape[1]
    tokens = acts.shape[0]
    row_count = acts.shape[1] // dp_count
    slab = cotangent.shape[1]
    local_blocks = owner_of.shape[2]
    rows = row_count // mp_count

    gathered = lax.all_gather(cotangent, "dp", axis=0, tiled=True)

    owners = lax.dynamic_index_in_dim(owner_of, dp_index, 0, keepdims=False)
    places = lax.dynamic_index_in_dim(slot_of, dp_index, 0, keepdims=False)
    fresh = lax.dynamic_index_in_dim(refresh_ids, dp_index, 0, keepdims=False)
    mine = lax.dynamic_index_in_dim(owners, mp_index, 0, keepdims=False)
    meta = jnp.concatenate(
        [
            jnp.stack([mp_index, dp_index]).astype(jnp.int32),
            mine,
            owners.reshape(-1),
            places.reshape(-1),
            fresh,
        ]
    )

    smem = pl.BlockSpec(memory_space=SMEM)
    vmem = pl.BlockSpec(memory_space=VMEM)
    hbm = pl.BlockSpec(memory_space=pl.ANY)

    picked = pl.pallas_call(
        pick_kernel,
        out_shape=jax.ShapeDtypeStruct((dp_count, rows, tokens), BF16),
        in_specs=[smem, vmem],
        out_specs=vmem,
    )(mp_index.astype(jnp.int32).reshape(1), acts)
    picked = lax.all_to_all(picked, "dp", split_axis=0, concat_axis=0, tiled=True)
    spread = jnp.broadcast_to(picked[None], (mp_count, dp_count, rows, tokens))
    left = lax.all_to_all(spread, "mp", split_axis=0, concat_axis=0, tiled=True)

    coded = jax.ShapeDtypeStruct((mp_count, edge + PAD, edge), jnp.int16)
    outgoing = pl.pallas_call(
        functools.partial(gradient_kernel, edge),
        out_shape=coded,
        in_specs=[smem, vmem, vmem],
        out_specs=vmem,
        compiler_params=pltpu.CompilerParams(vmem_limit_bytes=32 * 1024 * 1024),
    )(meta, left, gathered)
    incoming = lax.all_to_all(outgoing, "mp", split_axis=0, concat_axis=0, tiled=True)

    count = REFRESH_MOST * 2
    factors_next, roots_next, homeward = pl.pallas_call(
        functools.partial(owner_kernel, local_blocks),
        out_shape=(
            jax.ShapeDtypeStruct(factors.shape[1:], F32),
            jax.ShapeDtypeStruct(roots.shape[1:], BF16),
            coded,
        ),
        in_specs=[smem, vmem, hbm, hbm],
        out_specs=(hbm, hbm, vmem),
        scratch_shapes=[
            VMEM(factors.shape[1:], F32),
            VMEM(roots.shape[1:], BF16),
            VMEM((count, edge, edge), F32),
            VMEM((count, edge, edge), F32),
            SMEM((slots + 1,), jnp.int32),
            SMEM((REFRESH_MOST + 1,), jnp.int32),
            pltpu.SemaphoreType.DMA((slots,)),
            pltpu.SemaphoreType.DMA((slots,)),
            pltpu.SemaphoreType.DMA((2,)),
        ],
        compiler_params=pltpu.CompilerParams(vmem_limit_bytes=40 * 1024 * 1024),
    )(meta, incoming, factors[0], roots[0])
    returned = lax.all_to_all(homeward, "mp", split_axis=0, concat_axis=0, tiled=True)

    direction = pl.pallas_call(
        functools.partial(home_kernel, edge),
        out_shape=jax.ShapeDtypeStruct((row_count, slab), F32),
        in_specs=[smem, vmem],
        out_specs=vmem,
    )(meta, returned)
    return (direction, factors_next[None], roots_next[None])


def solution(mesh):
    in_specs = (
        P("dp", None),
        P("dp", "mp"),
        P("dp", "mp", None, None, None),
        P("dp", "mp", None, None, None),
        P(),
        P(),
        P(),
    )
    out_specs = (P("dp", "mp"), P("dp", "mp", None, None, None), P("dp", "mp", None, None, None))
    return jax.shard_map(body, mesh=mesh, in_specs=in_specs, out_specs=out_specs, check_vma=False)
```

time: 391 us -> 177 us (0.45)
  the two profiles are of different devices: /device:TPU:96 before, /device:TPU:2 now
where the time goes in v1:
time: 177 us; the launch traced here: 176 us
  blocking collectives  88.1 us (50%)
  Pallas kernels  32 us (18%)
  waiting for transfers between devices  28.9 us (16%)
  between operations  14.1 us (8%)
  starting transfers between devices  7.52 us (4%)
  local copies, waits for them, and re-layouts  5.35 us (3%)
    all_to_all x1, blocking collectives, body(): lax.all_to_all(outgoing, 'mp', split_axis=0, concat_axis=0, tiled=True)  36.5 us
    all_to_all x1, blocking collectives, body(): lax.all_to_all(homeward, 'mp', split_axis=0, concat_axis=0, tiled=True)  34.3 us
    all_to_all x1, waiting for transfers between devices, body(): left = lax.all_to_all(spread, 'mp', split_axis=0, concat_axis=0, tiled=True)  28.3 us
    pallas_call x1, Pallas kernels, body(): pl.pallas_call(functools.partial(owner_kernel, local_blocks), out_shape=(...  24.6 us
    all_to_all x1, blocking collectives, body(): lax.all_to_all(picked, 'dp', split_axis=0, concat_axis=0, tiled=True)  17.3 us
    all_to_all x1, starting transfers between devices, body(): left = lax.all_to_all(spread, 'mp', split_axis=0, concat_axis=0, tiled=True)  7.48 us
  transfers between devices with their start and end apart: 2, of which 1 were waited for; matrix products, arithmetic and copies ran while one was open for 2% of the time, Pallas kernels for 2%

profile of v1, /device:TPU:2, one launch (start us, length us, event | category | flops | bytes accessed | tf_op | source)
XLA Modules:
  0.0 176.0 jit_solution(3022997177842618803)
XLA Ops:
  7.2 0.0 copy-start
  7.2 0.0 all-gather.2.cloned.1.call-start
  7.2 0.7 all-gather.2.cloned.1.call-update
  7.9 2.6 %shard_map.94 = bf16[16,32,128]{2,1,0:T(8,128)(2,1)} custom-call(s32[1]{0:T(128)} %bitcast.meta_ref, bf16[128,8192]{1,0:T(8,128)(2,1)} %acts_ref.1), custom_call_target="tpu_custom_call" | custom-call | tf_op jit(solution)/shard_map/pallas_call | solution.py:269
  10.6 17.3 %all_to_all.20 = bf16[16,32,128]{2,1,0:T(8,128)(2,1)S(1)} all-to-all(bf16[16,32,128]{2,1,0:T(8,128)(2,1)} %shard_map.94), channel_id=1, replica_groups=mesh['dp'=16,'mp'=16] {'dp'}, dimensions={0} | all-to-all | bytes 262144 | tf_op jit(solution)/shard_map/all_to_all | solution.py:275
  27.9 1.7 broadcast_in_dim.12
  29.6 7.5 %all-to-all-start.1 = ((bf16[16,16,32,128]{3,2,1,0:T(8,128)(2,1)}), bf16[16,16,32,128]{3,2,1,0:T(8,128)(2,1)S(1)}, u32[]{:S(2)}, u32[]{:S(2)}) async-start(bf16[16,16,32,128]{3,2,1,0:T(8,128)(2,1)} %broadcast_in_dim.12), calls=%async_computation.1 | async-start | bytes 4194304 | tf_op jit(solution)/shard_map/all_to_all | solution.py:277
  37.1 0.7 constant_dynamic-slice_fusion.1
  37.8 0.1 copy.13
  37.9 0.1 reshape.19
  38.0 0.1 copy.12
  38.0 0.1 reshape.18
  38.1 0.9 dynamic-slice_reduce_fusion
  39.0 0.0 copy-done
  39.0 0.1 concatenate.3.meta_ref
  39.1 0.0 copy-start.4
  39.1 28.3 %all-to-all-done.1.left_ref = bf16[16,16,32,128]{3,2,1,0:T(8,128)(2,1)S(1)} async-done(((bf16[16,16,32,128]{3,2,1,0:T(8,128)(2,1)}), bf16[16,16,32,128]{3,2,1,0:T(8,128)(2,1)S(1)}, u32[]{:S(2)}, u32[]{:S(2)}) %all-to-all-start.1) | async-done | bytes 2097184 | tf_op jit(solution)/shard_map/all_to_all | solution.py:277
  67.4 0.0 all-gather.2.cloned.1.call-done.right_ref
  67.4 0.0 copy-start.2
  67.4 1.6 copy-done.2
  69.0 0.0 copy-start.3
  69.0 2.0 %shard_map.95 = s16[16,272,256]{2,1,0:T(8,128)(2,1)S(1)} custom-call(s32[150]{0:T(256)S(1)} %concatenate.3.meta_ref, bf16[16,16,32,128]{3,2,1,0:T(8,128)(2,1)S(1)} %all-to-all-done.1.left_ref, bf16[2048,512]{1,0:T(8,128)(2,1)S(1)} %copy-done.2), custom_call_target="tpu_custom_call" | custom-call | tf_op jit(solution)/shard_map/pallas_call | solution.py:280
  71.0 0.0 copy-start.1
  71.0 36.5 %all_to_all.21.in_ref = s16[16,272,256]{2,1,0:T(8,128)(2,1)S(1)} all-to-all(s16[16,272,256]{2,1,0:T(8,128)(2,1)S(1)} %shard_map.95), channel_id=1, replica_groups=mesh['dp'=16,'mp'=16] {'mp'}, dimensions={0} | all-to-all | bytes 4456448 | tf_op jit(solution)/shard_map/all_to_all | solution.py:287
  107.5 0.0 copy-done.4
  107.5 0.0 copy-done.3
  107.5 0.0 copy-done.1
  107.5 24.6 %shard_map.96 = (f32[6,2,256,256]{3,2,1,0:T(8,128)}, bf16[6,2,256,256]{3,2,1,0:T(8,128)(2,1)}, s16[16,272,256]{2,1,0:T(8,128)(2,1)S(1)}) custom-call(s32[150]{0:T(256)S(1)} %concatenate.3.meta_ref, s16[16,272,256]{2,1,0:T(8,128)(2,1)S(1)} %all_to_all.21.in_ref, f32[6,2,256,256]{3,2,1,0:T(8,128)S(1)} %bitcast.8, bf16[6,2,256,256]{3,2,1,0:T(8,128)(2,1)S(1)} %bitcast.9), custom_call_target="tpu_custom_call" | custom-call | tf_op jit(solution)/shard_map/pallas_call | solution.py:290
  132.2 34.3 %all_to_all.22.in_ref = s16[16,272,256]{2,1,0:T(8,128)(2,1)} all-to-all(s16[16,272,256]{2,1,0:T(8,128)(2,1)S(1)} %get-tuple-element.6), channel_id=1, replica_groups=mesh['dp'=16,'mp'=16] {'mp'}, dimensions={0} | all-to-all | bytes 4456448 | tf_op jit(solution)/shard_map/all_to_all | solution.py:312
  166.4 2.7 %shard_map.97 = f32[512,512]{1,0:T(8,128)} custom-call(s32[150]{0:T(256)} %copy-done.4, s16[16,272,256]{2,1,0:T(8,128)(2,1)} %all_to_all.22.in_ref), custom_call_target="tpu_custom_call" | custom-call | tf_op jit(solution)/shard_map/pallas_call | solution.py:314
  (1 shorter events, 0.0 us)
Async XLA Ops:
  7.2 31.8 %copy-start = (s32[16,16]{1,0:T(8,128)S(1)}, s32[16,16]{1,0:T(8,128)}, u32[]{:S(2)}) copy-start(s32[16,16]{1,0:T(8,128)} %param.13) | copy-start | bytes 3076
  7.2 60.2 %all-gather.2.cloned.1.call-start = ((), (), s32[]{:S(2)}) async-start(), calls=%async_computation.4 | async-start | bytes 2228224 | tf_op jit(solution)/shard_map/all_gather | solution.py:249
  29.6 37.8 %all-to-all-start.1 = ((bf16[16,16,32,128]{3,2,1,0:T(8,128)(2,1)}), bf16[16,16,32,128]{3,2,1,0:T(8,128)(2,1)S(1)}, u32[]{:S(2)}, u32[]{:S(2)}) async-start(bf16[16,16,32,128]{3,2,1,0:T(8,128)(2,1)} %broadcast_in_dim.12), calls=%async_computation.1 | async-start | bytes 4194304 | tf_op jit(solution)/shard_map/all_to_all | solution.py:277
  39.1 68.4 %copy-start.4 = (s32[150]{0:T(256)}, s32[150]{0:T(256)S(1)}, u32[]{:S(2)}) copy-start(s32[150]{0:T(256)S(1)} %concatenate.3.meta_ref) | copy-start | bytes 1804
  67.4 1.6 copy-start.2
  69.0 38.6 %copy-start.3 = (bf16[1,6,2,256,256]{4,3,2,1,0:T(8,128)(2,1)S(1)}, bf16[1,6,2,256,256]{4,3,2,1,0:T(8,128)(2,1)}, u32[]{:S(2)}) copy-start(bf16[1,6,2,256,256]{4,3,2,1,0:T(8,128)(2,1)} %param.10) | copy-start | bytes 4718596
  71.0 36.5 %copy-start.1 = (f32[1,6,2,256,256]{4,3,2,1,0:T(8,128)S(1)}, f32[1,6,2,256,256]{4,3,2,1,0:T(8,128)}, u32[]{:S(2)}) copy-start(f32[1,6,2,256,256]{4,3,2,1,0:T(8,128)} %param.9) | copy-start | bytes 9437188
Sparse Core Ops, SparseCore 0:
  9.8 42.4 all-gather.1

commit v2 on v1

v2 whole, which is shorter than its diff:
```python
import functools

import jax
import jax.numpy as jnp
from jax import lax
from jax.experimental import pallas as pl
from jax.experimental.pallas import tpu as pltpu
from jax.sharding import PartitionSpec as P

ITERS = 10
REFRESH_MOST = 2
EPSILON = 0.1
PAD = 16
TOP_BITS = 14
F32 = jnp.float32
BF16 = jnp.bfloat16
VMEM = pltpu.VMEM
SMEM = pltpu.SMEM


def matmul(left, right, dims=((1,), (0,))):
    return lax.dot_general(left, right, (dims, ((), ())), preferred_element_type=F32)


def split(x):
    high = x.astype(BF16)
    return high, (x - high.astype(F32)).astype(BF16)


def product(left, right):
    lh, ll = left
    rh, rl = right
    return matmul(
        jnp.concatenate([lh, lh, ll], axis=1), jnp.concatenate([rh, rl, rh], axis=0)
    )


def quantized(values, shift):
    scaled = jnp.clip(jnp.round(values * jnp.exp2(shift)), -32767.0, 32767.0)
    return scaled.astype(jnp.int32).astype(jnp.int16)


def code(block, out_ref, place):
    edge = block.shape[0]
    most = jnp.maximum(jnp.max(jnp.abs(block), axis=(0, 1), keepdims=True), 1e-30)
    shift = TOP_BITS - jnp.floor(jnp.log2(most))
    out_ref[place, :edge, :] = quantized(block, shift)
    out_ref[place, edge:, :] = jnp.broadcast_to(
        shift.astype(jnp.int32), (PAD, block.shape[1])
    ).astype(jnp.int16)


def decode(in_ref, place, edge):
    whole = in_ref[place, :edge, :].astype(jnp.int32).astype(F32)
    shift = in_ref[place, edge:, :].astype(jnp.int32).astype(F32)[:1, :]
    return whole, jnp.exp2(-shift)


def pick_kernel(acts_ref, out_ref):
    parts, rows, tokens = out_ref.shape
    width = acts_ref.shape[1] // parts
    lanes = 128
    mp_index = lax.axis_index("mp")
    group = mp_index * rows // lanes
    inside = lax.rem(mp_index * rows, lanes)
    row = lax.broadcasted_iota(jnp.int32, (rows, lanes), 0)
    col = lax.broadcasted_iota(jnp.int32, (rows, lanes), 1)
    chosen = (col == row + inside).astype(F32).astype(BF16)
    for part in range(parts):
        start = pl.multiple_of(part * width + group * lanes, lanes)
        piece = acts_ref[:, pl.ds(start, lanes)]
        out_ref[part] = matmul(chosen, piece, ((1,), (1,))).astype(BF16)


def strip_kernel(edge, cot_ref, out_ref):
    owners, rows, lanes = out_ref.shape
    blocks = cot_ref.shape[1] // edge
    depth = rows // blocks
    row = lax.broadcasted_iota(jnp.int32, (lanes, lanes), 0)
    col = lax.broadcasted_iota(jnp.int32, (lanes, lanes), 1)
    identity = (row == col).astype(F32).astype(BF16)
    for chunk in range(cot_ref.shape[1] // lanes):
        piece = cot_ref[:, chunk * lanes : (chunk + 1) * lanes]
        turned = matmul(identity, piece, ((1,), (1,))).astype(BF16)
        block, first = divmod(chunk * lanes, edge)
        for k in range(lanes // depth):
            out_ref[first // depth + k, block * depth : (block + 1) * depth, :] = turned[
                k * depth : (k + 1) * depth
            ]


def gradient_kernel(edge, slots, owner_ref, place_ref, left_hbm, *refs):
    rights_hbm, (out_ref, left_ref, rights, shifts, sems) = refs[:-5], refs[-5:]
    sources, times, rows, tokens = left_ref.shape
    copies = [pltpu.make_async_copy(left_hbm, left_ref, sems.at[times])] + [
        pltpu.make_async_copy(rights_hbm[k], rights.at[k], sems.at[k]) for k in range(times)
    ]
    for copy in copies:
        copy.start()
    depth = edge // sources
    dp_index = lax.axis_index("dp")
    shifts[...] = jnp.zeros_like(shifts)
    total = sources * rows
    when = [token_group(dp_index, times, k) for k in range(times)]
    for copy in copies:
        copy.wait()
    left = jnp.concatenate([left_ref[:, t].reshape(total, tokens) for t in when], axis=1)
    slab = rights.shape[1]
    col_blocks = slab // (sources * depth)
    for chunk in range(slab // edge):
        strips = jnp.concatenate(
            [rights[k, chunk * edge : (chunk + 1) * edge, :] for k in range(times)], axis=1
        )
        product_t = matmul(strips, left, ((1,), (1,))).reshape(edge // depth, depth, total)
        for row_block in range(total // edge):
            values = product_t[:, :, row_block * edge : (row_block + 1) * edge]
            most = jnp.max(jnp.abs(values), axis=(1, 2), keepdims=True)
            shift = TOP_BITS - jnp.floor(jnp.log2(jnp.maximum(most, 1e-30)))
            coded = quantized(values, shift)
            for k in range(edge // depth):
                m, col_block = divmod(chunk * (edge // depth) + k, col_blocks)
                j = row_block * col_blocks + col_block
                owner, place = owner_ref[dp_index, j, m], place_ref[dp_index, j, m]
                top = pl.multiple_of(place * depth, depth)
                out_ref[owner, pl.ds(top, depth), :] = coded[k]
                shifts[owner, pl.ds(place, 1), :] = jnp.broadcast_to(shift[k], (1, edge))
    out_ref[:, slots * depth :, :] = shifts[...].astype(jnp.int32).astype(jnp.int16)


def ring_offsets(chips):
    offsets = [0]
    for step in range(1, chips // 2):
        offsets += [-step, step]
    return offsets + [-(chips // 2)]


def token_group(dp_index, times, k):
    chips = times // 2
    offset = ring_offsets(chips)[k % chips]
    core = lax.rem(dp_index, 2)
    core = core if k < chips else 1 - core
    return lax.rem(dp_index // 2 + (offset + chips), chips) * 2 + core


def owner_kernel(
    owner_ref,
    place_ref,
    fresh_ref,
    in_ref,
    factors_hbm,
    roots_hbm,
    factors_out,
    roots_out,
    out_ref,
    state,
    roots,
    units,
    halves,
    moving,
    current,
    table,
    picked,
    state_in,
    state_done,
    roots_sems,
):
    slots, _, edge, _ = state.shape
    local_blocks, sources = owner_ref.shape[1:]
    dp_index, mp_index = lax.axis_index("dp"), lax.axis_index("mp")
    load_roots = pltpu.make_async_copy(roots_hbm, roots, roots_sems.at[0])
    load_roots.start()
    loads = [
        pltpu.make_async_copy(factors_hbm.at[s], state.at[s], state_in.at[s]) for s in range(slots)
    ]
    saves = [
        pltpu.make_async_copy(state.at[s], factors_out.at[s], state_done.at[s])
        for s in range(slots)
    ]
    for load in loads:
        load.start()

    for s in range(slots + 1):
        table[s] = -1
    for s in range(REFRESH_MOST + 1):
        picked[s] = -1

    def place_source(m, carry):
        for j in range(local_blocks):
            held = owner_ref[dp_index, j, m] == mp_index
            table[jnp.where(held, place_ref[dp_index, j, m], slots)] = m
        return carry

    lax.fori_loop(0, sources, place_source, 0)

    def place_fresh(i, count):
        block = fresh_ref[dp_index, i]
        m, j = block // local_blocks, lax.rem(block, local_blocks)
        held = owner_ref[dp_index, j, m] == mp_index
        picked[jnp.where(held, count, REFRESH_MOST)] = place_ref[dp_index, j, m]
        return count + held.astype(jnp.int32)

    lax.fori_loop(0, fresh_ref.shape[1], place_fresh, jnp.int32(0))

    depth = edge // sources
    units[...] = jnp.exp2(-in_ref[:, slots * depth :, :].astype(jnp.int32).astype(F32))
    for s in range(slots):
        loads[s].wait()

        @pl.when(table[s] >= 0)
        def _():
            whole = in_ref[:, s * depth : (s + 1) * depth, :].astype(jnp.int32).astype(F32)
            high, low = split((whole * units[:, s : s + 1, :]).reshape(edge, edge))
            halves[s, 0] = high
            halves[s, 1] = low
            left = jnp.concatenate([high, high, low], axis=0)
            right = jnp.concatenate([high, low, high], axis=0)
            state[s, 0] = state[s, 0] + matmul(left, right, ((0,), (0,)))
            left = jnp.concatenate([high, high, low], axis=1)
            right = jnp.concatenate([high, low, high], axis=1)
            state[s, 1] = state[s, 1] + matmul(left, right, ((1,), (1,)))

        saves[s].start()

    row = lax.broadcasted_iota(jnp.int32, (edge, edge), 0)
    col = lax.broadcasted_iota(jnp.int32, (edge, edge), 1)
    identity = (row == col).astype(F32)
    count = REFRESH_MOST * 2
    for b in range(count):
        slot = jnp.maximum(picked[b // 2], 0)
        shifted = state[slot, b % 2] + EPSILON * identity
        norm = jnp.sqrt(jnp.sum(shifted * shifted, axis=(0, 1), keepdims=True))
        scaled = shifted / norm
        factor = (5.0 * identity - scaled) * 0.25
        current[b] = factor / jnp.sqrt(jnp.sqrt(norm))
        half = split(factor)
        half = split(product(half, half))
        half = split(product(half, half))
        moving[b] = product(half, split(scaled))

    def step(iteration, carry):
        old = [moving[b] for b in range(count)]
        factors = [split((5.0 * identity - old[b]) * 0.25) for b in range(count)]
        squares = [split(product(factors[b], factors[b])) for b in range(count)]
        for b in range(count):
            current[b] = product(split(current[b]), factors[b])
        fourth = [split(product(squares[b], squares[b])) for b in range(count)]
        for b in range(count):
            moving[b] = product(fourth[b], split(old[b]))
        return carry

    lax.fori_loop(1, ITERS - 1, step, 0)
    load_roots.wait()
    for b in range(count):
        factor = split((5.0 * identity - moving[b]) * 0.25)
        final = product(split(current[b]), factor).astype(BF16)

        @pl.when(picked[b // 2] >= 0)
        def _():
            roots[picked[b // 2], b % 2] = final

    save_roots = pltpu.make_async_copy(roots, roots_out, roots_sems.at[1])
    save_roots.start()

    for s in range(slots):

        @pl.when(table[s] >= 0)
        def _():
            high, low = halves[s, 0], halves[s, 1]
            left = roots[s, 0]
            right = roots[s, 1]
            first = matmul(
                jnp.concatenate([high, low], axis=0),
                jnp.concatenate([right, right], axis=0),
                ((0,), (0,)),
            )
            fh, fl = split(first)
            precond = matmul(
                jnp.concatenate([left, left], axis=1), jnp.concatenate([fh, fl], axis=0)
            )
            block = high.astype(F32) + low.astype(F32)
            block_sum = jnp.sum(block * block, axis=(0, 1), keepdims=True)
            precond_sum = jnp.sum(precond * precond, axis=(0, 1), keepdims=True)
            ratio = jnp.sqrt(block_sum / (precond_sum + 1e-06))
            code(precond * ratio, out_ref, table[s])

    save_roots.wait()
    for save in saves:
        save.wait()


def home_kernel(edge, owner_ref, in_hbm, out_ref, blocks, sems):
    dp_index, mp_index = lax.axis_index("dp"), lax.axis_index("mp")
    col_blocks = out_ref.shape[1] // edge
    copies = [
        pltpu.make_async_copy(
            in_hbm.at[owner_ref[dp_index, j, mp_index]], blocks.at[j], sems.at[j]
        )
        for j in range(blocks.shape[0])
    ]
    for copy in copies:
        copy.start()
    for j, copy in enumerate(copies):
        copy.wait()
        top, left = (j // col_blocks) * edge, (j % col_blocks) * edge
        whole, unit = decode(blocks, j, edge)
        out_ref[top : top + edge, left : left + edge] = whole * unit


def body(acts, cotangent, factors, roots, owner_of, slot_of, refresh_ids):
    dp_count = lax.axis_size("dp")
    mp_count = lax.axis_size("mp")
    edge = factors.shape[-1]
    slots = factors.shape[1]
    tokens = acts.shape[0]
    row_count = acts.shape[1] // dp_count
    slab = cotangent.shape[1]
    rows = row_count // mp_count
    owner_of = owner_of.transpose(0, 2, 1)
    slot_of = slot_of.transpose(0, 2, 1)

    smem = pl.BlockSpec(memory_space=SMEM)
    vmem = pl.BlockSpec(memory_space=VMEM)
    hbm = pl.BlockSpec(memory_space=pl.ANY)

    up = [(i, (i + 2) % dp_count) for i in range(dp_count)]
    down = [(i, (i - 2) % dp_count) for i in range(dp_count)]
    swap = [(i, i ^ 1) for i in range(dp_count)]

    picked = pl.pallas_call(
        pick_kernel,
        out_shape=jax.ShapeDtypeStruct((dp_count, rows, tokens), BF16),
        in_specs=[vmem],
        out_specs=vmem,
    )(acts)

    def ring(above, below):
        return lax.ppermute(above, "dp", up), lax.ppermute(below, "dp", down)

    def swapped(x):
        return lax.ppermute(x, "dp", swap)

    strips = pl.pallas_call(
        functools.partial(strip_kernel, edge),
        out_shape=jax.ShapeDtypeStruct((mp_count, slab // mp_count, tokens), BF16),
        in_specs=[vmem],
        out_specs=vmem,
    )(cotangent)
    strips = lax.all_to_all(strips, "mp", split_axis=0, concat_axis=0, tiled=True)
    strips = strips.reshape(slab, tokens)
    first = ring(strips, strips)
    own = lax.all_to_all(picked, "dp", split_axis=0, concat_axis=0, tiled=True)
    own, first = lax.optimization_barrier((own, first))
    spread = jnp.broadcast_to(own[None], (mp_count, dp_count, rows, tokens))
    left = lax.all_to_all(spread, "mp", split_axis=0, concat_axis=0, tiled=True)
    second = ring(*first)
    third = ring(*second)
    third_swapped = [swapped(x) for x in third]
    last = ring(third[0], third_swapped[1])
    same = [strips, *first, *second, *third, last[0]]
    gathered = same + [swapped(x) for x in same[:5]] + third_swapped + [last[1]]

    depth = edge // mp_count
    outgoing = pl.pallas_call(
        functools.partial(gradient_kernel, edge, slots),
        out_shape=jax.ShapeDtypeStruct((mp_count, slots * depth + PAD, edge), jnp.int16),
        in_specs=[smem, smem, hbm] + [hbm] * len(gathered),
        out_specs=vmem,
        scratch_shapes=[
            VMEM((mp_count, dp_count, rows, tokens), BF16),
            VMEM((dp_count, slab, tokens), BF16),
            VMEM((mp_count, PAD, edge), F32),
            pltpu.SemaphoreType.DMA((dp_count + 1,)),
        ],
        compiler_params=pltpu.CompilerParams(vmem_limit_bytes=60 * 1024 * 1024),
    )(owner_of, slot_of, left, *gathered)
    incoming = lax.all_to_all(outgoing, "mp", split_axis=0, concat_axis=0, tiled=True)

    count = REFRESH_MOST * 2
    factors_next, roots_next, homeward = pl.pallas_call(
        owner_kernel,
        out_shape=(
            jax.ShapeDtypeStruct(factors.shape[1:], F32),
            jax.ShapeDtypeStruct(roots.shape[1:], BF16),
            jax.ShapeDtypeStruct((mp_count, edge + PAD, edge), jnp.int16),
        ),
        in_specs=[smem, smem, smem, vmem, hbm, hbm],
        out_specs=(hbm, hbm, vmem),
        scratch_shapes=[
            VMEM(factors.shape[1:], F32),
            VMEM(roots.shape[1:], BF16),
            VMEM((mp_count, PAD, edge), F32),
            VMEM((slots, 2, edge, edge), BF16),
            VMEM((count, edge, edge), F32),
            VMEM((count, edge, edge), F32),
            SMEM((slots + 1,), jnp.int32),
            SMEM((REFRESH_MOST + 1,), jnp.int32),
            pltpu.SemaphoreType.DMA((slots,)),
            pltpu.SemaphoreType.DMA((slots,)),
            pltpu.SemaphoreType.DMA((2,)),
        ],
        compiler_params=pltpu.CompilerParams(vmem_limit_bytes=28 * 1024 * 1024),
    )(owner_of, slot_of, refresh_ids, incoming, factors[0], roots[0])
    returned = lax.all_to_all(homeward, "mp", split_axis=0, concat_axis=0, tiled=True)

    local_blocks = owner_of.shape[1]
    direction = pl.pallas_call(
        functools.partial(home_kernel, edge),
        out_shape=jax.ShapeDtypeStruct((row_count, slab), F32),
        in_specs=[smem, hbm],
        out_specs=vmem,
        scratch_shapes=[
            VMEM((local_blocks, edge + PAD, edge), jnp.int16),
            pltpu.SemaphoreType.DMA((local_blocks,)),
        ],
    )(owner_of, returned)
    return (direction, factors_next[None], roots_next[None])


def solution(mesh):
    in_specs = (
        P("dp", None),
        P("dp", "mp"),
        P("dp", "mp", None, None, None),
        P("dp", "mp", None, None, None),
        P(),
        P(),
        P(),
    )
    out_specs = (P("dp", "mp"), P("dp", "mp", None, None, None), P("dp", "mp", None, None, None))
    return jax.shard_map(body, mesh=mesh, in_specs=in_specs, out_specs=out_specs, check_vma=False)
```

time: 177 us -> 165 us (0.932)
  the two profiles are of different devices: /device:TPU:2 before, /device:TPU:96 now
where the time goes in v2:
time: 165 us; the launch traced here: 164 us
  blocking collectives  49.7 us (30%)
  Pallas kernels  44 us (27%)
  waiting for transfers between devices  33.3 us (20%)
  starting transfers between devices  33.1 us (20%)
  local copies, waits for them, and re-layouts  3.11 us (2%)
    all_to_all x1, blocking collectives, body(): lax.all_to_all(homeward, 'mp', split_axis=0, concat_axis=0, tiled=True)  30.6 us
    pallas_call x1, Pallas kernels, body(): pl.pallas_call(owner_kernel, out_shape=(jax.ShapeDtypeStruct(factors.shap...  29.7 us
    all_to_all x1, blocking collectives, body(): lax.all_to_all(outgoing, 'mp', split_axis=0, concat_axis=0, tiled=True)  19.1 us
    ppermute x8, waiting for transfers between devices, ring(): return (lax.ppermute(above, 'dp', up), lax.ppermute(below, 'dp', down))  15.6 us
    ppermute x8, starting transfers between devices, ring(): return (lax.ppermute(above, 'dp', up), lax.ppermute(below, 'dp', down))  13 us
    all_to_all x1, waiting for transfers between devices, body(): left = lax.all_to_all(spread, 'mp', split_axis=0, concat_axis=0, tiled=True)  9.19 us
    all_to_all x1, starting transfers between devices, body(): own = lax.all_to_all(picked, 'dp', split_axis=0, concat_axis=0, tiled=True)  7.68 us
    all_to_all x1, starting transfers between devices, body(): lax.all_to_all(strips, 'mp', split_axis=0, concat_axis=0, tiled=True)  7.03 us
  transfers between devices with their start and end apart: 18, of which 8 were waited for; matrix products, arithmetic and copies ran while one was open for 0% of the time, Pallas kernels for 2%

profile of v2, /device:TPU:96, one launch (start us, length us, event | category | flops | bytes accessed | tf_op | source)
XLA Modules:
  0.0 164.2 jit_solution(11731224013247169352)
XLA Ops:
  0.6 1.8 %shard_map.95 = bf16[16,32,128]{2,1,0:T(8,128)(2,1)} custom-call(bf16[128,512]{1,0:T(8,128)(2,1)} %cot_ref.1), custom_call_target="tpu_custom_call" | custom-call | tf_op jit(solution)/shard_map/pallas_call | solution.py:342
  2.4 7.0 %all-to-all-start.1 = ((bf16[16,32,128]{2,1,0:T(8,128)(2,1)}), bf16[16,32,128]{2,1,0:T(8,128)(2,1)S(1)}, u32[]{:S(2)}, u32[]{:S(2)}) async-start(bf16[16,32,128]{2,1,0:T(8,128)(2,1)} %shard_map.95), calls=%async_computation.1 | async-start | bytes 262144 | tf_op jit(solution)/shard_map/all_to_all | solution.py:348
  9.4 2.6 %shard_map.94 = bf16[16,32,128]{2,1,0:T(8,128)(2,1)} custom-call(bf16[128,8192]{1,0:T(8,128)(2,1)} %acts_ref.1), custom_call_target="tpu_custom_call" | custom-call | tf_op jit(solution)/shard_map/pallas_call | solution.py:329
  12.1 5.3 %all-to-all-done.1 = bf16[16,32,128]{2,1,0:T(8,128)(2,1)S(1)} async-done(((bf16[16,32,128]{2,1,0:T(8,128)(2,1)}), bf16[16,32,128]{2,1,0:T(8,128)(2,1)S(1)}, u32[]{:S(2)}, u32[]{:S(2)}) %all-to-all-start.1) | async-done | bytes 131104 | tf_op jit(solution)/shard_map/all_to_all | solution.py:348
  17.4 7.7 %all-to-all-start = ((bf16[16,32,128]{2,1,0:T(8,128)(2,1)}), bf16[16,32,128]{2,1,0:T(8,128)(2,1)S(1)}, u32[]{:S(2)}, u32[]{:S(2)}) async-start(bf16[16,32,128]{2,1,0:T(8,128)(2,1)} %shard_map.94), calls=%async_computation | async-start | bytes 262144 | tf_op jit(solution)/shard_map/all_to_all | solution.py:351
  25.1 0.6 collective-permute-start.1
  25.7 2.7 %collective-permute-start = (bf16[512,128]{1,0:T(8,128)(2,1)S(1)}, bf16[512,128]{1,0:T(8,128)(2,1)S(1)}, u32[]{:S(2)}, u32[]{:S(2)}) collective-permute-start(bf16[512,128]{1,0:T(8,128)(2,1)S(1)} %bitcast.15), channel_id=1, source_target_pairs={{0,32},{16,48},{32,64},{48,80},{64,96},{80,112},{96,128},{112,144}... | collective-permute-start | bytes 393224 | tf_op jit(solution)/shard_map/ppermute | solution.py:337
  28.4 3.1 %all-to-all-done = bf16[16,32,128]{2,1,0:T(8,128)(2,1)S(1)} async-done(((bf16[16,32,128]{2,1,0:T(8,128)(2,1)}), bf16[16,32,128]{2,1,0:T(8,128)(2,1)S(1)}, u32[]{:S(2)}, u32[]{:S(2)}) %all-to-all-start) | async-done | bytes 131104 | tf_op jit(solution)/shard_map/all_to_all | solution.py:351
  31.5 3.1 %collective-permute-done.1.refs_2_ = bf16[512,128]{1,0:T(8,128)(2,1)S(1)} collective-permute-done((bf16[512,128]{1,0:T(8,128)(2,1)S(1)}, bf16[512,128]{1,0:T(8,128)(2,1)S(1)}, u32[]{:S(2)}, u32[]{:S(2)}) %collective-permute-start.1) | collective-permute-done | bytes 131104 | tf_op jit(solution)/shard_map/ppermute | solution.py:337
  34.6 0.0 collective-permute-done.refs_1_
  34.6 1.7 %broadcast_in_dim.12 = bf16[16,16,32,128]{3,2,1,0:T(8,128)(2,1)} broadcast(bf16[16,32,128]{2,1,0:T(8,128)(2,1)S(1)} %all-to-all-done), dimensions={1,2,3} | broadcast | bytes 2228224 | tf_op jit(solution)/shard_map/broadcast_in_dim | solution.py:353
  36.3 3.7 %all-to-all-start.2 = ((bf16[16,16,32,128]{3,2,1,0:T(8,128)(2,1)}), bf16[16,16,32,128]{3,2,1,0:T(8,128)(2,1)S(1)}, u32[]{:S(2)}, u32[]{:S(2)}) async-start(bf16[16,16,32,128]{3,2,1,0:T(8,128)(2,1)} %broadcast_in_dim.12), calls=%async_computation.2 | async-start | bytes 4194304 | tf_op jit(solution)/shard_map/all_to_all | solution.py:354
  40.1 0.1 collective-permute-start.3
  40.2 3.2 %collective-permute-start.2 = (bf16[512,128]{1,0:T(8,128)(2,1)S(1)}, bf16[512,128]{1,0:T(8,128)(2,1)S(1)}, u32[]{:S(2)}, u32[]{:S(2)}) collective-permute-start(bf16[512,128]{1,0:T(8,128)(2,1)S(1)} %collective-permute-done.refs_1_), channel_id=1, source_target_pairs={{0,32},{16,48},{32,64},{48,80},{64,96},{80,112},{96,128},{112,144}... | collective-permute-start | bytes 393224 | tf_op jit(solution)/shard_map/ppermute | solution.py:337
  43.4 3.3 %collective-permute-done.3.refs_4_ = bf16[512,128]{1,0:T(8,128)(2,1)S(1)} collective-permute-done((bf16[512,128]{1,0:T(8,128)(2,1)S(1)}, bf16[512,128]{1,0:T(8,128)(2,1)S(1)}, u32[]{:S(2)}, u32[]{:S(2)}) %collective-permute-start.3) | collective-permute-done | bytes 131104 | tf_op jit(solution)/shard_map/ppermute | solution.py:337
  46.7 0.0 collective-permute-start.5
  46.7 0.0 copy-done.6
  46.7 0.1 collective-permute-start.7
  46.8 0.0 copy-done.8
  46.8 0.5 collective-permute-start.8
  47.3 0.0 collective-permute-done.2.refs_3_
  47.3 3.1 %collective-permute-start.4 = (bf16[512,128]{1,0:T(8,128)(2,1)S(1)}, bf16[512,128]{1,0:T(8,128)(2,1)S(1)}, u32[]{:S(2)}, u32[]{:S(2)}) collective-permute-start(bf16[512,128]{1,0:T(8,128)(2,1)S(1)} %collective-permute-done.2.refs_3_), channel_id=1, source_target_pairs={{0,32},{16,48},{32,64},{48,80},{64,96},{80,112},{96,128},{112,144}... | collective-permute-start | bytes 393224 | tf_op jit(solution)/shard_map/ppermute | solution.py:337
  50.5 0.0 copy-done.7
  50.5 0.0 collective-permute-start.9
  50.5 2.4 %collective-permute-done.5.refs_6_ = bf16[512,128]{1,0:T(8,128)(2,1)S(1)} collective-permute-done((bf16[512,128]{1,0:T(8,128)(2,1)S(1)}, bf16[512,128]{1,0:T(8,128)(2,1)S(1)}, u32[]{:S(2)}, u32[]{:S(2)}) %collective-permute-start.5) | collective-permute-done | bytes 131104 | tf_op jit(solution)/shard_map/ppermute | solution.py:337
  52.9 0.0 collective-permute-start.13
  52.9 0.0 collective-permute-done.7.refs_8_
  52.9 0.0 copy-start.12
  52.9 0.5 collective-permute-start.10
  53.4 0.0 collective-permute-done.8.refs_9_
  53.4 0.1 collective-permute-start.11
  53.5 0.0 collective-permute-done.4.refs_5_
  53.5 0.4 collective-permute-start.12
  53.9 0.0 collective-permute-done.9.refs_10_
  53.9 3.3 %collective-permute-start.6 = (bf16[512,128]{1,0:T(8,128)(2,1)S(1)}, bf16[512,128]{1,0:T(8,128)(2,1)S(1)}, u32[]{:S(2)}, u32[]{:S(2)}) collective-permute-start(bf16[512,128]{1,0:T(8,128)(2,1)S(1)} %collective-permute-done.4.refs_5_), channel_id=1, source_target_pairs={{0,32},{16,48},{32,64},{48,80},{64,96},{80,112},{96,128},{112,144}... | collective-permute-start | bytes 393224 | tf_op jit(solution)/shard_map/ppermute | solution.py:337
  57.3 0.0 collective-permute-done.13.refs_14_
  57.3 0.0 collective-permute-start.14
  57.3 0.0 collective-permute-done.10.refs_11_
  57.3 0.0 copy-start.17
  57.3 0.0 collective-permute-done.11.refs_12_
  57.3 0.0 copy-start.18
  57.3 0.0 collective-permute-done.12.refs_13_
  57.3 0.0 copy-start.19
  57.3 3.3 %collective-permute-done.6.refs_7_ = bf16[512,128]{1,0:T(8,128)(2,1)S(1)} collective-permute-done((bf16[512,128]{1,0:T(8,128)(2,1)S(1)}, bf16[512,128]{1,0:T(8,128)(2,1)S(1)}, u32[]{:S(2)}, u32[]{:S(2)}) %collective-permute-start.6) | collective-permute-done | bytes 131104 | tf_op jit(solution)/shard_map/ppermute | solution.py:337
  60.6 0.0 copy-done.16
  60.6 0.0 copy-done.19
  60.6 3.5 %collective-permute-done.14.refs_15_ = bf16[512,128]{1,0:T(8,128)(2,1)} collective-permute-done((bf16[512,128]{1,0:T(8,128)(2,1)S(1)}, bf16[512,128]{1,0:T(8,128)(2,1)}, u32[]{:S(2)}, u32[]{:S(2)}) %collective-permute-start.14) | collective-permute-done | bytes 131104 | tf_op jit(solution)/shard_map/ppermute | solution.py:337
  64.1 9.2 %all-to-all-done.2.left_hbm = bf16[16,16,32,128]{3,2,1,0:T(8,128)(2,1)S(1)} async-done(((bf16[16,16,32,128]{3,2,1,0:T(8,128)(2,1)}), bf16[16,16,32,128]{3,2,1,0:T(8,128)(2,1)S(1)}, u32[]{:S(2)}, u32[]{:S(2)}) %all-to-all-start.2) | async-done | bytes 2097184 | tf_op jit(solution)/shard_map/all_to_all | solution.py:354
  73.3 0.0 copy-done.12
  73.3 0.0 copy-done.13
  73.3 0.0 copy-done.15
  73.4 1.3 copy-done.5
  74.6 0.0 copy-done.9
  74.7 0.0 copy-done.11
  74.7 0.0 copy-start
  74.7 0.0 copy-start.2
  74.7 0.0 copy-start.3
  74.7 0.0 copy-start.4
  74.7 6.6 %shard_map.96 = s16[16,112,256]{2,1,0:T(8,128)(2,1)} custom-call(s32[16,4,16]{2,1,0:T(4,128)} %bitcast.9, s32[16,4,16]{2,1,0:T(4,128)} %bitcast.12, bf16[16,16,32,128]{3,2,1,0:T(8,128)(2,1)} %copy-done.5, bf16[512,128]{1,0:T(8,128)(2,1)} %bitcast.17, bf16[512,128]{1,0:T(8,128)(2,1)} %copy-done.8, bf16[512,128]{1,0:T(8,128)(2,1)} %copy-done.7, ...), custom_call_target="tpu_custom_call" | custom-call | tf_op jit(solution)/shard_map/pallas_call | solution.py:363
  81.3 0.0 copy-start.1
  81.3 19.1 %all_to_all.25.in_ref = s16[16,112,256]{2,1,0:T(8,128)(2,1)S(1)} all-to-all(s16[16,112,256]{2,1,0:T(8,128)(2,1)} %shard_map.96), channel_id=1, replica_groups=mesh['dp'=16,'mp'=16] {'mp'}, dimensions={0} | all-to-all | bytes 1835008 | tf_op jit(solution)/shard_map/all_to_all | solution.py:376
  100.4 29.7 %shard_map.97 = (f32[6,2,256,256]{3,2,1,0:T(8,128)}, bf16[6,2,256,256]{3,2,1,0:T(8,128)(2,1)}, s16[16,272,256]{2,1,0:T(8,128)(2,1)S(1)}) custom-call(s32[16,4,16]{2,1,0:T(4,128)S(1)} %bitcast.11, s32[16,4,16]{2,1,0:T(4,128)S(1)} %bitcast.13, s32[16,16]{1,0:T(8,128)S(1)} %copy-done.4, s16[16,112,256]{2,1,0:T(8,128)(2,1)S(1)} %all_to_all.25.in_ref, ...), custom_call_target="tpu_custom_call" | custom-call | tf_op jit(solution)/shard_map/pallas_call | solution.py:379
  130.1 30.6 %all_to_all.26.in_hbm = s16[16,272,256]{2,1,0:T(8,128)(2,1)} all-to-all(s16[16,272,256]{2,1,0:T(8,128)(2,1)S(1)} %get-tuple-element.12), channel_id=1, replica_groups=mesh['dp'=16,'mp'=16] {'mp'}, dimensions={0} | all-to-all | bytes 4456448 | tf_op jit(solution)/shard_map/all_to_all | solution.py:403
  160.7 3.3 %shard_map.98 = f32[512,512]{1,0:T(8,128)} custom-call(s32[16,4,16]{2,1,0:T(4,128)} %bitcast.10, s16[16,272,256]{2,1,0:T(8,128)(2,1)} %all_to_all.26.in_hbm), custom_call_target="tpu_custom_call" | custom-call | tf_op jit(solution)/shard_map/pallas_call | solution.py:406
  (22 shorter events, 0.0 us)
Async XLA Ops:
  2.4 15.0 %all-to-all-start.1 = ((bf16[16,32,128]{2,1,0:T(8,128)(2,1)}), bf16[16,32,128]{2,1,0:T(8,128)(2,1)S(1)}, u32[]{:S(2)}, u32[]{:S(2)}) async-start(bf16[16,32,128]{2,1,0:T(8,128)(2,1)} %shard_map.95), calls=%async_computation.1 | async-start | bytes 262144 | tf_op jit(solution)/shard_map/all_to_all | solution.py:348
  17.4 29.3 %copy-start.6 = (bf16[16,32,128]{2,1,0:T(8,128)(2,1)}, bf16[16,32,128]{2,1,0:T(8,128)(2,1)S(1)}, u32[]{:S(2)}) copy-start(bf16[16,32,128]{2,1,0:T(8,128)(2,1)S(1)} %all-to-all-done.1) | copy-start | bytes 393220
  17.4 14.1 %all-to-all-start = ((bf16[16,32,128]{2,1,0:T(8,128)(2,1)}), bf16[16,32,128]{2,1,0:T(8,128)(2,1)S(1)}, u32[]{:S(2)}, u32[]{:S(2)}) async-start(bf16[16,32,128]{2,1,0:T(8,128)(2,1)} %shard_map.94), calls=%async_computation | async-start | bytes 262144 | tf_op jit(solution)/shard_map/all_to_all | solution.py:351
  25.1 9.5 %collective-permute-start.1 = (bf16[512,128]{1,0:T(8,128)(2,1)S(1)}, bf16[512,128]{1,0:T(8,128)(2,1)S(1)}, u32[]{:S(2)}, u32[]{:S(2)}) collective-permute-start(bf16[512,128]{1,0:T(8,128)(2,1)S(1)} %bitcast.14), channel_id=1, source_target_pairs={{0,224},{16,240},{32,0},{48,16},{64,32},{80,48},{96,64},{112,80},{... | collective-permute-start | bytes 393224 | tf_op jit(solution)/shard_map/ppermute | solution.py:337
  25.7 8.9 %collective-permute-start = (bf16[512,128]{1,0:T(8,128)(2,1)S(1)}, bf16[512,128]{1,0:T(8,128)(2,1)S(1)}, u32[]{:S(2)}, u32[]{:S(2)}) collective-permute-start(bf16[512,128]{1,0:T(8,128)(2,1)S(1)} %bitcast.15), channel_id=1, source_target_pairs={{0,32},{16,48},{32,64},{48,80},{64,96},{80,112},{96,128},{112,144}... | collective-permute-start | bytes 393224 | tf_op jit(solution)/shard_map/ppermute | solution.py:337
  34.6 15.8 %copy-start.7 = (bf16[512,128]{1,0:T(8,128)(2,1)}, bf16[512,128]{1,0:T(8,128)(2,1)S(1)}, u32[]{:S(2)}) copy-start(bf16[512,128]{1,0:T(8,128)(2,1)S(1)} %collective-permute-done.1.refs_2_) | copy-start | bytes 393220
  34.6 12.2 %copy-start.8 = (bf16[512,128]{1,0:T(8,128)(2,1)}, bf16[512,128]{1,0:T(8,128)(2,1)S(1)}, u32[]{:S(2)}) copy-start(bf16[512,128]{1,0:T(8,128)(2,1)S(1)} %collective-permute-done.refs_1_) | copy-start | bytes 393220
  36.3 37.0 %all-to-all-start.2 = ((bf16[16,16,32,128]{3,2,1,0:T(8,128)(2,1)}), bf16[16,16,32,128]{3,2,1,0:T(8,128)(2,1)S(1)}, u32[]{:S(2)}, u32[]{:S(2)}) async-start(bf16[16,16,32,128]{3,2,1,0:T(8,128)(2,1)} %broadcast_in_dim.12), calls=%async_computation.2 | async-start | bytes 4194304 | tf_op jit(solution)/shard_map/all_to_all | solution.py:354
  40.1 6.6 %collective-permute-start.3 = (bf16[512,128]{1,0:T(8,128)(2,1)S(1)}, bf16[512,128]{1,0:T(8,128)(2,1)S(1)}, u32[]{:S(2)}, u32[]{:S(2)}) collective-permute-start(bf16[512,128]{1,0:T(8,128)(2,1)S(1)} %collective-permute-done.1.refs_2_), channel_id=1, source_target_pairs={{0,224},{16,240},{32,0},{48,16},{64,32},{80,48},{96,64},{112,80},{... | collective-permute-start | bytes 393224 | tf_op jit(solution)/shard_map/ppermute | solution.py:337
  40.2 7.1 %collective-permute-start.2 = (bf16[512,128]{1,0:T(8,128)(2,1)S(1)}, bf16[512,128]{1,0:T(8,128)(2,1)S(1)}, u32[]{:S(2)}, u32[]{:S(2)}) collective-permute-start(bf16[512,128]{1,0:T(8,128)(2,1)S(1)} %collective-permute-done.refs_1_), channel_id=1, source_target_pairs={{0,32},{16,48},{32,64},{48,80},{64,96},{80,112},{96,128},{112,144}... | collective-permute-start | bytes 393224 | tf_op jit(solution)/shard_map/ppermute | solution.py:337
  46.7 28.0 %copy-start.9 = (bf16[512,128]{1,0:T(8,128)(2,1)}, bf16[512,128]{1,0:T(8,128)(2,1)S(1)}, u32[]{:S(2)}) copy-start(bf16[512,128]{1,0:T(8,128)(2,1)S(1)} %collective-permute-done.3.refs_4_) | copy-start | bytes 393220
  46.7 6.2 %collective-permute-start.5 = (bf16[512,128]{1,0:T(8,128)(2,1)S(1)}, bf16[512,128]{1,0:T(8,128)(2,1)S(1)}, u32[]{:S(2)}, u32[]{:S(2)}) collective-permute-start(bf16[512,128]{1,0:T(8,128)(2,1)S(1)} %collective-permute-done.3.refs_4_), channel_id=1, source_target_pairs={{0,224},{16,240},{32,0},{48,16},{64,32},{80,48},{96,64},{112,80},{... | collective-permute-start | bytes 393224 | tf_op jit(solution)/shard_map/ppermute | solution.py:337
  46.7 6.2 %collective-permute-start.7 = (bf16[512,128]{1,0:T(8,128)(2,1)S(1)}, bf16[512,128]{1,0:T(8,128)(2,1)S(1)}, u32[]{:S(2)}, u32[]{:S(2)}) collective-permute-start(bf16[512,128]{1,0:T(8,128)(2,1)S(1)} %bitcast.16), channel_id=1, source_target_pairs={{0,16},{16,0},{32,48},{48,32},{64,80},{80,64},{96,112},{112,96},{1... | collective-permute-start | bytes 393224 | tf_op jit(solution)/shard_map/ppermute | solution.py:340
  46.8 6.6 %collective-permute-start.8 = (bf16[512,128]{1,0:T(8,128)(2,1)S(1)}, bf16[512,128]{1,0:T(8,128)(2,1)S(1)}, u32[]{:S(2)}, u32[]{:S(2)}) collective-permute-start(bf16[512,128]{1,0:T(8,128)(2,1)S(1)} %collective-permute-done.refs_1_), channel_id=1, source_target_pairs={{0,16},{16,0},{32,48},{48,32},{64,80},{80,64},{96,112},{112,96},{1... | collective-permute-start | bytes 393224 | tf_op jit(solution)/shard_map/ppermute | solution.py:340
  47.3 27.3 %copy-start.10 = (bf16[512,128]{1,0:T(8,128)(2,1)}, bf16[512,128]{1,0:T(8,128)(2,1)S(1)}, u32[]{:S(2)}) copy-start(bf16[512,128]{1,0:T(8,128)(2,1)S(1)} %collective-permute-done.2.refs_3_) | copy-start | bytes 393220
  47.3 6.2 %collective-permute-start.4 = (bf16[512,128]{1,0:T(8,128)(2,1)S(1)}, bf16[512,128]{1,0:T(8,128)(2,1)S(1)}, u32[]{:S(2)}, u32[]{:S(2)}) collective-permute-start(bf16[512,128]{1,0:T(8,128)(2,1)S(1)} %collective-permute-done.2.refs_3_), channel_id=1, source_target_pairs={{0,32},{16,48},{32,64},{48,80},{64,96},{80,112},{96,128},{112,144}... | collective-permute-start | bytes 393224 | tf_op jit(solution)/shard_map/ppermute | solution.py:337
  50.5 3.5 %collective-permute-start.9 = (bf16[512,128]{1,0:T(8,128)(2,1)S(1)}, bf16[512,128]{1,0:T(8,128)(2,1)S(1)}, u32[]{:S(2)}, u32[]{:S(2)}) collective-permute-start(bf16[512,128]{1,0:T(8,128)(2,1)S(1)} %collective-permute-done.1.refs_2_), channel_id=1, source_target_pairs={{0,16},{16,0},{32,48},{48,32},{64,80},{80,64},{96,112},{112,96},{1... | collective-permute-start | bytes 393224 | tf_op jit(solution)/shard_map/ppermute | solution.py:340
  52.9 21.8 %copy-start.11 = (bf16[512,128]{1,0:T(8,128)(2,1)}, bf16[512,128]{1,0:T(8,128)(2,1)S(1)}, u32[]{:S(2)}) copy-start(bf16[512,128]{1,0:T(8,128)(2,1)S(1)} %collective-permute-done.5.refs_6_) | copy-start | bytes 393220
  52.9 4.4 %collective-permute-start.13 = (bf16[512,128]{1,0:T(8,128)(2,1)S(1)}, bf16[512,128]{1,0:T(8,128)(2,1)S(1)}, u32[]{:S(2)}, u32[]{:S(2)}) collective-permute-start(bf16[512,128]{1,0:T(8,128)(2,1)S(1)} %collective-permute-done.5.refs_6_), channel_id=1, source_target_pairs={{0,16},{16,0},{32,48},{48,32},{64,80},{80,64},{96,112},{112,96},{1... | collective-permute-start | bytes 393224 | tf_op jit(solution)/shard_map/ppermute | solution.py:340
  52.9 20.5 %copy-start.12 = (bf16[512,128]{1,0:T(8,128)(2,1)}, bf16[512,128]{1,0:T(8,128)(2,1)S(1)}, u32[]{:S(2)}) copy-start(bf16[512,128]{1,0:T(8,128)(2,1)S(1)} %collective-permute-done.7.refs_8_) | copy-start | bytes 393220
  52.9 4.4 %collective-permute-start.10 = (bf16[512,128]{1,0:T(8,128)(2,1)S(1)}, bf16[512,128]{1,0:T(8,128)(2,1)S(1)}, u32[]{:S(2)}, u32[]{:S(2)}) collective-permute-start(bf16[512,128]{1,0:T(8,128)(2,1)S(1)} %collective-permute-done.2.refs_3_), channel_id=1, source_target_pairs={{0,16},{16,0},{32,48},{48,32},{64,80},{80,64},{96,112},{112,96},{1... | collective-permute-start | bytes 393224 | tf_op jit(solution)/shard_map/ppermute | solution.py:340
  53.4 19.9 %copy-start.13 = (bf16[512,128]{1,0:T(8,128)(2,1)}, bf16[512,128]{1,0:T(8,128)(2,1)S(1)}, u32[]{:S(2)}) copy-start(bf16[512,128]{1,0:T(8,128)(2,1)S(1)} %collective-permute-done.8.refs_9_) | copy-start | bytes 393220
  53.4 3.9 %collective-permute-start.11 = (bf16[512,128]{1,0:T(8,128)(2,1)S(1)}, bf16[512,128]{1,0:T(8,128)(2,1)S(1)}, u32[]{:S(2)}, u32[]{:S(2)}) collective-permute-start(bf16[512,128]{1,0:T(8,128)(2,1)S(1)} %collective-permute-done.3.refs_4_), channel_id=1, source_target_pairs={{0,16},{16,0},{32,48},{48,32},{64,80},{80,64},{96,112},{112,96},{1... | collective-permute-start | bytes 393224 | tf_op jit(solution)/shard_map/ppermute | solution.py:340
  53.5 19.8 %copy-start.14 = (bf16[512,128]{1,0:T(8,128)(2,1)}, bf16[512,128]{1,0:T(8,128)(2,1)S(1)}, u32[]{:S(2)}) copy-start(bf16[512,128]{1,0:T(8,128)(2,1)S(1)} %collective-permute-done.4.refs_5_) | copy-start | bytes 393220
  53.5 3.8 %collective-permute-start.12 = (bf16[512,128]{1,0:T(8,128)(2,1)S(1)}, bf16[512,128]{1,0:T(8,128)(2,1)S(1)}, u32[]{:S(2)}, u32[]{:S(2)}) collective-permute-start(bf16[512,128]{1,0:T(8,128)(2,1)S(1)} %collective-permute-done.4.refs_5_), channel_id=1, source_target_pairs={{0,16},{16,0},{32,48},{48,32},{64,80},{80,64},{96,112},{112,96},{1... | collective-permute-start | bytes 393224 | tf_op jit(solution)/shard_map/ppermute | solution.py:340
  53.9 19.4 %copy-start.15 = (bf16[512,128]{1,0:T(8,128)(2,1)}, bf16[512,128]{1,0:T(8,128)(2,1)S(1)}, u32[]{:S(2)}) copy-start(bf16[512,128]{1,0:T(8,128)(2,1)S(1)} %collective-permute-done.9.refs_10_) | copy-start | bytes 393220
  53.9 6.7 %collective-permute-start.6 = (bf16[512,128]{1,0:T(8,128)(2,1)S(1)}, bf16[512,128]{1,0:T(8,128)(2,1)S(1)}, u32[]{:S(2)}, u32[]{:S(2)}) collective-permute-start(bf16[512,128]{1,0:T(8,128)(2,1)S(1)} %collective-permute-done.4.refs_5_), channel_id=1, source_target_pairs={{0,32},{16,48},{32,64},{48,80},{64,96},{80,112},{96,128},{112,144}... | collective-permute-start | bytes 393224 | tf_op jit(solution)/shard_map/ppermute | solution.py:337
  57.3 3.4 %copy-start.16 = (bf16[512,128]{1,0:T(8,128)(2,1)}, bf16[512,128]{1,0:T(8,128)(2,1)S(1)}, u32[]{:S(2)}) copy-start(bf16[512,128]{1,0:T(8,128)(2,1)S(1)} %collective-permute-done.13.refs_14_) | copy-start | bytes 393220
  57.3 6.9 %collective-permute-start.14 = (bf16[512,128]{1,0:T(8,128)(2,1)S(1)}, bf16[512,128]{1,0:T(8,128)(2,1)}, u32[]{:S(2)}, u32[]{:S(2)}) collective-permute-start(bf16[512,128]{1,0:T(8,128)(2,1)S(1)} %collective-permute-done.13.refs_14_), channel_id=1, source_target_pairs={{0,224},{16,240},{32,0},{48,16},{64,32},{80,48},{96,64},{112,80},{... | collective-permute-start | bytes 393224 | tf_op jit(solution)/shard_map/ppermute | solution.py:337
  57.3 17.4 %copy-start.17 = (bf16[512,128]{1,0:T(8,128)(2,1)}, bf16[512,128]{1,0:T(8,128)(2,1)S(1)}, u32[]{:S(2)}) copy-start(bf16[512,128]{1,0:T(8,128)(2,1)S(1)} %collective-permute-done.10.refs_11_) | copy-start | bytes 393220
  57.3 17.4 %copy-start.18 = (bf16[512,128]{1,0:T(8,128)(2,1)}, bf16[512,128]{1,0:T(8,128)(2,1)S(1)}, u32[]{:S(2)}) copy-start(bf16[512,128]{1,0:T(8,128)(2,1)S(1)} %collective-permute-done.11.refs_12_) | copy-start | bytes 393220
  57.3 3.3 %copy-start.19 = (bf16[512,128]{1,0:T(8,128)(2,1)}, bf16[512,128]{1,0:T(8,128)(2,1)S(1)}, u32[]{:S(2)}) copy-start(bf16[512,128]{1,0:T(8,128)(2,1)S(1)} %collective-permute-done.12.refs_13_) | copy-start | bytes 393220
  60.6 14.1 %copy-start.20 = (bf16[512,128]{1,0:T(8,128)(2,1)}, bf16[512,128]{1,0:T(8,128)(2,1)S(1)}, u32[]{:S(2)}) copy-start(bf16[512,128]{1,0:T(8,128)(2,1)S(1)} %collective-permute-done.6.refs_7_) | copy-start | bytes 393220
  73.3 1.3 copy-start.5
  74.7 25.7 %copy-start = (f32[1,6,2,256,256]{4,3,2,1,0:T(8,128)S(1)}, f32[1,6,2,256,256]{4,3,2,1,0:T(8,128)}, u32[]{:S(2)}) copy-start(f32[1,6,2,256,256]{4,3,2,1,0:T(8,128)} %param.9) | copy-start | bytes 9437188
  74.7 25.7 %copy-start.2 = (s32[16,16,4]{1,2,0:T(4,128)S(1)}, s32[16,16,4]{1,2,0:T(4,128)}, u32[]{:S(2)}) copy-start(s32[16,16,4]{1,2,0:T(4,128)} %param.11) | copy-start | bytes 12292
  74.7 25.7 %copy-start.3 = (s32[16,16,4]{1,2,0:T(4,128)S(1)}, s32[16,16,4]{1,2,0:T(4,128)}, u32[]{:S(2)}) copy-start(s32[16,16,4]{1,2,0:T(4,128)} %param.12) | copy-start | bytes 12292
  74.7 25.7 %copy-start.4 = (s32[16,16]{1,0:T(8,128)S(1)}, s32[16,16]{1,0:T(8,128)}, u32[]{:S(2)}) copy-start(s32[16,16]{1,0:T(8,128)} %fresh_ref.1) | copy-start | bytes 3076
  81.3 19.1 %copy-start.1 = (bf16[1,6,2,256,256]{4,3,2,1,0:T(8,128)(2,1)S(1)}, bf16[1,6,2,256,256]{4,3,2,1,0:T(8,128)(2,1)}, u32[]{:S(2)}) copy-start(bf16[1,6,2,256,256]{4,3,2,1,0:T(8,128)(2,1)} %param.10) | copy-start | bytes 4718596

commit v3 on v2

v3 whole, which is shorter than its diff:
```python
import functools
import math

import jax
import jax.numpy as jnp
from jax import lax
from jax.experimental import pallas as pl
from jax.experimental.pallas import tpu as pltpu
from jax.sharding import PartitionSpec as P

ITERS = 10
REFRESH_MOST = 2
EPSILON = 0.1
PAD = 16
TOP_BITS = 14
MIDDLE = 1.125
F32 = jnp.float32
BF16 = jnp.bfloat16
VMEM = pltpu.VMEM
SMEM = pltpu.SMEM


def matmul(left, right, dims=((1,), (0,))):
    return lax.dot_general(left, right, (dims, ((), ())), preferred_element_type=F32)


def split(x):
    high = x.astype(BF16)
    return high, (x - high.astype(F32)).astype(BF16)


def product(left, right):
    lh, ll = left
    rh, rl = right
    return matmul(
        jnp.concatenate([lh, lh, ll], axis=1), jnp.concatenate([rh, rl, rh], axis=0)
    )


def quantized(values, shift):
    scaled = jnp.clip(jnp.round(values * jnp.exp2(shift)), -32767.0, 32767.0)
    return scaled.astype(jnp.int32).astype(jnp.int16)


def code(block, out_ref, place):
    edge = block.shape[0]
    most = jnp.maximum(jnp.max(jnp.abs(block), axis=(0, 1), keepdims=True), 1e-30)
    shift = TOP_BITS - jnp.floor(jnp.log2(most))
    out_ref[place, :edge, :] = quantized(block, shift)
    out_ref[place, edge:, :] = jnp.broadcast_to(
        shift.astype(jnp.int32), (PAD, block.shape[1])
    ).astype(jnp.int16)


def decode(in_ref, place, edge):
    whole = in_ref[place, :edge, :].astype(jnp.int32).astype(F32)
    shift = in_ref[place, edge:, :].astype(jnp.int32).astype(F32)[:1, :]
    return whole, jnp.exp2(-shift)


def position(ways):
    mp_index = lax.axis_index("mp")
    return mp_index // ways, lax.rem(mp_index, ways)


def pick_kernel(edge, acts_ref, out_ref):
    parts, rows, tokens = out_ref.shape
    half = rows // 2
    width = acts_ref.shape[1] // parts
    lanes = 128
    row = lax.broadcasted_iota(jnp.int32, (half, lanes), 0)
    col = lax.broadcasted_iota(jnp.int32, (half, lanes), 1)
    for side in range(2):
        first = position(edge // half)[side] * half
        group = first // lanes
        inside = lax.rem(first, lanes)
        chosen = (col == row + inside).astype(F32).astype(BF16)
        for part in range(parts):
            start = pl.multiple_of(part * width + side * edge + group * lanes, lanes)
            piece = acts_ref[:, pl.ds(start, lanes)]
            out_ref[part, side * half : (side + 1) * half, :] = matmul(
                chosen, piece, ((1,), (1,))
            ).astype(BF16)


def strip_kernel(edge, cot_ref, out_ref):
    owners, rows, lanes = out_ref.shape
    blocks = cot_ref.shape[1] // edge
    depth = rows // blocks
    row = lax.broadcasted_iota(jnp.int32, (lanes, lanes), 0)
    col = lax.broadcasted_iota(jnp.int32, (lanes, lanes), 1)
    identity = (row == col).astype(F32).astype(BF16)
    for chunk in range(cot_ref.shape[1] // lanes):
        piece = cot_ref[:, chunk * lanes : (chunk + 1) * lanes]
        turned = matmul(identity, piece, ((1,), (1,))).astype(BF16)
        block, first = divmod(chunk * lanes, edge)
        for k in range(lanes // depth):
            out_ref[first // depth + k, block * depth : (block + 1) * depth, :] = turned[
                k * depth : (k + 1) * depth
            ]


def gradient_kernel(edge, slots, owner_ref, place_ref, own_hbm, *refs):
    out_ref, left, rights, shifts, sems = refs[-5:]
    chips = rights.shape[0]
    rights_hbm, lefts_hbm = refs[-5 - chips : -5], refs[: -5 - chips]
    times, rows, tokens = own_hbm.shape
    half = rows // 2
    ways = edge // half
    sources = ways * ways
    depth = edge // sources
    dp_index = lax.axis_index("dp")
    copies = [(rights_hbm[k], rights.at[k]) for k in range(chips)]
    for side, place in enumerate(position(ways)):
        for away in range(ways):
            part = lax.rem(place + (ways - away), ways)
            top = pl.multiple_of(side * edge + part * half, half)
            if away == 0:
                source = own_hbm.at[:, side * half : (side + 1) * half, :]
            else:
                source = lefts_hbm[side * (ways - 1) + away - 1]
            copies.append((source, left.at[:, pl.ds(top, half), :]))
    copies = [
        pltpu.make_async_copy(source, target, sems.at[i])
        for i, (source, target) in enumerate(copies)
    ]
    for copy in copies:
        copy.start()
    shifts[...] = jnp.zeros_like(shifts)
    total = left.shape[1]
    when = token_groups(dp_index, chips)
    for copy in copies:
        copy.wait()
    left = jnp.concatenate([left[t] for t in when], axis=1)
    slab = rights.shape[2]
    col_blocks = slab // (sources * depth)
    for chunk in range(slab // edge):
        strips = jnp.concatenate(
            [rights[k // 2, k % 2, chunk * edge : (chunk + 1) * edge, :] for k in range(times)],
            axis=1,
        )
        product_t = matmul(strips, left, ((1,), (1,))).reshape(edge // depth, depth, total)
        for row_block in range(total // edge):
            values = product_t[:, :, row_block * edge : (row_block + 1) * edge]
            most = jnp.max(jnp.abs(values), axis=(1, 2), keepdims=True)
            shift = TOP_BITS - jnp.floor(jnp.log2(jnp.maximum(most, 1e-30)))
            coded = quantized(values, shift)
            for k in range(edge // depth):
                m, col_block = divmod(chunk * (edge // depth) + k, col_blocks)
                j = row_block * col_blocks + col_block
                owner, place = owner_ref[dp_index, j, m], place_ref[dp_index, j, m]
                top = pl.multiple_of(place * depth, depth)
                out_ref[owner, pl.ds(top, depth), :] = coded[k]
                shifts[owner, pl.ds(place, 1), :] = jnp.broadcast_to(shift[k], (1, edge))
    out_ref[:, slots * depth :, :] = shifts[...].astype(jnp.int32).astype(jnp.int16)


def token_groups(dp_index, chips):
    chip, core = dp_index // 2, lax.rem(dp_index, 2)
    away = 1 - 2 * core
    groups = [2 * chip + core, 2 * chip + 1 - core]
    for step in range(1, chips // 2 + 1):
        for side in (-1, 1)[: 2 if step < chips // 2 else 1]:
            first = core if side < 0 else 1 - core
            base = 2 * lax.rem(chip + side * step * away + chips, chips)
            groups += [base + first, base + 1 - first]
    return groups


def owner_kernel(
    owner_ref,
    place_ref,
    fresh_ref,
    in_ref,
    factors_hbm,
    roots_hbm,
    factors_out,
    roots_out,
    out_ref,
    state,
    roots,
    units,
    halves,
    results,
    moving,
    current,
    table,
    picked,
    state_in,
    state_done,
    roots_sems,
):
    slots, _, edge, _ = state.shape
    local_blocks, sources = owner_ref.shape[1:]
    dp_index, mp_index = lax.axis_index("dp"), lax.axis_index("mp")
    load_roots = pltpu.make_async_copy(roots_hbm, roots, roots_sems.at[0])
    load_roots.start()
    loads = [
        pltpu.make_async_copy(factors_hbm.at[s], state.at[s], state_in.at[s]) for s in range(slots)
    ]
    saves = [
        pltpu.make_async_copy(state.at[s], factors_out.at[s], state_done.at[s])
        for s in range(slots)
    ]
    for load in loads:
        load.start()

    for s in range(slots + 1):
        table[s] = -1
    for s in range(REFRESH_MOST + 1):
        picked[s] = -1

    def place_source(m, carry):
        for j in range(local_blocks):
            held = owner_ref[dp_index, j, m] == mp_index
            table[jnp.where(held, place_ref[dp_index, j, m], slots)] = m
        return carry

    lax.fori_loop(0, sources, place_source, 0)

    def place_fresh(i, count):
        block = fresh_ref[dp_index, i]
        m, j = block // local_blocks, lax.rem(block, local_blocks)
        held = owner_ref[dp_index, j, m] == mp_index
        picked[jnp.where(held, count, REFRESH_MOST)] = place_ref[dp_index, j, m]
        return count + held.astype(jnp.int32)

    lax.fori_loop(0, fresh_ref.shape[1], place_fresh, jnp.int32(0))

    depth = edge // sources
    units[...] = jnp.exp2(-in_ref[:, slots * depth :, :].astype(jnp.int32).astype(F32))
    for load in loads:
        load.wait()
    for s in range(slots):
        whole = in_ref[:, s * depth : (s + 1) * depth, :].astype(jnp.int32).astype(F32)
        block = jnp.where(table[s] >= 0, whole * units[:, s : s + 1, :], 0.0)
        high, low = split(block.reshape(edge, edge))
        halves[s, 0] = high
        halves[s, 1] = low
        left = jnp.concatenate([high, high, low], axis=0)
        right = jnp.concatenate([high, low, high], axis=0)
        state[s, 0] = state[s, 0] + matmul(left, right, ((0,), (0,)))
        left = jnp.concatenate([high, high, low], axis=1)
        right = jnp.concatenate([high, low, high], axis=1)
        state[s, 1] = state[s, 1] + matmul(left, right, ((1,), (1,)))
    for save in saves:
        save.start()

    row = lax.broadcasted_iota(jnp.int32, (edge, edge), 0)
    col = lax.broadcasted_iota(jnp.int32, (edge, edge), 1)
    identity = (row == col).astype(F32)
    count = REFRESH_MOST * 2

    def less_middle(old):
        small = [(1.25 - MIDDLE) * identity - 0.25 * x for x in old]
        for middle in (MIDDLE, MIDDLE**2):
            high = [x.astype(BF16) for x in small]
            small = [2.0 * middle * x + matmul(h, h) for x, h in zip(small, high)]
        return small

    starts = []
    for b in range(count):
        slot = jnp.maximum(picked[b // 2], 0)
        shifted = state[slot, b % 2] + EPSILON * identity
        norm = jnp.sqrt(jnp.sum(shifted * shifted, axis=(0, 1), keepdims=True))
        scaled = shifted / norm
        current[b] = (5.0 * identity - scaled) * 0.25 / jnp.sqrt(jnp.sqrt(norm))
        starts.append(scaled)
    fourth = less_middle(starts)
    for b in range(count):
        moving[b] = MIDDLE**4 * starts[b] + product(split(fourth[b]), split(starts[b]))

    def step(iteration, carry):
        old = [moving[b] for b in range(count)]
        halves = [split(x) for x in old]
        small = [(1.25 - MIDDLE) * identity - 0.25 * x for x in old]
        high = [x.astype(BF16) for x in small]
        small = [2.0 * MIDDLE * x + matmul(h, h) for x, h in zip(small, high)]
        for b in range(count):
            x = current[b]
            current[b] = 1.25 * x - 0.25 * product(split(x), halves[b])
        high = [x.astype(BF16) for x in small]
        fourth = [2.0 * MIDDLE**2 * x + matmul(h, h) for x, h in zip(small, high)]
        for b in range(count):
            moving[b] = MIDDLE**4 * old[b] + product(split(fourth[b]), halves[b])
        return carry

    lax.fori_loop(1, ITERS - 1, step, 0, unroll=2)
    load_roots.wait()
    for b in range(count):
        x = current[b]
        final = (1.25 * x - 0.25 * product(split(x), split(moving[b]))).astype(BF16)

        @pl.when(picked[b // 2] >= 0)
        def _():
            roots[picked[b // 2], b % 2] = final

    save_roots = pltpu.make_async_copy(roots, roots_out, roots_sems.at[1])
    save_roots.start()

    for s in range(slots):
        high, low = halves[s, 0], halves[s, 1]
        left = roots[s, 0]
        right = roots[s, 1]
        first = matmul(
            jnp.concatenate([high, low], axis=0),
            jnp.concatenate([right, right], axis=0),
            ((0,), (0,)),
        )
        fh, fl = split(first)
        precond = matmul(
            jnp.concatenate([left, left], axis=1), jnp.concatenate([fh, fl], axis=0)
        )
        block = high.astype(F32) + low.astype(F32)
        block_sum = jnp.sum(block * block, axis=(0, 1), keepdims=True)
        precond_sum = jnp.sum(precond * precond, axis=(0, 1), keepdims=True)
        ratio = jnp.sqrt(block_sum / (precond_sum + 1e-06))
        code(precond * ratio, results, s)
    for s in range(slots):

        @pl.when(table[s] >= 0)
        def _():
            out_ref[table[s]] = results[s]

    save_roots.wait()
    for save in saves:
        save.wait()


def home_kernel(edge, owner_ref, in_hbm, out_hbm, blocks, values, sems):
    dp_index, mp_index = lax.axis_index("dp"), lax.axis_index("mp")
    col_blocks = out_hbm.shape[1] // edge
    loads, saves = [], []
    for j in range(blocks.shape[0]):
        owner = owner_ref[dp_index, j, mp_index]
        top, left = (j // col_blocks) * edge, (j % col_blocks) * edge
        loads.append(pltpu.make_async_copy(in_hbm.at[owner], blocks.at[j], sems.at[0, j]))
        saves.append(
            pltpu.make_async_copy(
                values.at[j], out_hbm.at[top : top + edge, left : left + edge], sems.at[1, j]
            )
        )
    for load in loads:
        load.start()
    for j, load in enumerate(loads):
        load.wait()
        whole, unit = decode(blocks, j, edge)
        values[j] = whole * unit
        saves[j].start()
    for save in saves:
        save.wait()


def body(acts, cotangent, factors, roots, owner_of, slot_of, refresh_ids):
    dp_count = lax.axis_size("dp")
    mp_count = lax.axis_size("mp")
    edge = factors.shape[-1]
    slots = factors.shape[1]
    tokens = acts.shape[0]
    row_count = acts.shape[1] // dp_count
    slab = cotangent.shape[1]
    ways = math.isqrt(mp_count)
    rows = 2 * edge // ways
    half = rows // 2
    owner_of = owner_of.transpose(0, 2, 1)
    slot_of = slot_of.transpose(0, 2, 1)

    smem = pl.BlockSpec(memory_space=SMEM)
    vmem = pl.BlockSpec(memory_space=VMEM)
    hbm = pl.BlockSpec(memory_space=pl.ANY)

    around = [(i, (i + (2, -2)[i % 2]) % dp_count) for i in range(dp_count)]
    swap = [(i, i ^ 1) for i in range(dp_count)]

    def along_y(x, k):
        return lax.ppermute(x, "mp", [(i, (i + ways * k) % mp_count) for i in range(mp_count)])

    def along_x(x, k):
        return lax.ppermute(
            x, "mp", [(i, (i // ways) * ways + (i + k) % ways) for i in range(mp_count)]
        )

    def swapped(x):
        return lax.ppermute(x, "dp", swap)

    def ring(x):
        return lax.ppermute(x, "dp", around)

    picked = pl.pallas_call(
        functools.partial(pick_kernel, edge),
        out_shape=jax.ShapeDtypeStruct((dp_count, rows, tokens), BF16),
        in_specs=[vmem],
        out_specs=vmem,
    )(acts)

    strips = pl.pallas_call(
        functools.partial(strip_kernel, edge),
        out_shape=jax.ShapeDtypeStruct((mp_count, slab // mp_count, tokens), BF16),
        in_specs=[vmem],
        out_specs=vmem,
    )(cotangent)
    strips = lax.all_to_all(strips, "mp", split_axis=0, concat_axis=0, tiled=True)
    strips = strips.reshape(slab, tokens)
    both = jnp.stack([strips, swapped(strips)])
    first = ring(both)
    second = ring(first)
    own = lax.all_to_all(picked, "dp", split_axis=0, concat_axis=0, tiled=True)
    own, both, first, second = lax.optimization_barrier((own, both, first, second))
    by_y, by_x = own[:, :half], own[:, half:]
    near = [along_y(by_y, 1), along_y(by_y, ways - 1), along_x(by_x, 1), along_x(by_x, ways - 1)]
    third = ring(second)
    near, third, by_y, by_x = lax.optimization_barrier((near, third, by_y, by_x))
    far = [along_y(by_y, ways // 2), along_x(by_x, ways // 2)]
    others = [near[0], far[0], near[1], near[2], far[1], near[3]]
    gathered = [both]
    for part in (first, second, third):
        gathered += [part, swapped(part)]
    gathered.append(ring(third))

    depth = edge // mp_count
    outgoing = pl.pallas_call(
        functools.partial(gradient_kernel, edge, slots),
        out_shape=jax.ShapeDtypeStruct((mp_count, slots * depth + PAD, edge), jnp.int16),
        in_specs=[smem, smem, hbm] + [hbm] * len(others + gathered),
        out_specs=vmem,
        scratch_shapes=[
            VMEM((dp_count, row_count, tokens), BF16),
            VMEM((dp_count // 2, 2, slab, tokens), BF16),
            VMEM((mp_count, PAD, edge), F32),
            pltpu.SemaphoreType.DMA((2 + len(others + gathered),)),
        ],
        compiler_params=pltpu.CompilerParams(vmem_limit_bytes=60 * 1024 * 1024),
    )(owner_of, slot_of, own, *others, *gathered)
    incoming = lax.all_to_all(outgoing, "mp", split_axis=0, concat_axis=0, tiled=True)

    count = REFRESH_MOST * 2
    factors_next, roots_next, homeward = pl.pallas_call(
        owner_kernel,
        out_shape=(
            jax.ShapeDtypeStruct(factors.shape[1:], F32),
            jax.ShapeDtypeStruct(roots.shape[1:], BF16),
            jax.ShapeDtypeStruct((mp_count, edge + PAD, edge), jnp.int16),
        ),
        in_specs=[smem, smem, smem, vmem, hbm, hbm],
        out_specs=(hbm, hbm, vmem),
        scratch_shapes=[
            VMEM(factors.shape[1:], F32),
            VMEM(roots.shape[1:], BF16),
            VMEM((mp_count, PAD, edge), F32),
            VMEM((slots, 2, edge, edge), BF16),
            VMEM((slots, edge + PAD, edge), jnp.int16),
            VMEM((count, edge, edge), F32),
            VMEM((count, edge, edge), F32),
            SMEM((slots + 1,), jnp.int32),
            SMEM((REFRESH_MOST + 1,), jnp.int32),
            pltpu.SemaphoreType.DMA((slots,)),
            pltpu.SemaphoreType.DMA((slots,)),
            pltpu.SemaphoreType.DMA((2,)),
        ],
        compiler_params=pltpu.CompilerParams(vmem_limit_bytes=28 * 1024 * 1024),
    )(owner_of, slot_of, refresh_ids, incoming, factors[0], roots[0])
    returned = lax.all_to_all(homeward, "mp", split_axis=0, concat_axis=0, tiled=True)

    local_blocks = owner_of.shape[1]
    direction = pl.pallas_call(
        functools.partial(home_kernel, edge),
        out_shape=jax.ShapeDtypeStruct((row_count, slab), F32),
        in_specs=[smem, hbm],
        out_specs=hbm,
        scratch_shapes=[
            VMEM((local_blocks, edge + PAD, edge), jnp.int16),
            VMEM((local_blocks, edge, edge), F32),
            pltpu.SemaphoreType.DMA((2, local_blocks)),
        ],
    )(owner_of, returned)
    return (direction, factors_next[None], roots_next[None])


def solution(mesh):
    in_specs = (
        P("dp", None),
        P("dp", "mp"),
        P("dp", "mp", None, None, None),
        P("dp", "mp", None, None, None),
        P(),
        P(),
        P(),
    )
    out_specs = (P("dp", "mp"), P("dp", "mp", None, None, None), P("dp", "mp", None, None, None))
    return jax.shard_map(body, mesh=mesh, in_specs=in_specs, out_specs=out_specs, check_vma=False)
```

time: 165 us -> 152 us (0.921)
  Pallas kernels: 44 us -> 34.2 us
  local copies, waits for them, and re-layouts: 3.11 us -> 0.87 us
    pallas_call x1, Pallas kernels: 29.7 us -> 19.4 us  [body(): pl.pallas_call(owner_kernel, out_shape=(jax.ShapeDtypeStruct(factors.shap...]
    ppermute x8 -> x10, waiting for transfers between devices: 15.6 us -> 25.8 us  [the longest x4 15.6 us: ring(): return lax.ppermute(x, 'dp', around)]
    all_to_all x1 -> x0, waiting for transfers between devices: 9.19 us -> none  [body(): left = lax.all_to_all(spread, 'mp', split_axis=0, concat_axis=0, tiled=True)]
    ppermute x8 -> x10, starting transfers between devices: 13 us -> 17.2 us  [the longest x4 11.3 us: ring(): return lax.ppermute(x, 'dp', around)]
    all_to_all x1 -> x0, starting transfers between devices: 3.72 us -> none  [body(): left = lax.all_to_all(spread, 'mp', split_axis=0, concat_axis=0, tiled=True)]
    all_to_all x1, waiting for transfers between devices: 3.13 us -> 0.01 us  [body(): own = lax.all_to_all(picked, 'dp', split_axis=0, concat_axis=0, tiled=True)]
    broadcast_in_dim x1 -> x0, local copies, waits for them, and re-layouts: 1.73 us -> none  [body(): spread = jnp.broadcast_to(own[None], (mp_count, dp_count, rows, tokens))]
  transfers between devices with their start and end apart: 18 -> 16, of which waited for: 8 -> 9; matrix products, arithmetic and copies ran while one was open for 0% -> 0% of each run, Pallas kernels for 2% -> 2%
where the time goes in v3:
time: 152 us; the launch traced here: 150 us
  blocking collectives  50.1 us (33%)
  Pallas kernels  34.2 us (23%)
  starting transfers between devices  32.4 us (21%)
  waiting for transfers between devices  31.8 us (21%)
    all_to_all x1, blocking collectives, body(): lax.all_to_all(homeward, 'mp', split_axis=0, concat_axis=0, tiled=True)  29.8 us
    all_to_all x1, blocking collectives, body(): lax.all_to_all(outgoing, 'mp', split_axis=0, concat_axis=0, tiled=True)  20.2 us
    pallas_call x1, Pallas kernels, body(): pl.pallas_call(owner_kernel, out_shape=(jax.ShapeDtypeStruct(factors.shap...  19.4 us
    ppermute x4, waiting for transfers between devices, ring(): return lax.ppermute(x, 'dp', around)  15.6 us
    ppermute x4, starting transfers between devices, ring(): return lax.ppermute(x, 'dp', around)  11.3 us
    all_to_all x1, starting transfers between devices, body(): own = lax.all_to_all(picked, 'dp', split_axis=0, concat_axis=0, tiled=True)  7.68 us
    all_to_all x1, starting transfers between devices, body(): lax.all_to_all(strips, 'mp', split_axis=0, concat_axis=0, tiled=True)  7.03 us
    pallas_call x1, Pallas kernels, body(): pl.pallas_call(functools.partial(gradient_kernel, edge, slots), out_shape...  6.56 us
  transfers between devices with their start and end apart: 16, of which 9 were waited for; matrix products, arithmetic and copies ran while one was open for 0% of the time, Pallas kernels for 2%

profile of v3, /device:TPU:96, one launch (start us, length us, event | category | flops | bytes accessed | tf_op | source)
XLA Modules:
  0.0 150.3 jit_solution(9247481807566244294)
XLA Ops:
  0.6 1.8 %shard_map.95 = bf16[16,32,128]{2,1,0:T(8,128)(2,1)} custom-call(bf16[128,512]{1,0:T(8,128)(2,1)} %cot_ref.1), custom_call_target="tpu_custom_call" | custom-call | tf_op jit(solution)/shard_map/pallas_call | solution.py:396
  2.4 7.0 %all-to-all-start.1 = ((bf16[16,32,128]{2,1,0:T(8,128)(2,1)}), bf16[16,32,128]{2,1,0:T(8,128)(2,1)S(1)}, u32[]{:S(2)}, u32[]{:S(2)}) async-start(bf16[16,32,128]{2,1,0:T(8,128)(2,1)} %shard_map.95), calls=%async_computation.1 | async-start | bytes 262144 | tf_op jit(solution)/shard_map/all_to_all | solution.py:402
  9.4 3.2 %shard_map.94 = bf16[16,128,128]{2,1,0:T(8,128)(2,1)} custom-call(bf16[128,8192]{1,0:T(8,128)(2,1)} %acts_ref.1), custom_call_target="tpu_custom_call" | custom-call | tf_op jit(solution)/shard_map/pallas_call | solution.py:389
  12.7 4.8 %all-to-all-done.1 = bf16[16,32,128]{2,1,0:T(8,128)(2,1)S(1)} async-done(((bf16[16,32,128]{2,1,0:T(8,128)(2,1)}), bf16[16,32,128]{2,1,0:T(8,128)(2,1)S(1)}, u32[]{:S(2)}, u32[]{:S(2)}) %all-to-all-start.1) | async-done | bytes 131104 | tf_op jit(solution)/shard_map/all_to_all | solution.py:402
  17.4 7.7 %all-to-all-start = ((bf16[16,128,128]{2,1,0:T(8,128)(2,1)}), bf16[16,128,128]{2,1,0:T(8,128)(2,1)S(1)}, u32[]{:S(2)}, u32[]{:S(2)}) async-start(bf16[16,128,128]{2,1,0:T(8,128)(2,1)} %shard_map.94), calls=%async_computation | async-start | bytes 1048576 | tf_op jit(solution)/shard_map/all_to_all | solution.py:407
  25.1 0.1 collective-permute-start
  25.3 1.2 collective-permute-done
  26.5 0.0 copy-start.6
  26.5 2.8 %collective-permute-start.1 = (bf16[2,512,128]{2,1,0:T(8,128)(2,1)S(1)}, bf16[2,512,128]{2,1,0:T(8,128)(2,1)S(1)}, u32[]{:S(2)}, u32[]{:S(2)}) collective-permute-start(bf16[2,512,128]{2,1,0:T(8,128)(2,1)S(1)} %pad_maximum_fusion.refs_6_), channel_id=1, source_target_pairs={{0,32},{16,240},{32,64},{48,16},{64,96},{80,48},{96,128},{112,80},... | collective-permute-start | bytes 786440 | tf_op jit(solution)/shard_map/ppermute | solution.py:387
  29.3 11.7 %collective-permute-done.1.refs_7_ = bf16[2,512,128]{2,1,0:T(8,128)(2,1)S(1)} collective-permute-done((bf16[2,512,128]{2,1,0:T(8,128)(2,1)S(1)}, bf16[2,512,128]{2,1,0:T(8,128)(2,1)S(1)}, u32[]{:S(2)}, u32[]{:S(2)}) %collective-permute-start.1) | collective-permute-done | bytes 262176 | tf_op jit(solution)/shard_map/ppermute | solution.py:387
  40.9 2.7 %collective-permute-start.2 = (bf16[2,512,128]{2,1,0:T(8,128)(2,1)S(1)}, bf16[2,512,128]{2,1,0:T(8,128)(2,1)S(1)}, u32[]{:S(2)}, u32[]{:S(2)}) collective-permute-start(bf16[2,512,128]{2,1,0:T(8,128)(2,1)S(1)} %collective-permute-done.1.refs_7_), channel_id=1, source_target_pairs={{0,32},{16,240},{32,64},{48,16},{64,96},{80,48},{96,128},{112,80},... | collective-permute-start | bytes 786440 | tf_op jit(solution)/shard_map/ppermute | solution.py:387
  43.6 3.9 %collective-permute-done.2.refs_9_ = bf16[2,512,128]{2,1,0:T(8,128)(2,1)S(1)} collective-permute-done((bf16[2,512,128]{2,1,0:T(8,128)(2,1)S(1)}, bf16[2,512,128]{2,1,0:T(8,128)(2,1)S(1)}, u32[]{:S(2)}, u32[]{:S(2)}) %collective-permute-start.2) | collective-permute-done | bytes 262176 | tf_op jit(solution)/shard_map/ppermute | solution.py:387
  47.5 0.0 all-to-all-done.own_hbm
  47.5 3.8 %collective-permute-start.7 = (bf16[2,512,128]{2,1,0:T(8,128)(2,1)S(1)}, bf16[2,512,128]{2,1,0:T(8,128)(2,1)S(1)}, u32[]{:S(2)}, u32[]{:S(2)}) collective-permute-start(bf16[2,512,128]{2,1,0:T(8,128)(2,1)S(1)} %collective-permute-done.2.refs_9_), channel_id=1, source_target_pairs={{0,32},{16,240},{32,64},{48,16},{64,96},{80,48},{96,128},{112,80},... | collective-permute-start | bytes 786440 | tf_op jit(solution)/shard_map/ppermute | solution.py:387
  51.3 1.0 collective-permute-start.6
  52.3 1.1 collective-permute-start.5
  53.4 0.9 collective-permute-start.4
  54.3 1.2 collective-permute-start.3
  55.4 0.0 collective-permute-done.7.refs_11_
  55.4 0.4 collective-permute-start.10
  55.8 1.9 %collective-permute-done.6.refs_5_ = bf16[16,64,128]{2,1,0:T(8,128)(2,1)S(1)} collective-permute-done((bf16[16,64,128]{2,1,0:T(8,128)(2,1)S(1)}, bf16[16,64,128]{2,1,0:T(8,128)(2,1)S(1)}, u32[]{:S(2)}, u32[]{:S(2)}) %collective-permute-start.6) | collective-permute-done | bytes 262176 | tf_op jit(solution)/shard_map/ppermute | solution.py:379
  57.7 0.0 collective-permute-start.11
  57.8 2.1 %collective-permute-done.5.refs_3_ = bf16[16,64,128]{2,1,0:T(8,128)(2,1)S(1)} collective-permute-done((bf16[16,64,128]{2,1,0:T(8,128)(2,1)S(1)}, bf16[16,64,128]{2,1,0:T(8,128)(2,1)S(1)}, u32[]{:S(2)}, u32[]{:S(2)}) %collective-permute-start.5) | collective-permute-done | bytes 262176 | tf_op jit(solution)/shard_map/ppermute | solution.py:379
  59.9 0.0 collective-permute-done.4.refs_2_
  59.9 1.9 %collective-permute-done.3.refs_0_ = bf16[16,64,128]{2,1,0:T(8,128)(2,1)S(1)} collective-permute-done((bf16[16,64,128]{2,1,0:T(8,128)(2,1)S(1)}, bf16[16,64,128]{2,1,0:T(8,128)(2,1)S(1)}, u32[]{:S(2)}, u32[]{:S(2)}) %collective-permute-start.3) | collective-permute-done | bytes 262176 | tf_op jit(solution)/shard_map/ppermute | solution.py:376
  61.8 0.3 collective-permute-start.8
  62.1 1.5 %collective-permute-start.9 = (bf16[16,64,128]{2,1,0:T(8,128)(2,1)S(1)}, bf16[16,64,128]{2,1,0:T(8,128)(2,1)S(1)}, u32[]{:S(2)}, u32[]{:S(2)}) collective-permute-start(bf16[16,64,128]{2,1,0:T(8,128)(2,1)S(1)} %get-tuple-element.23), channel_id=1, source_target_pairs={{0,2},{1,3},{2,0},{3,1},{4,6},{5,7},{6,4},{7,5},{8,10},{9,11},{10,... | collective-permute-start | bytes 786440 | tf_op jit(solution)/shard_map/ppermute | solution.py:379
  63.6 2.1 %collective-permute-start.13 = (bf16[2,512,128]{2,1,0:T(8,128)(2,1)S(1)}, bf16[2,512,128]{2,1,0:T(8,128)(2,1)S(1)}, u32[]{:S(2)}, u32[]{:S(2)}) collective-permute-start(bf16[2,512,128]{2,1,0:T(8,128)(2,1)S(1)} %collective-permute-done.7.refs_11_), channel_id=1, source_target_pairs={{0,32},{16,240},{32,64},{48,16},{64,96},{80,48},{96,128},{112,80},... | collective-permute-start | bytes 786440 | tf_op jit(solution)/shard_map/ppermute | solution.py:387
  65.7 0.0 collective-permute-done.10.refs_8_
  65.7 0.0 collective-permute-start.12
  65.7 0.0 collective-permute-done.11.refs_10_
  65.7 0.0 copy-start.15
  65.7 4.0 %collective-permute-done.8.refs_1_ = bf16[16,64,128]{2,1,0:T(8,128)(2,1)S(1)} collective-permute-done((bf16[16,64,128]{2,1,0:T(8,128)(2,1)S(1)}, bf16[16,64,128]{2,1,0:T(8,128)(2,1)S(1)}, u32[]{:S(2)}, u32[]{:S(2)}) %collective-permute-start.8) | collective-permute-done | bytes 262176 | tf_op jit(solution)/shard_map/ppermute | solution.py:376
  69.7 0.2 collective-permute-done.9.refs_4_
  70.0 0.0 collective-permute-done.13.refs_13_
  70.0 0.0 collective-permute-done.12.refs_12_
  70.0 0.0 copy-done.7
  70.0 0.0 copy-done.8
  70.0 0.0 copy-done.9
  70.0 0.0 copy-done.10
  70.0 0.0 copy-done.11
  70.0 0.0 copy-done.12
  70.1 0.0 copy-done.13
  70.1 0.0 copy-done.14
  70.1 0.0 copy-done.15
  70.1 0.3 copy-done.16
  70.4 0.2 copy-done.17
  70.7 0.1 copy-done.18
  70.8 0.1 copy-done.19
  70.8 0.0 copy-done.6
  70.9 0.0 copy-done.5
  70.9 0.0 copy-start.3
  70.9 0.0 copy-start.4
  70.9 6.6 %shard_map.96 = s16[16,112,256]{2,1,0:T(8,128)(2,1)} custom-call(s32[16,4,16]{2,1,0:T(4,128)} %bitcast.11, s32[16,4,16]{2,1,0:T(4,128)} %bitcast.14, bf16[16,128,128]{2,1,0:T(8,128)(2,1)} %copy-done.5, bf16[16,64,128]{2,1,0:T(8,128)(2,1)} %copy-done.13, bf16[16,64,128]{2,1,0:T(8,128)(2,1)} %copy-done.16, bf16[16,64,128]{2,1,0:T(8,128)(2,1)} %copy-done.12, ...), custom_call_target="tpu_custom_call" | custom-call | tf_op jit(solution)/shard_map/pallas_call | solution.py:421
  77.5 0.0 copy-start.1
  77.5 20.2 %all_to_all.20.in_ref = s16[16,112,256]{2,1,0:T(8,128)(2,1)S(1)} all-to-all(s16[16,112,256]{2,1,0:T(8,128)(2,1)} %shard_map.96), channel_id=1, replica_groups=mesh['dp'=16,'mp'=16] {'mp'}, dimensions={0} | all-to-all | bytes 1835008 | tf_op jit(solution)/shard_map/all_to_all | solution.py:434
  97.7 0.0 copy-done
  97.7 0.0 copy-done.2
  97.7 0.0 copy-done.3
  97.7 0.0 copy-done.4
  97.7 0.0 copy-done.1
  97.7 19.4 %shard_map.97 = (f32[6,2,256,256]{3,2,1,0:T(8,128)}, bf16[6,2,256,256]{3,2,1,0:T(8,128)(2,1)}, s16[16,272,256]{2,1,0:T(8,128)(2,1)S(1)}) custom-call(s32[16,4,16]{2,1,0:T(4,128)S(1)} %bitcast.13, s32[16,4,16]{2,1,0:T(4,128)S(1)} %bitcast.15, s32[16,16]{1,0:T(8,128)S(1)} %copy-done.4, s16[16,112,256]{2,1,0:T(8,128)(2,1)S(1)} %all_to_all.20.in_ref, ...), custom_call_target="tpu_custom_call" | custom-call | tf_op jit(solution)/shard_map/pallas_call | solution.py:437
  117.2 29.8 %all_to_all.21.in_hbm = s16[16,272,256]{2,1,0:T(8,128)(2,1)} all-to-all(s16[16,272,256]{2,1,0:T(8,128)(2,1)S(1)} %get-tuple-element.28), channel_id=1, replica_groups=mesh['dp'=16,'mp'=16] {'mp'}, dimensions={0} | all-to-all | bytes 4456448 | tf_op jit(solution)/shard_map/all_to_all | solution.py:462
  147.0 3.2 %shard_map.98 = f32[512,512]{1,0:T(8,128)} custom-call(s32[16,4,16]{2,1,0:T(4,128)} %bitcast.12, s16[16,272,256]{2,1,0:T(8,128)(2,1)} %all_to_all.21.in_hbm), custom_call_target="tpu_custom_call" | custom-call | tf_op jit(solution)/shard_map/pallas_call | solution.py:465
  (17 shorter events, 0.1 us)
Async XLA Ops:
  2.4 15.0 %all-to-all-start.1 = ((bf16[16,32,128]{2,1,0:T(8,128)(2,1)}), bf16[16,32,128]{2,1,0:T(8,128)(2,1)S(1)}, u32[]{:S(2)}, u32[]{:S(2)}) async-start(bf16[16,32,128]{2,1,0:T(8,128)(2,1)} %shard_map.95), calls=%async_computation.1 | async-start | bytes 262144 | tf_op jit(solution)/shard_map/all_to_all | solution.py:402
  17.4 30.1 %all-to-all-start = ((bf16[16,128,128]{2,1,0:T(8,128)(2,1)}), bf16[16,128,128]{2,1,0:T(8,128)(2,1)S(1)}, u32[]{:S(2)}, u32[]{:S(2)}) async-start(bf16[16,128,128]{2,1,0:T(8,128)(2,1)} %shard_map.94), calls=%async_computation | async-start | bytes 1048576 | tf_op jit(solution)/shard_map/all_to_all | solution.py:407
  25.1 1.3 collective-permute-start
  26.5 44.4 %copy-start.6 = (bf16[2,512,128]{2,1,0:T(8,128)(2,1)}, bf16[2,512,128]{2,1,0:T(8,128)(2,1)S(1)}, u32[]{:S(2)}) copy-start(bf16[2,512,128]{2,1,0:T(8,128)(2,1)S(1)} %pad_maximum_fusion.refs_6_) | copy-start | bytes 786436
  26.5 14.4 %collective-permute-start.1 = (bf16[2,512,128]{2,1,0:T(8,128)(2,1)S(1)}, bf16[2,512,128]{2,1,0:T(8,128)(2,1)S(1)}, u32[]{:S(2)}, u32[]{:S(2)}) collective-permute-start(bf16[2,512,128]{2,1,0:T(8,128)(2,1)S(1)} %pad_maximum_fusion.refs_6_), channel_id=1, source_target_pairs={{0,32},{16,240},{32,64},{48,16},{64,96},{80,48},{96,128},{112,80},... | collective-permute-start | bytes 786440 | tf_op jit(solution)/shard_map/ppermute | solution.py:387
  40.9 29.1 %copy-start.7 = (bf16[2,512,128]{2,1,0:T(8,128)(2,1)}, bf16[2,512,128]{2,1,0:T(8,128)(2,1)S(1)}, u32[]{:S(2)}) copy-start(bf16[2,512,128]{2,1,0:T(8,128)(2,1)S(1)} %collective-permute-done.1.refs_7_) | copy-start | bytes 786436
  40.9 6.6 %collective-permute-start.2 = (bf16[2,512,128]{2,1,0:T(8,128)(2,1)S(1)}, bf16[2,512,128]{2,1,0:T(8,128)(2,1)S(1)}, u32[]{:S(2)}, u32[]{:S(2)}) collective-permute-start(bf16[2,512,128]{2,1,0:T(8,128)(2,1)S(1)} %collective-permute-done.1.refs_7_), channel_id=1, source_target_pairs={{0,32},{16,240},{32,64},{48,16},{64,96},{80,48},{96,128},{112,80},... | collective-permute-start | bytes 786440 | tf_op jit(solution)/shard_map/ppermute | solution.py:387
  47.5 22.5 %copy-start.8 = (bf16[2,512,128]{2,1,0:T(8,128)(2,1)}, bf16[2,512,128]{2,1,0:T(8,128)(2,1)S(1)}, u32[]{:S(2)}) copy-start(bf16[2,512,128]{2,1,0:T(8,128)(2,1)S(1)} %collective-permute-done.2.refs_9_) | copy-start | bytes 786436
  47.5 23.4 %copy-start.5 = (bf16[16,128,128]{2,1,0:T(8,128)(2,1)}, bf16[16,128,128]{2,1,0:T(8,128)(2,1)S(1)}, u32[]{:S(2)}) copy-start(bf16[16,128,128]{2,1,0:T(8,128)(2,1)S(1)} %all-to-all-done.own_hbm) | copy-start | bytes 1572868
  47.5 7.9 %collective-permute-start.7 = (bf16[2,512,128]{2,1,0:T(8,128)(2,1)S(1)}, bf16[2,512,128]{2,1,0:T(8,128)(2,1)S(1)}, u32[]{:S(2)}, u32[]{:S(2)}) collective-permute-start(bf16[2,512,128]{2,1,0:T(8,128)(2,1)S(1)} %collective-permute-done.2.refs_9_), channel_id=1, source_target_pairs={{0,32},{16,240},{32,64},{48,16},{64,96},{80,48},{96,128},{112,80},... | collective-permute-start | bytes 786440 | tf_op jit(solution)/shard_map/ppermute | solution.py:387
  51.3 6.4 %collective-permute-start.6 = (bf16[16,64,128]{2,1,0:T(8,128)(2,1)S(1)}, bf16[16,64,128]{2,1,0:T(8,128)(2,1)S(1)}, u32[]{:S(2)}, u32[]{:S(2)}) collective-permute-start(bf16[16,64,128]{2,1,0:T(8,128)(2,1)S(1)} %get-tuple-element.23), channel_id=1, source_target_pairs={{0,3},{1,0},{2,1},{3,2},{4,7},{5,4},{6,5},{7,6},{8,11},{9,8},{10,9... | collective-permute-start | bytes 786440 | tf_op jit(solution)/shard_map/ppermute | solution.py:379
  52.3 7.6 %collective-permute-start.5 = (bf16[16,64,128]{2,1,0:T(8,128)(2,1)S(1)}, bf16[16,64,128]{2,1,0:T(8,128)(2,1)S(1)}, u32[]{:S(2)}, u32[]{:S(2)}) collective-permute-start(bf16[16,64,128]{2,1,0:T(8,128)(2,1)S(1)} %get-tuple-element.23), channel_id=1, source_target_pairs={{0,1},{1,2},{2,3},{3,0},{4,5},{5,6},{6,7},{7,4},{8,9},{9,10},{10,1... | collective-permute-start | bytes 786440 | tf_op jit(solution)/shard_map/ppermute | solution.py:379
  53.4 6.5 %collective-permute-start.4 = (bf16[16,64,128]{2,1,0:T(8,128)(2,1)S(1)}, bf16[16,64,128]{2,1,0:T(8,128)(2,1)S(1)}, u32[]{:S(2)}, u32[]{:S(2)}) collective-permute-start(bf16[16,64,128]{2,1,0:T(8,128)(2,1)S(1)} %get-tuple-element.20), channel_id=1, source_target_pairs={{0,12},{1,13},{2,14},{3,15},{4,0},{5,1},{6,2},{7,3},{8,4},{9,5},{1... | collective-permute-start | bytes 786440 | tf_op jit(solution)/shard_map/ppermute | solution.py:376
  54.3 7.6 %collective-permute-start.3 = (bf16[16,64,128]{2,1,0:T(8,128)(2,1)S(1)}, bf16[16,64,128]{2,1,0:T(8,128)(2,1)S(1)}, u32[]{:S(2)}, u32[]{:S(2)}) collective-permute-start(bf16[16,64,128]{2,1,0:T(8,128)(2,1)S(1)} %get-tuple-element.20), channel_id=1, source_target_pairs={{0,4},{1,5},{2,6},{3,7},{4,8},{5,9},{6,10},{7,11},{8,12},{9,13},{1... | collective-permute-start | bytes 786440 | tf_op jit(solution)/shard_map/ppermute | solution.py:376
  55.4 14.6 %copy-start.9 = (bf16[2,512,128]{2,1,0:T(8,128)(2,1)}, bf16[2,512,128]{2,1,0:T(8,128)(2,1)S(1)}, u32[]{:S(2)}) copy-start(bf16[2,512,128]{2,1,0:T(8,128)(2,1)S(1)} %collective-permute-done.7.refs_11_) | copy-start | bytes 786436
  55.4 10.2 %collective-permute-start.10 = (bf16[2,512,128]{2,1,0:T(8,128)(2,1)S(1)}, bf16[2,512,128]{2,1,0:T(8,128)(2,1)S(1)}, u32[]{:S(2)}, u32[]{:S(2)}) collective-permute-start(bf16[2,512,128]{2,1,0:T(8,128)(2,1)S(1)} %collective-permute-done.1.refs_7_), channel_id=1, source_target_pairs={{0,16},{16,0},{32,48},{48,32},{64,80},{80,64},{96,112},{112,96},{1... | collective-permute-start | bytes 786440 | tf_op jit(solution)/shard_map/ppermute | solution.py:384
  57.7 12.3 %copy-start.10 = (bf16[16,64,128]{2,1,0:T(8,128)(2,1)}, bf16[16,64,128]{2,1,0:T(8,128)(2,1)S(1)}, u32[]{:S(2)}) copy-start(bf16[16,64,128]{2,1,0:T(8,128)(2,1)S(1)} %collective-permute-done.6.refs_5_) | copy-start | bytes 786436
  57.7 7.9 %collective-permute-start.11 = (bf16[2,512,128]{2,1,0:T(8,128)(2,1)S(1)}, bf16[2,512,128]{2,1,0:T(8,128)(2,1)S(1)}, u32[]{:S(2)}, u32[]{:S(2)}) collective-permute-start(bf16[2,512,128]{2,1,0:T(8,128)(2,1)S(1)} %collective-permute-done.2.refs_9_), channel_id=1, source_target_pairs={{0,16},{16,0},{32,48},{48,32},{64,80},{80,64},{96,112},{112,96},{1... | collective-permute-start | bytes 786440 | tf_op jit(solution)/shard_map/ppermute | solution.py:384
  59.9 10.1 %copy-start.11 = (bf16[16,64,128]{2,1,0:T(8,128)(2,1)}, bf16[16,64,128]{2,1,0:T(8,128)(2,1)S(1)}, u32[]{:S(2)}) copy-start(bf16[16,64,128]{2,1,0:T(8,128)(2,1)S(1)} %collective-permute-done.5.refs_3_) | copy-start | bytes 786436
  59.9 10.1 %copy-start.12 = (bf16[16,64,128]{2,1,0:T(8,128)(2,1)}, bf16[16,64,128]{2,1,0:T(8,128)(2,1)S(1)}, u32[]{:S(2)}) copy-start(bf16[16,64,128]{2,1,0:T(8,128)(2,1)S(1)} %collective-permute-done.4.refs_2_) | copy-start | bytes 786436
  61.8 8.2 %copy-start.13 = (bf16[16,64,128]{2,1,0:T(8,128)(2,1)}, bf16[16,64,128]{2,1,0:T(8,128)(2,1)S(1)}, u32[]{:S(2)}) copy-start(bf16[16,64,128]{2,1,0:T(8,128)(2,1)S(1)} %collective-permute-done.3.refs_0_) | copy-start | bytes 786436
  61.8 7.9 %collective-permute-start.8 = (bf16[16,64,128]{2,1,0:T(8,128)(2,1)S(1)}, bf16[16,64,128]{2,1,0:T(8,128)(2,1)S(1)}, u32[]{:S(2)}, u32[]{:S(2)}) collective-permute-start(bf16[16,64,128]{2,1,0:T(8,128)(2,1)S(1)} %get-tuple-element.20), channel_id=1, source_target_pairs={{0,8},{1,9},{2,10},{3,11},{4,12},{5,13},{6,14},{7,15},{8,0},{9,1},... | collective-permute-start | bytes 786440 | tf_op jit(solution)/shard_map/ppermute | solution.py:376
  62.1 7.9 %collective-permute-start.9 = (bf16[16,64,128]{2,1,0:T(8,128)(2,1)S(1)}, bf16[16,64,128]{2,1,0:T(8,128)(2,1)S(1)}, u32[]{:S(2)}, u32[]{:S(2)}) collective-permute-start(bf16[16,64,128]{2,1,0:T(8,128)(2,1)S(1)} %get-tuple-element.23), channel_id=1, source_target_pairs={{0,2},{1,3},{2,0},{3,1},{4,6},{5,7},{6,4},{7,5},{8,10},{9,11},{10,... | collective-permute-start | bytes 786440 | tf_op jit(solution)/shard_map/ppermute | solution.py:379
  63.6 6.4 %collective-permute-start.13 = (bf16[2,512,128]{2,1,0:T(8,128)(2,1)S(1)}, bf16[2,512,128]{2,1,0:T(8,128)(2,1)S(1)}, u32[]{:S(2)}, u32[]{:S(2)}) collective-permute-start(bf16[2,512,128]{2,1,0:T(8,128)(2,1)S(1)} %collective-permute-done.7.refs_11_), channel_id=1, source_target_pairs={{0,32},{16,240},{32,64},{48,16},{64,96},{80,48},{96,128},{112,80},... | collective-permute-start | bytes 786440 | tf_op jit(solution)/shard_map/ppermute | solution.py:387
  65.7 4.4 %copy-start.14 = (bf16[2,512,128]{2,1,0:T(8,128)(2,1)}, bf16[2,512,128]{2,1,0:T(8,128)(2,1)S(1)}, u32[]{:S(2)}) copy-start(bf16[2,512,128]{2,1,0:T(8,128)(2,1)S(1)} %collective-permute-done.10.refs_8_) | copy-start | bytes 786436
  65.7 4.3 %collective-permute-start.12 = (bf16[2,512,128]{2,1,0:T(8,128)(2,1)S(1)}, bf16[2,512,128]{2,1,0:T(8,128)(2,1)S(1)}, u32[]{:S(2)}, u32[]{:S(2)}) collective-permute-start(bf16[2,512,128]{2,1,0:T(8,128)(2,1)S(1)} %collective-permute-done.7.refs_11_), channel_id=1, source_target_pairs={{0,16},{16,0},{32,48},{48,32},{64,80},{80,64},{96,112},{112,96},{1... | collective-permute-start | bytes 786440 | tf_op jit(solution)/shard_map/ppermute | solution.py:384
  65.7 4.4 %copy-start.15 = (bf16[2,512,128]{2,1,0:T(8,128)(2,1)}, bf16[2,512,128]{2,1,0:T(8,128)(2,1)S(1)}, u32[]{:S(2)}) copy-start(bf16[2,512,128]{2,1,0:T(8,128)(2,1)S(1)} %collective-permute-done.11.refs_10_) | copy-start | bytes 786436
  69.7 0.7 copy-start.16
  70.0 0.7 copy-start.17
  70.0 0.8 copy-start.18
  70.0 0.9 copy-start.19
  70.9 26.8 %copy-start = (f32[1,6,2,256,256]{4,3,2,1,0:T(8,128)S(1)}, f32[1,6,2,256,256]{4,3,2,1,0:T(8,128)}, u32[]{:S(2)}) copy-start(f32[1,6,2,256,256]{4,3,2,1,0:T(8,128)} %param.9) | copy-start | bytes 9437188
  70.9 26.9 %copy-start.2 = (s32[16,16,4]{1,2,0:T(4,128)S(1)}, s32[16,16,4]{1,2,0:T(4,128)}, u32[]{:S(2)}) copy-start(s32[16,16,4]{1,2,0:T(4,128)} %param.11) | copy-start | bytes 12292
  70.9 26.8 %copy-start.3 = (s32[16,16,4]{1,2,0:T(4,128)S(1)}, s32[16,16,4]{1,2,0:T(4,128)}, u32[]{:S(2)}) copy-start(s32[16,16,4]{1,2,0:T(4,128)} %param.12) | copy-start | bytes 12292
  70.9 26.8 %copy-start.4 = (s32[16,16]{1,0:T(8,128)S(1)}, s32[16,16]{1,0:T(8,128)}, u32[]{:S(2)}) copy-start(s32[16,16]{1,0:T(8,128)} %fresh_ref.1) | copy-start | bytes 3076
  77.5 20.3 %copy-start.1 = (bf16[1,6,2,256,256]{4,3,2,1,0:T(8,128)(2,1)S(1)}, bf16[1,6,2,256,256]{4,3,2,1,0:T(8,128)(2,1)}, u32[]{:S(2)}) copy-start(bf16[1,6,2,256,256]{4,3,2,1,0:T(8,128)(2,1)} %param.10) | copy-start | bytes 4718596

commit v4 on v3

--- a/solution.py
+++ b/solution.py
@@ -100,43 +100,33 @@
             ]
 
 
-def gradient_kernel(edge, slots, owner_ref, place_ref, own_hbm, *refs):
-    out_ref, left, rights, shifts, sems = refs[-5:]
-    chips = rights.shape[0]
-    rights_hbm, lefts_hbm = refs[-5 - chips : -5], refs[: -5 - chips]
-    times, rows, tokens = own_hbm.shape
+def gradient_kernel(edge, slots, owner_ref, place_ref, own_ref, *refs):
+    out_ref, left, shifts = refs[-3:]
+    times, rows, tokens = own_ref.shape
+    chips = times // 2
+    rights, others = refs[-3 - chips : -3], refs[: -3 - chips]
     half = rows // 2
     ways = edge // half
     sources = ways * ways
     depth = edge // sources
     dp_index = lax.axis_index("dp")
-    copies = [(rights_hbm[k], rights.at[k]) for k in range(chips)]
     for side, place in enumerate(position(ways)):
         for away in range(ways):
             part = lax.rem(place + (ways - away), ways)
             top = pl.multiple_of(side * edge + part * half, half)
             if away == 0:
-                source = own_hbm.at[:, side * half : (side + 1) * half, :]
+                left[:, pl.ds(top, half), :] = own_ref[:, side * half : (side + 1) * half, :]
             else:
-                source = lefts_hbm[side * (ways - 1) + away - 1]
-            copies.append((source, left.at[:, pl.ds(top, half), :]))
-    copies = [
-        pltpu.make_async_copy(source, target, sems.at[i])
-        for i, (source, target) in enumerate(copies)
-    ]
-    for copy in copies:
-        copy.start()
+                left[:, pl.ds(top, half), :] = others[side * (ways - 1) + away - 1][...]
     shifts[...] = jnp.zeros_like(shifts)
     total = left.shape[1]
     when = token_groups(dp_index, chips)
-    for copy in copies:
-        copy.wait()
     left = jnp.concatenate([left[t] for t in when], axis=1)
-    slab = rights.shape[2]
+    slab = rights[0].shape[1]
     col_blocks = slab // (sources * depth)
     for chunk in range(slab // edge):
         strips = jnp.concatenate(
-            [rights[k // 2, k % 2, chunk * edge : (chunk + 1) * edge, :] for k in range(times)],
+            [rights[k // 2][k % 2, chunk * edge : (chunk + 1) * edge, :] for k in range(times)],
             axis=1,
         )
         product_t = matmul(strips, left, ((1,), (1,))).reshape(edge // depth, depth, total)
@@ -172,8 +162,8 @@
     place_ref,
     fresh_ref,
     in_ref,
-    factors_hbm,
-    roots_hbm,
+    factors_ref,
+    roots_ref,
     factors_out,
     roots_out,
     out_ref,
@@ -186,24 +176,16 @@
     current,
     table,
     picked,
-    state_in,
-    state_done,
-    roots_sems,
+    state_sems,
+    roots_sem,
 ):
     slots, _, edge, _ = state.shape
     local_blocks, sources = owner_ref.shape[1:]
     dp_index, mp_index = lax.axis_index("dp"), lax.axis_index("mp")
-    load_roots = pltpu.make_async_copy(roots_hbm, roots, roots_sems.at[0])
-    load_roots.start()
-    loads = [
-        pltpu.make_async_copy(factors_hbm.at[s], state.at[s], state_in.at[s]) for s in range(slots)
-    ]
     saves = [
-        pltpu.make_async_copy(state.at[s], factors_out.at[s], state_done.at[s])
+        pltpu.make_async_copy(state.at[s], factors_out.at[s], state_sems.at[s])
         for s in range(slots)
     ]
-    for load in loads:
-        load.start()
 
     for s in range(slots + 1):
         table[s] = -1
@@ -229,8 +211,6 @@
 
     depth = edge // sources
     units[...] = jnp.exp2(-in_ref[:, slots * depth :, :].astype(jnp.int32).astype(F32))
-    for load in loads:
-        load.wait()
     for s in range(slots):
         whole = in_ref[:, s * depth : (s + 1) * depth, :].astype(jnp.int32).astype(F32)
         block = jnp.where(table[s] >= 0, whole * units[:, s : s + 1, :], 0.0)
@@ -239,12 +219,12 @@
         halves[s, 1] = low
         left = jnp.concatenate([high, high, low], axis=0)
         right = jnp.concatenate([high, low, high], axis=0)
-        state[s, 0] = state[s, 0] + matmul(left, right, ((0,), (0,)))
+        state[s, 0] = factors_ref[s, 0] + matmul(left, right, ((0,), (0,)))
         left = jnp.concatenate([high, high, low], axis=1)
         right = jnp.concatenate([high, low, high], axis=1)
-        state[s, 1] = state[s, 1] + matmul(left, right, ((1,), (1,)))
-    for save in saves:
-        save.start()
+        state[s, 1] = factors_ref[s, 1] + matmul(left, right, ((1,), (1,)))
+        saves[s].start()
+    roots[...] = roots_ref[...]
 
     row = lax.broadcasted_iota(jnp.int32, (edge, edge), 0)
     col = lax.broadcasted_iota(jnp.int32, (edge, edge), 1)
@@ -286,7 +266,6 @@
         return carry
 
     lax.fori_loop(1, ITERS - 1, step, 0, unroll=2)
-    load_roots.wait()
     for b in range(count):
         x = current[b]
         final = (1.25 * x - 0.25 * product(split(x), split(moving[b]))).astype(BF16)
@@ -295,7 +274,7 @@
         def _():
             roots[picked[b // 2], b % 2] = final
 
-    save_roots = pltpu.make_async_copy(roots, roots_out, roots_sems.at[1])
+    save_roots = pltpu.make_async_copy(roots, roots_out, roots_sem)
     save_roots.start()
 
     for s in range(slots):
@@ -401,13 +380,15 @@
     )(cotangent)
     strips = lax.all_to_all(strips, "mp", split_axis=0, concat_axis=0, tiled=True)
     strips = strips.reshape(slab, tokens)
+    picked, strips = lax.optimization_barrier((picked, strips))
     both = jnp.stack([strips, swapped(strips)])
+    picked, both = lax.optimization_barrier((picked, both))
     first = ring(both)
-    second = ring(first)
     own = lax.all_to_all(picked, "dp", split_axis=0, concat_axis=0, tiled=True)
-    own, both, first, second = lax.optimization_barrier((own, both, first, second))
+    own, both, first = lax.optimization_barrier((own, both, first))
     by_y, by_x = own[:, :half], own[:, half:]
     near = [along_y(by_y, 1), along_y(by_y, ways - 1), along_x(by_x, 1), along_x(by_x, ways - 1)]
+    second = ring(first)
     third = ring(second)
     near, third, by_y, by_x = lax.optimization_barrier((near, third, by_y, by_x))
     far = [along_y(by_y, ways // 2), along_x(by_x, ways // 2)]
@@ -421,15 +402,13 @@
     outgoing = pl.pallas_call(
         functools.partial(gradient_kernel, edge, slots),
         out_shape=jax.ShapeDtypeStruct((mp_count, slots * depth + PAD, edge), jnp.int16),
-        in_specs=[smem, smem, hbm] + [hbm] * len(others + gathered),
+        in_specs=[smem, smem, vmem] + [vmem] * len(others + gathered),
         out_specs=vmem,
         scratch_shapes=[
             VMEM((dp_count, row_count, tokens), BF16),
-            VMEM((dp_count // 2, 2, slab, tokens), BF16),
             VMEM((mp_count, PAD, edge), F32),
-            pltpu.SemaphoreType.DMA((2 + len(others + gathered),)),
         ],
-        compiler_params=pltpu.CompilerParams(vmem_limit_bytes=60 * 1024 * 1024),
+        compiler_params=pltpu.CompilerParams(vmem_limit_bytes=20 * 1024 * 1024),
     )(owner_of, slot_of, own, *others, *gathered)
     incoming = lax.all_to_all(outgoing, "mp", split_axis=0, concat_axis=0, tiled=True)
 
@@ -441,7 +420,7 @@
             jax.ShapeDtypeStruct(roots.shape[1:], BF16),
             jax.ShapeDtypeStruct((mp_count, edge + PAD, edge), jnp.int16),
         ),
-        in_specs=[smem, smem, smem, vmem, hbm, hbm],
+        in_specs=[smem, smem, smem, vmem, vmem, vmem],
         out_specs=(hbm, hbm, vmem),
         scratch_shapes=[
             VMEM(factors.shape[1:], F32),
@@ -454,8 +433,7 @@
             SMEM((slots + 1,), jnp.int32),
             SMEM((REFRESH_MOST + 1,), jnp.int32),
             pltpu.SemaphoreType.DMA((slots,)),
-            pltpu.SemaphoreType.DMA((slots,)),
-            pltpu.SemaphoreType.DMA((2,)),
+            pltpu.SemaphoreType.DMA,
         ],
         compiler_params=pltpu.CompilerParams(vmem_limit_bytes=28 * 1024 * 1024),
     )(owner_of, slot_of, refresh_ids, incoming, factors[0], roots[0])

time: 152 us -> 147 us (0.967)
  waiting for transfers between devices: 31.8 us -> 28 us
  Pallas kernels: 34.2 us -> 30.6 us
  blocking collectives: 50.1 us -> 52.7 us
    pallas_call x1, Pallas kernels: 6.56 us -> 3.35 us  [body(): pl.pallas_call(functools.partial(gradient_kernel, edge, slots), out_shape...]
    all_to_all x1, blocking collectives: 29.8 us -> 32.8 us  [body(): lax.all_to_all(homeward, 'mp', split_axis=0, concat_axis=0, tiled=True)]
    ppermute x4, waiting for transfers between devices: 15.6 us -> 13.8 us  [ring(): return lax.ppermute(x, 'dp', around)]
    ppermute x3, waiting for transfers between devices: 4.33 us -> 2.54 us  [along_x(): lax.ppermute(x, 'mp', [(i, i // ways * ways + (i + k) % ways) for i in ra...]
  transfers between devices with their start and end apart: 16 -> 16, of which waited for: 9 -> 8; matrix products, arithmetic and copies ran while one was open for 0% -> 0% of each run, Pallas kernels for 2% -> 2%
where the time goes in v4:
time: 147 us; the launch traced here: 146 us
  blocking collectives  52.7 us (36%)
  starting transfers between devices  33.8 us (23%)
  Pallas kernels  30.6 us (21%)
  waiting for transfers between devices  28 us (19%)
    all_to_all x1, blocking collectives, body(): lax.all_to_all(homeward, 'mp', split_axis=0, concat_axis=0, tiled=True)  32.8 us
    all_to_all x1, blocking collectives, body(): lax.all_to_all(outgoing, 'mp', split_axis=0, concat_axis=0, tiled=True)  19.9 us
    pallas_call x1, Pallas kernels, body(): pl.pallas_call(owner_kernel, out_shape=(jax.ShapeDtypeStruct(factors.shap...  19.1 us
    ppermute x4, waiting for transfers between devices, ring(): return lax.ppermute(x, 'dp', around)  13.8 us
    ppermute x4, starting transfers between devices, ring(): return lax.ppermute(x, 'dp', around)  12.4 us
    all_to_all x1, starting transfers between devices, body(): own = lax.all_to_all(picked, 'dp', split_axis=0, concat_axis=0, tiled=True)  7.69 us
    all_to_all x1, starting transfers between devices, body(): lax.all_to_all(strips, 'mp', split_axis=0, concat_axis=0, tiled=True)  7.03 us
    ppermute x3, waiting for transfers between devices, along_y(): lax.ppermute(x, 'mp', [(i, (i + ways * k) % mp_count) for i in range(mp_c...  5.59 us
  transfers between devices with their start and end apart: 16, of which 8 were waited for; matrix products, arithmetic and copies ran while one was open for 0% of the time, Pallas kernels for 2%

profile of v4, /device:TPU:96, one launch (start us, length us, event | category | flops | bytes accessed | tf_op | source)
XLA Modules:
  0.0 146.1 jit_solution(791006745553494885)
XLA Ops:
  0.6 1.8 %shard_map.95 = bf16[16,32,128]{2,1,0:T(8,128)(2,1)} custom-call(bf16[128,512]{1,0:T(8,128)(2,1)} %cot_ref.1), custom_call_target="tpu_custom_call" | custom-call | tf_op jit(solution)/shard_map/pallas_call | solution.py:375
  2.4 7.0 %all-to-all-start = ((bf16[16,32,128]{2,1,0:T(8,128)(2,1)}), bf16[16,32,128]{2,1,0:T(8,128)(2,1)S(1)}, u32[]{:S(2)}, u32[]{:S(2)}) async-start(bf16[16,32,128]{2,1,0:T(8,128)(2,1)} %shard_map.95), calls=%async_computation | async-start | bytes 262144 | tf_op jit(solution)/shard_map/all_to_all | solution.py:381
  9.4 0.0 copy-start.2
  9.5 0.0 copy-start.3
  9.5 3.2 %shard_map.94 = bf16[16,128,128]{2,1,0:T(8,128)(2,1)} custom-call(bf16[128,8192]{1,0:T(8,128)(2,1)} %acts_ref.1), custom_call_target="tpu_custom_call" | custom-call | tf_op jit(solution)/shard_map/pallas_call | solution.py:368
  12.7 4.7 %all-to-all-done = bf16[16,32,128]{2,1,0:T(8,128)(2,1)S(1)} async-done(((bf16[16,32,128]{2,1,0:T(8,128)(2,1)}), bf16[16,32,128]{2,1,0:T(8,128)(2,1)S(1)}, u32[]{:S(2)}, u32[]{:S(2)}) %all-to-all-start) | async-done | bytes 131104 | tf_op jit(solution)/shard_map/all_to_all | solution.py:381
  17.4 0.0 collective-permute-start
  17.4 1.3 collective-permute-done
  18.8 7.7 %all-to-all-start.1 = ((bf16[16,128,128]{2,1,0:T(8,128)(2,1)}), bf16[16,128,128]{2,1,0:T(8,128)(2,1)S(1)}, u32[]{:S(2)}, u32[]{:S(2)}) async-start(bf16[16,128,128]{2,1,0:T(8,128)(2,1)} %shard_map.94), calls=%async_computation.1 | async-start | bytes 1048576 | tf_op jit(solution)/shard_map/all_to_all | solution.py:387
  26.5 2.7 %collective-permute-start.1 = (bf16[2,512,128]{2,1,0:T(8,128)(2,1)S(1)}, bf16[2,512,128]{2,1,0:T(8,128)(2,1)S(1)}, u32[]{:S(2)}, u32[]{:S(2)}) collective-permute-start(bf16[2,512,128]{2,1,0:T(8,128)(2,1)S(1)} %pad_maximum_fusion.refs_6_), channel_id=1, source_target_pairs={{0,32},{16,240},{32,64},{48,16},{64,96},{80,48},{96,128},{112,80},... | collective-permute-start | bytes 786440 | tf_op jit(solution)/shard_map/ppermute | solution.py:366
  29.2 13.1 %collective-permute-done.1.refs_7_ = bf16[2,512,128]{2,1,0:T(8,128)(2,1)S(1)} collective-permute-done((bf16[2,512,128]{2,1,0:T(8,128)(2,1)S(1)}, bf16[2,512,128]{2,1,0:T(8,128)(2,1)S(1)}, u32[]{:S(2)}, u32[]{:S(2)}) %collective-permute-start.1) | collective-permute-done | bytes 262176 | tf_op jit(solution)/shard_map/ppermute | solution.py:366
  42.3 0.0 all-to-all-done.1.own_ref
  42.3 2.7 %collective-permute-start.6 = (bf16[2,512,128]{2,1,0:T(8,128)(2,1)S(1)}, bf16[2,512,128]{2,1,0:T(8,128)(2,1)S(1)}, u32[]{:S(2)}, u32[]{:S(2)}) collective-permute-start(bf16[2,512,128]{2,1,0:T(8,128)(2,1)S(1)} %collective-permute-done.1.refs_7_), channel_id=1, source_target_pairs={{0,32},{16,240},{32,64},{48,16},{64,96},{80,48},{96,128},{112,80},... | collective-permute-start | bytes 786440 | tf_op jit(solution)/shard_map/ppermute | solution.py:366
  45.0 1.0 collective-permute-start.5
  46.0 1.1 collective-permute-start.4
  47.1 0.9 collective-permute-start.3
  48.0 1.2 collective-permute-start.2
  49.2 0.0 collective-permute-done.6.refs_9_
  49.2 3.4 %collective-permute-start.7 = (bf16[2,512,128]{2,1,0:T(8,128)(2,1)S(1)}, bf16[2,512,128]{2,1,0:T(8,128)(2,1)S(1)}, u32[]{:S(2)}, u32[]{:S(2)}) collective-permute-start(bf16[2,512,128]{2,1,0:T(8,128)(2,1)S(1)} %collective-permute-done.6.refs_9_), channel_id=1, source_target_pairs={{0,32},{16,240},{32,64},{48,16},{64,96},{80,48},{96,128},{112,80},... | collective-permute-start | bytes 786440 | tf_op jit(solution)/shard_map/ppermute | solution.py:366
  52.6 0.0 collective-permute-done.5.refs_5_
  52.6 0.0 collective-permute-start.10
  52.6 1.9 %collective-permute-done.4.refs_3_ = bf16[16,64,128]{2,1,0:T(8,128)(2,1)S(1)} collective-permute-done((bf16[16,64,128]{2,1,0:T(8,128)(2,1)S(1)}, bf16[16,64,128]{2,1,0:T(8,128)(2,1)S(1)}, u32[]{:S(2)}, u32[]{:S(2)}) %collective-permute-start.4) | collective-permute-done | bytes 262176 | tf_op jit(solution)/shard_map/ppermute | solution.py:358
  54.4 0.0 collective-permute-start.11
  54.4 0.0 collective-permute-done.3.refs_2_
  54.4 1.4 collective-permute-done.2.refs_0_
  55.8 0.6 collective-permute-done.7.refs_11_
  56.5 1.0 collective-permute-start.8
  57.4 1.5 %collective-permute-start.9 = (bf16[16,64,128]{2,1,0:T(8,128)(2,1)S(1)}, bf16[16,64,128]{2,1,0:T(8,128)(2,1)S(1)}, u32[]{:S(2)}, u32[]{:S(2)}) collective-permute-start(bf16[16,64,128]{2,1,0:T(8,128)(2,1)S(1)} %get-tuple-element.30), channel_id=1, source_target_pairs={{0,2},{1,3},{2,0},{3,1},{4,6},{5,7},{6,4},{7,5},{8,10},{9,11},{10,... | collective-permute-start | bytes 786440 | tf_op jit(solution)/shard_map/ppermute | solution.py:358
  58.9 3.7 %collective-permute-start.13 = (bf16[2,512,128]{2,1,0:T(8,128)(2,1)S(1)}, bf16[2,512,128]{2,1,0:T(8,128)(2,1)S(1)}, u32[]{:S(2)}, u32[]{:S(2)}) collective-permute-start(bf16[2,512,128]{2,1,0:T(8,128)(2,1)S(1)} %collective-permute-done.7.refs_11_), channel_id=1, source_target_pairs={{0,32},{16,240},{32,64},{48,16},{64,96},{80,48},{96,128},{112,80},... | collective-permute-start | bytes 786440 | tf_op jit(solution)/shard_map/ppermute | solution.py:366
  62.6 0.0 collective-permute-done.10.refs_8_
  62.6 0.0 collective-permute-start.12
  62.6 0.0 collective-permute-done.11.refs_10_
  62.6 4.2 %collective-permute-done.8.refs_1_ = bf16[16,64,128]{2,1,0:T(8,128)(2,1)S(1)} collective-permute-done((bf16[16,64,128]{2,1,0:T(8,128)(2,1)S(1)}, bf16[16,64,128]{2,1,0:T(8,128)(2,1)S(1)}, u32[]{:S(2)}, u32[]{:S(2)}) %collective-permute-start.8) | collective-permute-done | bytes 262176 | tf_op jit(solution)/shard_map/ppermute | solution.py:355
  66.8 0.7 collective-permute-done.9.refs_4_
  67.5 0.0 collective-permute-done.13.refs_13_
  67.5 0.0 collective-permute-done.12.refs_12_
  67.5 0.0 copy-done.2
  67.5 0.0 copy-done.3
  67.5 0.0 copy-start
  67.5 0.0 copy-start.1
  67.5 0.0 copy-start.4
  67.6 3.3 %shard_map.96 = s16[16,112,256]{2,1,0:T(8,128)(2,1)S(1)} custom-call(s32[16,4,16]{2,1,0:T(4,128)S(1)} %bitcast.12, s32[16,4,16]{2,1,0:T(4,128)S(1)} %bitcast.14, bf16[16,128,128]{2,1,0:T(8,128)(2,1)S(1)} %all-to-all-done.1.own_ref, bf16[16,64,128]{2,1,0:T(8,128)(2,1)S(1)} %collective-permute-done.2.refs_0_, ...), custom_call_target="tpu_custom_call" | custom-call | tf_op jit(solution)/shard_map/pallas_call | solution.py:402
  70.9 19.9 %all_to_all.20.in_ref = s16[16,112,256]{2,1,0:T(8,128)(2,1)S(1)} all-to-all(s16[16,112,256]{2,1,0:T(8,128)(2,1)S(1)} %shard_map.96), channel_id=1, replica_groups=mesh['dp'=16,'mp'=16] {'mp'}, dimensions={0} | all-to-all | bytes 1835008 | tf_op jit(solution)/shard_map/all_to_all | solution.py:413
  90.8 0.0 copy-done
  90.8 0.0 copy-done.1
  90.8 0.0 copy-done.4
  90.8 19.1 %shard_map.97 = (f32[6,2,256,256]{3,2,1,0:T(8,128)}, bf16[6,2,256,256]{3,2,1,0:T(8,128)(2,1)}, s16[16,272,256]{2,1,0:T(8,128)(2,1)S(1)}) custom-call(s32[16,4,16]{2,1,0:T(4,128)S(1)} %bitcast.13, s32[16,4,16]{2,1,0:T(4,128)S(1)} %bitcast.15, s32[16,16]{1,0:T(8,128)S(1)} %copy-done.4, s16[16,112,256]{2,1,0:T(8,128)(2,1)S(1)} %all_to_all.20.in_ref, ...), custom_call_target="tpu_custom_call" | custom-call | tf_op jit(solution)/shard_map/pallas_call | solution.py:416
  109.9 32.8 %all_to_all.21.in_hbm = s16[16,272,256]{2,1,0:T(8,128)(2,1)} all-to-all(s16[16,272,256]{2,1,0:T(8,128)(2,1)S(1)} %get-tuple-element.34), channel_id=1, replica_groups=mesh['dp'=16,'mp'=16] {'mp'}, dimensions={0} | all-to-all | bytes 4456448 | tf_op jit(solution)/shard_map/all_to_all | solution.py:440
  142.7 3.2 %shard_map.98 = f32[512,512]{1,0:T(8,128)} custom-call(s32[16,4,16]{2,1,0:T(4,128)} %bitcast.11, s16[16,272,256]{2,1,0:T(8,128)(2,1)} %all_to_all.21.in_hbm), custom_call_target="tpu_custom_call" | custom-call | tf_op jit(solution)/shard_map/pallas_call | solution.py:443
  (2 shorter events, 0.1 us)
Async XLA Ops:
  2.4 15.0 %all-to-all-start = ((bf16[16,32,128]{2,1,0:T(8,128)(2,1)}), bf16[16,32,128]{2,1,0:T(8,128)(2,1)S(1)}, u32[]{:S(2)}, u32[]{:S(2)}) async-start(bf16[16,32,128]{2,1,0:T(8,128)(2,1)} %shard_map.95), calls=%async_computation | async-start | bytes 262144 | tf_op jit(solution)/shard_map/all_to_all | solution.py:381
  9.4 58.1 %copy-start.2 = (s32[16,16,4]{1,2,0:T(4,128)S(1)}, s32[16,16,4]{1,2,0:T(4,128)}, u32[]{:S(2)}) copy-start(s32[16,16,4]{1,2,0:T(4,128)} %param.11) | copy-start | bytes 12292
  9.5 58.1 %copy-start.3 = (s32[16,16,4]{1,2,0:T(4,128)S(1)}, s32[16,16,4]{1,2,0:T(4,128)}, u32[]{:S(2)}) copy-start(s32[16,16,4]{1,2,0:T(4,128)} %param.12) | copy-start | bytes 12292
  17.4 1.3 collective-permute-start
  18.8 23.5 %all-to-all-start.1 = ((bf16[16,128,128]{2,1,0:T(8,128)(2,1)}), bf16[16,128,128]{2,1,0:T(8,128)(2,1)S(1)}, u32[]{:S(2)}, u32[]{:S(2)}) async-start(bf16[16,128,128]{2,1,0:T(8,128)(2,1)} %shard_map.94), calls=%async_computation.1 | async-start | bytes 1048576 | tf_op jit(solution)/shard_map/all_to_all | solution.py:387
  26.5 15.8 %collective-permute-start.1 = (bf16[2,512,128]{2,1,0:T(8,128)(2,1)S(1)}, bf16[2,512,128]{2,1,0:T(8,128)(2,1)S(1)}, u32[]{:S(2)}, u32[]{:S(2)}) collective-permute-start(bf16[2,512,128]{2,1,0:T(8,128)(2,1)S(1)} %pad_maximum_fusion.refs_6_), channel_id=1, source_target_pairs={{0,32},{16,240},{32,64},{48,16},{64,96},{80,48},{96,128},{112,80},... | collective-permute-start | bytes 786440 | tf_op jit(solution)/shard_map/ppermute | solution.py:366
  42.3 6.8 %collective-permute-start.6 = (bf16[2,512,128]{2,1,0:T(8,128)(2,1)S(1)}, bf16[2,512,128]{2,1,0:T(8,128)(2,1)S(1)}, u32[]{:S(2)}, u32[]{:S(2)}) collective-permute-start(bf16[2,512,128]{2,1,0:T(8,128)(2,1)S(1)} %collective-permute-done.1.refs_7_), channel_id=1, source_target_pairs={{0,32},{16,240},{32,64},{48,16},{64,96},{80,48},{96,128},{112,80},... | collective-permute-start | bytes 786440 | tf_op jit(solution)/shard_map/ppermute | solution.py:366
  45.0 7.6 %collective-permute-start.5 = (bf16[16,64,128]{2,1,0:T(8,128)(2,1)S(1)}, bf16[16,64,128]{2,1,0:T(8,128)(2,1)S(1)}, u32[]{:S(2)}, u32[]{:S(2)}) collective-permute-start(bf16[16,64,128]{2,1,0:T(8,128)(2,1)S(1)} %get-tuple-element.30), channel_id=1, source_target_pairs={{0,3},{1,0},{2,1},{3,2},{4,7},{5,4},{6,5},{7,6},{8,11},{9,8},{10,9... | collective-permute-start | bytes 786440 | tf_op jit(solution)/shard_map/ppermute | solution.py:358
  46.0 8.4 %collective-permute-start.4 = (bf16[16,64,128]{2,1,0:T(8,128)(2,1)S(1)}, bf16[16,64,128]{2,1,0:T(8,128)(2,1)S(1)}, u32[]{:S(2)}, u32[]{:S(2)}) collective-permute-start(bf16[16,64,128]{2,1,0:T(8,128)(2,1)S(1)} %get-tuple-element.30), channel_id=1, source_target_pairs={{0,1},{1,2},{2,3},{3,0},{4,5},{5,6},{6,7},{7,4},{8,9},{9,10},{10,1... | collective-permute-start | bytes 786440 | tf_op jit(solution)/shard_map/ppermute | solution.py:358
  47.1 7.3 %collective-permute-start.3 = (bf16[16,64,128]{2,1,0:T(8,128)(2,1)S(1)}, bf16[16,64,128]{2,1,0:T(8,128)(2,1)S(1)}, u32[]{:S(2)}, u32[]{:S(2)}) collective-permute-start(bf16[16,64,128]{2,1,0:T(8,128)(2,1)S(1)} %get-tuple-element.27), channel_id=1, source_target_pairs={{0,12},{1,13},{2,14},{3,15},{4,0},{5,1},{6,2},{7,3},{8,4},{9,5},{1... | collective-permute-start | bytes 786440 | tf_op jit(solution)/shard_map/ppermute | solution.py:355
  48.0 7.8 %collective-permute-start.2 = (bf16[16,64,128]{2,1,0:T(8,128)(2,1)S(1)}, bf16[16,64,128]{2,1,0:T(8,128)(2,1)S(1)}, u32[]{:S(2)}, u32[]{:S(2)}) collective-permute-start(bf16[16,64,128]{2,1,0:T(8,128)(2,1)S(1)} %get-tuple-element.27), channel_id=1, source_target_pairs={{0,4},{1,5},{2,6},{3,7},{4,8},{5,9},{6,10},{7,11},{8,12},{9,13},{1... | collective-permute-start | bytes 786440 | tf_op jit(solution)/shard_map/ppermute | solution.py:355
  49.2 7.3 %collective-permute-start.7 = (bf16[2,512,128]{2,1,0:T(8,128)(2,1)S(1)}, bf16[2,512,128]{2,1,0:T(8,128)(2,1)S(1)}, u32[]{:S(2)}, u32[]{:S(2)}) collective-permute-start(bf16[2,512,128]{2,1,0:T(8,128)(2,1)S(1)} %collective-permute-done.6.refs_9_), channel_id=1, source_target_pairs={{0,32},{16,240},{32,64},{48,16},{64,96},{80,48},{96,128},{112,80},... | collective-permute-start | bytes 786440 | tf_op jit(solution)/shard_map/ppermute | solution.py:366
  52.6 10.0 %collective-permute-start.10 = (bf16[2,512,128]{2,1,0:T(8,128)(2,1)S(1)}, bf16[2,512,128]{2,1,0:T(8,128)(2,1)S(1)}, u32[]{:S(2)}, u32[]{:S(2)}) collective-permute-start(bf16[2,512,128]{2,1,0:T(8,128)(2,1)S(1)} %collective-permute-done.1.refs_7_), channel_id=1, source_target_pairs={{0,16},{16,0},{32,48},{48,32},{64,80},{80,64},{96,112},{112,96},{1... | collective-permute-start | bytes 786440 | tf_op jit(solution)/shard_map/ppermute | solution.py:363
  54.4 8.2 %collective-permute-start.11 = (bf16[2,512,128]{2,1,0:T(8,128)(2,1)S(1)}, bf16[2,512,128]{2,1,0:T(8,128)(2,1)S(1)}, u32[]{:S(2)}, u32[]{:S(2)}) collective-permute-start(bf16[2,512,128]{2,1,0:T(8,128)(2,1)S(1)} %collective-permute-done.6.refs_9_), channel_id=1, source_target_pairs={{0,16},{16,0},{32,48},{48,32},{64,80},{80,64},{96,112},{112,96},{1... | collective-permute-start | bytes 786440 | tf_op jit(solution)/shard_map/ppermute | solution.py:363
  56.5 10.4 %collective-permute-start.8 = (bf16[16,64,128]{2,1,0:T(8,128)(2,1)S(1)}, bf16[16,64,128]{2,1,0:T(8,128)(2,1)S(1)}, u32[]{:S(2)}, u32[]{:S(2)}) collective-permute-start(bf16[16,64,128]{2,1,0:T(8,128)(2,1)S(1)} %get-tuple-element.27), channel_id=1, source_target_pairs={{0,8},{1,9},{2,10},{3,11},{4,12},{5,13},{6,14},{7,15},{8,0},{9,1},... | collective-permute-start | bytes 786440 | tf_op jit(solution)/shard_map/ppermute | solution.py:355
  57.4 10.1 %collective-permute-start.9 = (bf16[16,64,128]{2,1,0:T(8,128)(2,1)S(1)}, bf16[16,64,128]{2,1,0:T(8,128)(2,1)S(1)}, u32[]{:S(2)}, u32[]{:S(2)}) collective-permute-start(bf16[16,64,128]{2,1,0:T(8,128)(2,1)S(1)} %get-tuple-element.30), channel_id=1, source_target_pairs={{0,2},{1,3},{2,0},{3,1},{4,6},{5,7},{6,4},{7,5},{8,10},{9,11},{10,... | collective-permute-start | bytes 786440 | tf_op jit(solution)/shard_map/ppermute | solution.py:358
  58.9 8.6 %collective-permute-start.13 = (bf16[2,512,128]{2,1,0:T(8,128)(2,1)S(1)}, bf16[2,512,128]{2,1,0:T(8,128)(2,1)S(1)}, u32[]{:S(2)}, u32[]{:S(2)}) collective-permute-start(bf16[2,512,128]{2,1,0:T(8,128)(2,1)S(1)} %collective-permute-done.7.refs_11_), channel_id=1, source_target_pairs={{0,32},{16,240},{32,64},{48,16},{64,96},{80,48},{96,128},{112,80},... | collective-permute-start | bytes 786440 | tf_op jit(solution)/shard_map/ppermute | solution.py:366
  62.6 4.9 %collective-permute-start.12 = (bf16[2,512,128]{2,1,0:T(8,128)(2,1)S(1)}, bf16[2,512,128]{2,1,0:T(8,128)(2,1)S(1)}, u32[]{:S(2)}, u32[]{:S(2)}) collective-permute-start(bf16[2,512,128]{2,1,0:T(8,128)(2,1)S(1)} %collective-permute-done.7.refs_11_), channel_id=1, source_target_pairs={{0,16},{16,0},{32,48},{48,32},{64,80},{80,64},{96,112},{112,96},{1... | collective-permute-start | bytes 786440 | tf_op jit(solution)/shard_map/ppermute | solution.py:363
  67.5 23.3 %copy-start = (f32[1,6,2,256,256]{4,3,2,1,0:T(8,128)S(1)}, f32[1,6,2,256,256]{4,3,2,1,0:T(8,128)}, u32[]{:S(2)}) copy-start(f32[1,6,2,256,256]{4,3,2,1,0:T(8,128)} %param.9) | copy-start | bytes 9437188
  67.5 23.3 %copy-start.1 = (bf16[1,6,2,256,256]{4,3,2,1,0:T(8,128)(2,1)S(1)}, bf16[1,6,2,256,256]{4,3,2,1,0:T(8,128)(2,1)}, u32[]{:S(2)}) copy-start(bf16[1,6,2,256,256]{4,3,2,1,0:T(8,128)(2,1)} %param.10) | copy-start | bytes 4718596
  67.5 23.3 %copy-start.4 = (s32[16,16]{1,0:T(8,128)S(1)}, s32[16,16]{1,0:T(8,128)}, u32[]{:S(2)}) copy-start(s32[16,16]{1,0:T(8,128)} %fresh_ref.1) | copy-start | bytes 3076

commit v5 on v4

--- a/solution.py
+++ b/solution.py
@@ -306,25 +306,19 @@
         save.wait()
 
 
-def home_kernel(edge, owner_ref, in_hbm, out_hbm, blocks, values, sems):
+def home_kernel(edge, owner_ref, in_ref, out_hbm, values, sems):
     dp_index, mp_index = lax.axis_index("dp"), lax.axis_index("mp")
     col_blocks = out_hbm.shape[1] // edge
-    loads, saves = [], []
-    for j in range(blocks.shape[0]):
-        owner = owner_ref[dp_index, j, mp_index]
+    saves = []
+    for j in range(values.shape[0]):
         top, left = (j // col_blocks) * edge, (j % col_blocks) * edge
-        loads.append(pltpu.make_async_copy(in_hbm.at[owner], blocks.at[j], sems.at[0, j]))
+        whole, unit = decode(in_ref, owner_ref[dp_index, j, mp_index], edge)
+        values[j] = whole * unit
         saves.append(
             pltpu.make_async_copy(
-                values.at[j], out_hbm.at[top : top + edge, left : left + edge], sems.at[1, j]
+                values.at[j], out_hbm.at[top : top + edge, left : left + edge], sems.at[j]
             )
         )
-    for load in loads:
-        load.start()
-    for j, load in enumerate(loads):
-        load.wait()
-        whole, unit = decode(blocks, j, edge)
-        values[j] = whole * unit
         saves[j].start()
     for save in saves:
         save.wait()
@@ -390,7 +384,7 @@
     near = [along_y(by_y, 1), along_y(by_y, ways - 1), along_x(by_x, 1), along_x(by_x, ways - 1)]
     second = ring(first)
     third = ring(second)
-    near, third, by_y, by_x = lax.optimization_barrier((near, third, by_y, by_x))
+    near, second, by_y, by_x = lax.optimization_barrier((near, second, by_y, by_x))
     far = [along_y(by_y, ways // 2), along_x(by_x, ways // 2)]
     others = [near[0], far[0], near[1], near[2], far[1], near[3]]
     gathered = [both]
@@ -443,12 +437,11 @@
     direction = pl.pallas_call(
         functools.partial(home_kernel, edge),
         out_shape=jax.ShapeDtypeStruct((row_count, slab), F32),
-        in_specs=[smem, hbm],
+        in_specs=[smem, vmem],
         out_specs=hbm,
         scratch_shapes=[
-            VMEM((local_blocks, edge + PAD, edge), jnp.int16),
             VMEM((local_blocks, edge, edge), F32),
-            pltpu.SemaphoreType.DMA((2, local_blocks)),
+            pltpu.SemaphoreType.DMA((local_blocks,)),
         ],
     )(owner_of, returned)
     return (direction, factors_next[None], roots_next[None])

time: 147 us -> 145 us (0.986)
  blocking collectives: 52.7 us -> 54.6 us
  waiting for transfers between devices: 28 us -> 26.4 us
  starting transfers between devices: 33.8 us -> 32.3 us
    all_to_all x1, blocking collectives: 19.9 us -> 21.9 us  [body(): lax.all_to_all(outgoing, 'mp', split_axis=0, concat_axis=0, tiled=True)]
where the time goes in v5:
time: 145 us; the launch traced here: 144 us
  blocking collectives  54.6 us (38%)
  starting transfers between devices  32.3 us (22%)
  Pallas kernels  30.1 us (21%)
  waiting for transfers between devices  26.4 us (18%)
    all_to_all x1, blocking collectives, body(): lax.all_to_all(homeward, 'mp', split_axis=0, concat_axis=0, tiled=True)  32.7 us
    all_to_all x1, blocking collectives, body(): lax.all_to_all(outgoing, 'mp', split_axis=0, concat_axis=0, tiled=True)  21.9 us
    pallas_call x1, Pallas kernels, body(): pl.pallas_call(owner_kernel, out_shape=(jax.ShapeDtypeStruct(factors.shap...  19.1 us
    ppermute x4, waiting for transfers between devices, ring(): return lax.ppermute(x, 'dp', around)  13.6 us
    ppermute x4, starting transfers between devices, ring(): return lax.ppermute(x, 'dp', around)  11.7 us
    all_to_all x1, starting transfers between devices, body(): own = lax.all_to_all(picked, 'dp', split_axis=0, concat_axis=0, tiled=True)  7.69 us
    all_to_all x1, starting transfers between devices, body(): lax.all_to_all(strips, 'mp', split_axis=0, concat_axis=0, tiled=True)  7.03 us
    all_to_all x1, waiting for transfers between devices, body(): lax.all_to_all(strips, 'mp', split_axis=0, concat_axis=0, tiled=True)  4.75 us
  transfers between devices with their start and end apart: 16, of which 8 were waited for; matrix products, arithmetic and copies ran while one was open for 0% of the time, Pallas kernels for 2%

profile of v5, /device:TPU:96, one launch (start us, length us, event | category | flops | bytes accessed | tf_op | source)
XLA Modules:
  0.0 144.4 jit_solution(11625393506533378091)
XLA Ops:
  0.6 1.8 %shard_map.95 = bf16[16,32,128]{2,1,0:T(8,128)(2,1)} custom-call(bf16[128,512]{1,0:T(8,128)(2,1)} %cot_ref.1), custom_call_target="tpu_custom_call" | custom-call | tf_op jit(solution)/shard_map/pallas_call | solution.py:369
  2.4 7.0 %all-to-all-start = ((bf16[16,32,128]{2,1,0:T(8,128)(2,1)}), bf16[16,32,128]{2,1,0:T(8,128)(2,1)S(1)}, u32[]{:S(2)}, u32[]{:S(2)}) async-start(bf16[16,32,128]{2,1,0:T(8,128)(2,1)} %shard_map.95), calls=%async_computation | async-start | bytes 262144 | tf_op jit(solution)/shard_map/all_to_all | solution.py:375
  9.4 0.0 copy-start.2
  9.5 0.0 copy-start.3
  9.5 3.2 %shard_map.94 = bf16[16,128,128]{2,1,0:T(8,128)(2,1)} custom-call(bf16[128,8192]{1,0:T(8,128)(2,1)} %acts_ref.1), custom_call_target="tpu_custom_call" | custom-call | tf_op jit(solution)/shard_map/pallas_call | solution.py:362
  12.7 4.7 %all-to-all-done = bf16[16,32,128]{2,1,0:T(8,128)(2,1)S(1)} async-done(((bf16[16,32,128]{2,1,0:T(8,128)(2,1)}), bf16[16,32,128]{2,1,0:T(8,128)(2,1)S(1)}, u32[]{:S(2)}, u32[]{:S(2)}) %all-to-all-start) | async-done | bytes 131104 | tf_op jit(solution)/shard_map/all_to_all | solution.py:375
  17.4 0.0 collective-permute-start
  17.4 1.3 collective-permute-done
  18.8 7.7 %all-to-all-start.1 = ((bf16[16,128,128]{2,1,0:T(8,128)(2,1)}), bf16[16,128,128]{2,1,0:T(8,128)(2,1)S(1)}, u32[]{:S(2)}, u32[]{:S(2)}) async-start(bf16[16,128,128]{2,1,0:T(8,128)(2,1)} %shard_map.94), calls=%async_computation.1 | async-start | bytes 1048576 | tf_op jit(solution)/shard_map/all_to_all | solution.py:381
  26.5 2.7 %collective-permute-start.1 = (bf16[2,512,128]{2,1,0:T(8,128)(2,1)S(1)}, bf16[2,512,128]{2,1,0:T(8,128)(2,1)S(1)}, u32[]{:S(2)}, u32[]{:S(2)}) collective-permute-start(bf16[2,512,128]{2,1,0:T(8,128)(2,1)S(1)} %pad_maximum_fusion.refs_6_), channel_id=1, source_target_pairs={{0,32},{16,240},{32,64},{48,16},{64,96},{80,48},{96,128},{112,80},... | collective-permute-start | bytes 786440 | tf_op jit(solution)/shard_map/ppermute | solution.py:360
  29.2 13.1 %collective-permute-done.1.refs_7_ = bf16[2,512,128]{2,1,0:T(8,128)(2,1)S(1)} collective-permute-done((bf16[2,512,128]{2,1,0:T(8,128)(2,1)S(1)}, bf16[2,512,128]{2,1,0:T(8,128)(2,1)S(1)}, u32[]{:S(2)}, u32[]{:S(2)}) %collective-permute-start.1) | collective-permute-done | bytes 262176 | tf_op jit(solution)/shard_map/ppermute | solution.py:360
  42.3 0.0 all-to-all-done.1.own_ref
  42.3 2.7 %collective-permute-start.6 = (bf16[2,512,128]{2,1,0:T(8,128)(2,1)S(1)}, bf16[2,512,128]{2,1,0:T(8,128)(2,1)S(1)}, u32[]{:S(2)}, u32[]{:S(2)}) collective-permute-start(bf16[2,512,128]{2,1,0:T(8,128)(2,1)S(1)} %collective-permute-done.1.refs_7_), channel_id=1, source_target_pairs={{0,32},{16,240},{32,64},{48,16},{64,96},{80,48},{96,128},{112,80},... | collective-permute-start | bytes 786440 | tf_op jit(solution)/shard_map/ppermute | solution.py:360
  45.0 1.0 collective-permute-start.5
  46.0 1.1 collective-permute-start.4
  47.1 0.9 collective-permute-start.3
  48.0 1.2 collective-permute-start.2
  49.2 0.0 collective-permute-done.6.refs_9_
  49.2 3.4 %collective-permute-start.11 = (bf16[2,512,128]{2,1,0:T(8,128)(2,1)S(1)}, bf16[2,512,128]{2,1,0:T(8,128)(2,1)S(1)}, u32[]{:S(2)}, u32[]{:S(2)}) collective-permute-start(bf16[2,512,128]{2,1,0:T(8,128)(2,1)S(1)} %collective-permute-done.6.refs_9_), channel_id=1, source_target_pairs={{0,32},{16,240},{32,64},{48,16},{64,96},{80,48},{96,128},{112,80},... | collective-permute-start | bytes 786440 | tf_op jit(solution)/shard_map/ppermute | solution.py:360
  52.6 0.0 collective-permute-done.5.refs_5_
  52.6 0.0 collective-permute-start.9
  52.6 1.9 %collective-permute-done.4.refs_3_ = bf16[16,64,128]{2,1,0:T(8,128)(2,1)S(1)} collective-permute-done((bf16[16,64,128]{2,1,0:T(8,128)(2,1)S(1)}, bf16[16,64,128]{2,1,0:T(8,128)(2,1)S(1)}, u32[]{:S(2)}, u32[]{:S(2)}) %collective-permute-start.4) | collective-permute-done | bytes 262176 | tf_op jit(solution)/shard_map/ppermute | solution.py:352
  54.4 0.0 collective-permute-done.3.refs_2_
  54.4 1.4 collective-permute-done.2.refs_0_
  55.8 0.3 collective-permute-start.7
  56.1 1.5 %collective-permute-start.8 = (bf16[16,64,128]{2,1,0:T(8,128)(2,1)S(1)}, bf16[16,64,128]{2,1,0:T(8,128)(2,1)S(1)}, u32[]{:S(2)}, u32[]{:S(2)}) collective-permute-start(bf16[16,64,128]{2,1,0:T(8,128)(2,1)S(1)} %get-tuple-element.30), channel_id=1, source_target_pairs={{0,2},{1,3},{2,0},{3,1},{4,6},{5,7},{6,4},{7,5},{8,10},{9,11},{10,... | collective-permute-start | bytes 786440 | tf_op jit(solution)/shard_map/ppermute | solution.py:352
  57.6 0.0 collective-permute-start.10
  57.6 0.0 collective-permute-done.11.refs_11_
  57.6 3.0 %collective-permute-start.13 = (bf16[2,512,128]{2,1,0:T(8,128)(2,1)S(1)}, bf16[2,512,128]{2,1,0:T(8,128)(2,1)S(1)}, u32[]{:S(2)}, u32[]{:S(2)}) collective-permute-start(bf16[2,512,128]{2,1,0:T(8,128)(2,1)S(1)} %collective-permute-done.11.refs_11_), channel_id=1, source_target_pairs={{0,32},{16,240},{32,64},{48,16},{64,96},{80,48},{96,128},{112,80},... | collective-permute-start | bytes 786440 | tf_op jit(solution)/shard_map/ppermute | solution.py:360
  60.6 0.0 collective-permute-done.9.refs_8_
  60.6 0.0 collective-permute-start.12
  60.6 3.1 %collective-permute-done.7.refs_1_ = bf16[16,64,128]{2,1,0:T(8,128)(2,1)S(1)} collective-permute-done((bf16[16,64,128]{2,1,0:T(8,128)(2,1)S(1)}, bf16[16,64,128]{2,1,0:T(8,128)(2,1)S(1)}, u32[]{:S(2)}, u32[]{:S(2)}) %collective-permute-start.7) | collective-permute-done | bytes 262176 | tf_op jit(solution)/shard_map/ppermute | solution.py:349
  63.7 0.3 collective-permute-done.8.refs_4_
  64.0 0.0 collective-permute-done.10.refs_10_
  64.0 0.5 collective-permute-done.13.refs_13_
  64.4 0.0 collective-permute-done.12.refs_12_
  64.5 0.0 copy-done.2
  64.5 0.0 copy-done.3
  64.5 0.0 copy-start
  64.5 0.0 copy-start.1
  64.5 0.0 copy-start.4
  64.5 3.3 %shard_map.96 = s16[16,112,256]{2,1,0:T(8,128)(2,1)S(1)} custom-call(s32[16,4,16]{2,1,0:T(4,128)S(1)} %bitcast.12, s32[16,4,16]{2,1,0:T(4,128)S(1)} %bitcast.14, bf16[16,128,128]{2,1,0:T(8,128)(2,1)S(1)} %all-to-all-done.1.own_ref, bf16[16,64,128]{2,1,0:T(8,128)(2,1)S(1)} %collective-permute-done.2.refs_0_, ...), custom_call_target="tpu_custom_call" | custom-call | tf_op jit(solution)/shard_map/pallas_call | solution.py:396
  67.8 21.9 %all_to_all.20.in_ref = s16[16,112,256]{2,1,0:T(8,128)(2,1)S(1)} all-to-all(s16[16,112,256]{2,1,0:T(8,128)(2,1)S(1)} %shard_map.96), channel_id=1, replica_groups=mesh['dp'=16,'mp'=16] {'mp'}, dimensions={0} | all-to-all | bytes 1835008 | tf_op jit(solution)/shard_map/all_to_all | solution.py:407
  89.8 0.0 copy-done
  89.8 0.0 copy-done.1
  89.8 0.0 copy-done.4
  89.8 19.1 %shard_map.97 = (f32[6,2,256,256]{3,2,1,0:T(8,128)}, bf16[6,2,256,256]{3,2,1,0:T(8,128)(2,1)}, s16[16,272,256]{2,1,0:T(8,128)(2,1)S(1)}) custom-call(s32[16,4,16]{2,1,0:T(4,128)S(1)} %bitcast.13, s32[16,4,16]{2,1,0:T(4,128)S(1)} %bitcast.15, s32[16,16]{1,0:T(8,128)S(1)} %copy-done.4, s16[16,112,256]{2,1,0:T(8,128)(2,1)S(1)} %all_to_all.20.in_ref, ...), custom_call_target="tpu_custom_call" | custom-call | tf_op jit(solution)/shard_map/pallas_call | solution.py:410
  108.9 32.7 %all_to_all.21.in_ref = s16[16,272,256]{2,1,0:T(8,128)(2,1)} all-to-all(s16[16,272,256]{2,1,0:T(8,128)(2,1)S(1)} %get-tuple-element.34), channel_id=1, replica_groups=mesh['dp'=16,'mp'=16] {'mp'}, dimensions={0} | all-to-all | bytes 4456448 | tf_op jit(solution)/shard_map/all_to_all | solution.py:434
  141.6 2.7 %shard_map.98 = f32[512,512]{1,0:T(8,128)} custom-call(s32[16,4,16]{2,1,0:T(4,128)} %bitcast.11, s16[16,272,256]{2,1,0:T(8,128)(2,1)} %all_to_all.21.in_ref), custom_call_target="tpu_custom_call" | custom-call | tf_op jit(solution)/shard_map/pallas_call | solution.py:437
  (2 shorter events, 0.1 us)
Async XLA Ops:
  2.4 15.0 %all-to-all-start = ((bf16[16,32,128]{2,1,0:T(8,128)(2,1)}), bf16[16,32,128]{2,1,0:T(8,128)(2,1)S(1)}, u32[]{:S(2)}, u32[]{:S(2)}) async-start(bf16[16,32,128]{2,1,0:T(8,128)(2,1)} %shard_map.95), calls=%async_computation | async-start | bytes 262144 | tf_op jit(solution)/shard_map/all_to_all | solution.py:375
  9.4 55.0 %copy-start.2 = (s32[16,16,4]{1,2,0:T(4,128)S(1)}, s32[16,16,4]{1,2,0:T(4,128)}, u32[]{:S(2)}) copy-start(s32[16,16,4]{1,2,0:T(4,128)} %param.11) | copy-start | bytes 12292
  9.5 55.0 %copy-start.3 = (s32[16,16,4]{1,2,0:T(4,128)S(1)}, s32[16,16,4]{1,2,0:T(4,128)}, u32[]{:S(2)}) copy-start(s32[16,16,4]{1,2,0:T(4,128)} %param.12) | copy-start | bytes 12292
  17.4 1.3 collective-permute-start
  18.8 23.5 %all-to-all-start.1 = ((bf16[16,128,128]{2,1,0:T(8,128)(2,1)}), bf16[16,128,128]{2,1,0:T(8,128)(2,1)S(1)}, u32[]{:S(2)}, u32[]{:S(2)}) async-start(bf16[16,128,128]{2,1,0:T(8,128)(2,1)} %shard_map.94), calls=%async_computation.1 | async-start | bytes 1048576 | tf_op jit(solution)/shard_map/all_to_all | solution.py:381
  26.5 15.8 %collective-permute-start.1 = (bf16[2,512,128]{2,1,0:T(8,128)(2,1)S(1)}, bf16[2,512,128]{2,1,0:T(8,128)(2,1)S(1)}, u32[]{:S(2)}, u32[]{:S(2)}) collective-permute-start(bf16[2,512,128]{2,1,0:T(8,128)(2,1)S(1)} %pad_maximum_fusion.refs_6_), channel_id=1, source_target_pairs={{0,32},{16,240},{32,64},{48,16},{64,96},{80,48},{96,128},{112,80},... | collective-permute-start | bytes 786440 | tf_op jit(solution)/shard_map/ppermute | solution.py:360
  42.3 6.8 %collective-permute-start.6 = (bf16[2,512,128]{2,1,0:T(8,128)(2,1)S(1)}, bf16[2,512,128]{2,1,0:T(8,128)(2,1)S(1)}, u32[]{:S(2)}, u32[]{:S(2)}) collective-permute-start(bf16[2,512,128]{2,1,0:T(8,128)(2,1)S(1)} %collective-permute-done.1.refs_7_), channel_id=1, source_target_pairs={{0,32},{16,240},{32,64},{48,16},{64,96},{80,48},{96,128},{112,80},... | collective-permute-start | bytes 786440 | tf_op jit(solution)/shard_map/ppermute | solution.py:360
  45.0 7.6 %collective-permute-start.5 = (bf16[16,64,128]{2,1,0:T(8,128)(2,1)S(1)}, bf16[16,64,128]{2,1,0:T(8,128)(2,1)S(1)}, u32[]{:S(2)}, u32[]{:S(2)}) collective-permute-start(bf16[16,64,128]{2,1,0:T(8,128)(2,1)S(1)} %get-tuple-element.30), channel_id=1, source_target_pairs={{0,3},{1,0},{2,1},{3,2},{4,7},{5,4},{6,5},{7,6},{8,11},{9,8},{10,9... | collective-permute-start | bytes 786440 | tf_op jit(solution)/shard_map/ppermute | solution.py:352
  46.0 8.4 %collective-permute-start.4 = (bf16[16,64,128]{2,1,0:T(8,128)(2,1)S(1)}, bf16[16,64,128]{2,1,0:T(8,128)(2,1)S(1)}, u32[]{:S(2)}, u32[]{:S(2)}) collective-permute-start(bf16[16,64,128]{2,1,0:T(8,128)(2,1)S(1)} %get-tuple-element.30), channel_id=1, source_target_pairs={{0,1},{1,2},{2,3},{3,0},{4,5},{5,6},{6,7},{7,4},{8,9},{9,10},{10,1... | collective-permute-start | bytes 786440 | tf_op jit(solution)/shard_map/ppermute | solution.py:352
  47.1 7.3 %collective-permute-start.3 = (bf16[16,64,128]{2,1,0:T(8,128)(2,1)S(1)}, bf16[16,64,128]{2,1,0:T(8,128)(2,1)S(1)}, u32[]{:S(2)}, u32[]{:S(2)}) collective-permute-start(bf16[16,64,128]{2,1,0:T(8,128)(2,1)S(1)} %get-tuple-element.27), channel_id=1, source_target_pairs={{0,12},{1,13},{2,14},{3,15},{4,0},{5,1},{6,2},{7,3},{8,4},{9,5},{1... | collective-permute-start | bytes 786440 | tf_op jit(solution)/shard_map/ppermute | solution.py:349
  48.0 7.8 %collective-permute-start.2 = (bf16[16,64,128]{2,1,0:T(8,128)(2,1)S(1)}, bf16[16,64,128]{2,1,0:T(8,128)(2,1)S(1)}, u32[]{:S(2)}, u32[]{:S(2)}) collective-permute-start(bf16[16,64,128]{2,1,0:T(8,128)(2,1)S(1)} %get-tuple-element.27), channel_id=1, source_target_pairs={{0,4},{1,5},{2,6},{3,7},{4,8},{5,9},{6,10},{7,11},{8,12},{9,13},{1... | collective-permute-start | bytes 786440 | tf_op jit(solution)/shard_map/ppermute | solution.py:349
  49.2 8.4 %collective-permute-start.11 = (bf16[2,512,128]{2,1,0:T(8,128)(2,1)S(1)}, bf16[2,512,128]{2,1,0:T(8,128)(2,1)S(1)}, u32[]{:S(2)}, u32[]{:S(2)}) collective-permute-start(bf16[2,512,128]{2,1,0:T(8,128)(2,1)S(1)} %collective-permute-done.6.refs_9_), channel_id=1, source_target_pairs={{0,32},{16,240},{32,64},{48,16},{64,96},{80,48},{96,128},{112,80},... | collective-permute-start | bytes 786440 | tf_op jit(solution)/shard_map/ppermute | solution.py:360
  52.6 8.0 %collective-permute-start.9 = (bf16[2,512,128]{2,1,0:T(8,128)(2,1)S(1)}, bf16[2,512,128]{2,1,0:T(8,128)(2,1)S(1)}, u32[]{:S(2)}, u32[]{:S(2)}) collective-permute-start(bf16[2,512,128]{2,1,0:T(8,128)(2,1)S(1)} %collective-permute-done.1.refs_7_), channel_id=1, source_target_pairs={{0,16},{16,0},{32,48},{48,32},{64,80},{80,64},{96,112},{112,96},{1... | collective-permute-start | bytes 786440 | tf_op jit(solution)/shard_map/ppermute | solution.py:357
  55.8 7.9 %collective-permute-start.7 = (bf16[16,64,128]{2,1,0:T(8,128)(2,1)S(1)}, bf16[16,64,128]{2,1,0:T(8,128)(2,1)S(1)}, u32[]{:S(2)}, u32[]{:S(2)}) collective-permute-start(bf16[16,64,128]{2,1,0:T(8,128)(2,1)S(1)} %get-tuple-element.27), channel_id=1, source_target_pairs={{0,8},{1,9},{2,10},{3,11},{4,12},{5,13},{6,14},{7,15},{8,0},{9,1},... | collective-permute-start | bytes 786440 | tf_op jit(solution)/shard_map/ppermute | solution.py:349
  56.1 7.9 %collective-permute-start.8 = (bf16[16,64,128]{2,1,0:T(8,128)(2,1)S(1)}, bf16[16,64,128]{2,1,0:T(8,128)(2,1)S(1)}, u32[]{:S(2)}, u32[]{:S(2)}) collective-permute-start(bf16[16,64,128]{2,1,0:T(8,128)(2,1)S(1)} %get-tuple-element.30), channel_id=1, source_target_pairs={{0,2},{1,3},{2,0},{3,1},{4,6},{5,7},{6,4},{7,5},{8,10},{9,11},{10,... | collective-permute-start | bytes 786440 | tf_op jit(solution)/shard_map/ppermute | solution.py:352
  57.6 6.4 %collective-permute-start.10 = (bf16[2,512,128]{2,1,0:T(8,128)(2,1)S(1)}, bf16[2,512,128]{2,1,0:T(8,128)(2,1)S(1)}, u32[]{:S(2)}, u32[]{:S(2)}) collective-permute-start(bf16[2,512,128]{2,1,0:T(8,128)(2,1)S(1)} %collective-permute-done.6.refs_9_), channel_id=1, source_target_pairs={{0,16},{16,0},{32,48},{48,32},{64,80},{80,64},{96,112},{112,96},{1... | collective-permute-start | bytes 786440 | tf_op jit(solution)/shard_map/ppermute | solution.py:357
  57.6 6.8 %collective-permute-start.13 = (bf16[2,512,128]{2,1,0:T(8,128)(2,1)S(1)}, bf16[2,512,128]{2,1,0:T(8,128)(2,1)S(1)}, u32[]{:S(2)}, u32[]{:S(2)}) collective-permute-start(bf16[2,512,128]{2,1,0:T(8,128)(2,1)S(1)} %collective-permute-done.11.refs_11_), channel_id=1, source_target_pairs={{0,32},{16,240},{32,64},{48,16},{64,96},{80,48},{96,128},{112,80},... | collective-permute-start | bytes 786440 | tf_op jit(solution)/shard_map/ppermute | solution.py:360
  60.6 3.9 %collective-permute-start.12 = (bf16[2,512,128]{2,1,0:T(8,128)(2,1)S(1)}, bf16[2,512,128]{2,1,0:T(8,128)(2,1)S(1)}, u32[]{:S(2)}, u32[]{:S(2)}) collective-permute-start(bf16[2,512,128]{2,1,0:T(8,128)(2,1)S(1)} %collective-permute-done.11.refs_11_), channel_id=1, source_target_pairs={{0,16},{16,0},{32,48},{48,32},{64,80},{80,64},{96,112},{112,96},{1... | collective-permute-start | bytes 786440 | tf_op jit(solution)/shard_map/ppermute | solution.py:357
  64.5 25.3 %copy-start = (f32[1,6,2,256,256]{4,3,2,1,0:T(8,128)S(1)}, f32[1,6,2,256,256]{4,3,2,1,0:T(8,128)}, u32[]{:S(2)}) copy-start(f32[1,6,2,256,256]{4,3,2,1,0:T(8,128)} %param.9) | copy-start | bytes 9437188
  64.5 25.3 %copy-start.1 = (bf16[1,6,2,256,256]{4,3,2,1,0:T(8,128)(2,1)S(1)}, bf16[1,6,2,256,256]{4,3,2,1,0:T(8,128)(2,1)}, u32[]{:S(2)}) copy-start(bf16[1,6,2,256,256]{4,3,2,1,0:T(8,128)(2,1)} %param.10) | copy-start | bytes 4718596
  64.5 25.3 %copy-start.4 = (s32[16,16]{1,0:T(8,128)S(1)}, s32[16,16]{1,0:T(8,128)}, u32[]{:S(2)}) copy-start(s32[16,16]{1,0:T(8,128)} %fresh_ref.1) | copy-start | bytes 3076
